TPU v7x, 32 devices: a whole 2x2x4 slice. The times are simulated.
32 devices in a mesh: stream: 8 (over z, x), span: 4 (over y, core).
Axes of the slice: x: 2, y: 2, z: 4, core: 2. Of those that a mesh axis runs over, the one named last changes fastest.
Arguments:
- checkpoint: float32 [5, 192, 8, 512], P(None, None, 'stream', 'span'), may hold values from -4.8 to 4.8
- adjoint: float32 [5, 192, 8, 512], P(None, None, 'stream', 'span'), may hold values from -6 to 6
- line_inverse: bfloat16 [8, 3, 320, 320], P('stream'), may hold values from -0.3125 to 0.3125
- row_source: int32 [768], replicated, may hold values from 0 to 767, as said below
Outputs:
- adjoint_start: float32 [5, 192, 8, 512], P(None, None, 'stream', 'span')
Inputs may be any that keep to these rules, and one draw needn't show every extreme that they name: `row_source`: every rotor outlet row is taken by exactly one stator inlet row, and each stator span tile takes exactly 48 rows from each rotor span tile.
All inputs are finite; a program needn't handle non-finite values.
Results may differ from a plain program's by a relative error of at most 0.0029.
Values sent between devices are 32-bit elements; how exact they have to be, the bound alone decides.
No kernel may reach another device: no remote copies, remote signals or barrier semaphores. Data moves between devices by JAX's collectives and lax.ppermute only.
A program may use at most 64 MiB of HBM per device.

v0:
```python
import jax
import jax.numpy as jnp
from jax import lax
from jax.sharding import PartitionSpec as P

time_step = 0.5
ADVECTION = (1.0, 0.6, 0.8, 1.2, 0.7)
DISSIPATION = (0.3, 0.25, 0.35, 0.3, 0.4)
SPREADING = (0.4, 0.3, 0.5, 0.35, 0.45)


def with_halo(block, sides, width):
    for axis, dim in sides:
        count = lax.axis_size(axis)
        forward = [(i, i + 1) for i in range(count - 1)]
        forward.append((count - 1, 0))
        backward = [(target, source) for source, target in forward]
        low = lax.ppermute(
            lax.slice_in_dim(block, block.shape[dim] - width, None, axis=dim), axis, forward
        )
        high = lax.ppermute(lax.slice_in_dim(block, 0, width, axis=dim), axis, backward)
        block = jnp.concatenate([low, block, high], axis=dim)
    return block


def per_state(values):
    return jnp.array(values, jnp.float32).reshape(5, 1, 1, 1)


def plane_remap(lower_rim, upper_rim, row_source):
    span_count = lax.axis_size("span")
    position = lax.axis_index("span")
    line_points = lower_rim.shape[1]
    capacity = line_points // span_count
    src_dev = (row_source // line_points).reshape(span_count, line_points)
    src_row = (row_source % line_points).reshape(span_count, line_points)
    devices = jnp.arange(span_count, dtype=jnp.int32)
    slot_ids = jnp.arange(capacity, dtype=jnp.int32)
    point_ids = jnp.arange(line_points, dtype=jnp.int32)
    onehot = (src_dev[:, :, None] == devices[None, None, :]).astype(jnp.int32)
    arrival = jnp.sum((jnp.cumsum(onehot, axis=1) - onehot) * onehot, axis=2)
    pick_lower = (
        (src_dev == position)[:, :, None] & (arrival[:, :, None] == slot_ids[None, None, :])
    ).astype(jnp.int32)
    send_lower = jnp.sum(pick_lower * src_row[:, :, None], axis=1).reshape(span_count * capacity)
    own_dev = lax.dynamic_index_in_dim(src_dev, position, 0, keepdims=False)
    own_arrival = lax.dynamic_index_in_dim(arrival, position, 0, keepdims=False)
    pick_upper = (
        (own_dev[None, :] == devices[:, None])[:, :, None]
        & (own_arrival[None, :, None] == slot_ids[None, None, :])
    ).astype(jnp.int32)
    send_upper = jnp.sum(pick_upper * point_ids[None, :, None], axis=1).reshape(
        span_count * capacity
    )
    outgoing = (jnp.take(lower_rim, send_lower, axis=1), jnp.take(upper_rim, send_upper, axis=1))
    got_lower, got_upper = (
        lax.all_to_all(outgoing[0], "span", split_axis=1, concat_axis=1, tiled=True),
        lax.all_to_all(outgoing[1], "span", split_axis=1, concat_axis=1, tiled=True),
    )
    lower_mapped = jnp.take(got_lower, own_dev * capacity + own_arrival, axis=1)
    matches = (
        (src_dev == position)[:, :, None] & (src_row[:, :, None] == point_ids[None, None, :])
    ).astype(jnp.int32)
    where_from = devices[:, None] * capacity + arrival
    upper_pos = jnp.sum(matches * where_from[:, :, None], axis=(0, 1))
    upper_mapped = jnp.take(got_upper, upper_pos, axis=1)
    return (lower_mapped, upper_mapped)


def gather_rims(field, row_source):
    stream_count = lax.axis_size("stream")
    stream_place = lax.axis_index("stream")
    halfway = stream_count // 2
    padded = with_halo(field, (("stream", 2), ("span", 3)), 1)
    lower_rim = padded[:, :, 0, 1:-1]
    upper_rim = padded[:, :, -1, 1:-1]
    left_rim = padded[:, :, 1:-1, :-2]
    right_rim = padded[:, :, 1:-1, 2:]
    lower_rim = jnp.where(stream_place == 0, 0.0, lower_rim)
    upper_rim = jnp.where(stream_place == stream_count - 1, 0.0, upper_rim)
    lower_mapped, upper_mapped = plane_remap(lower_rim, upper_rim, row_source)
    lower_rim = jnp.where(stream_place == halfway, lower_mapped, lower_rim)
    upper_rim = jnp.where(stream_place == halfway - 1, upper_mapped, upper_rim)
    return (lower_rim, upper_rim, left_rim, right_rim)


def apply_operator(field, rims, coef_down, coef_up, center, lateral):
    lower_rim, upper_rim, left_rim, right_rim = rims
    upstream = jnp.concatenate([lower_rim[:, :, None], field[:, :, :-1]], axis=2)
    downstream = jnp.concatenate([field[:, :, 1:], upper_rim[:, :, None]], axis=2)
    lateral_sum = left_rim + right_rim - 2.0 * field
    return coef_down * downstream + coef_up * upstream + center * field + lateral * lateral_sum


def local(checkpoint, adjoint, line_inverse, row_source):
    advect = per_state(ADVECTION)
    dissip = per_state(DISSIPATION)
    lateral = per_state(SPREADING)
    toward_down = -0.5 * advect + dissip
    toward_up = 0.5 * advect + dissip
    center = -2.0 * dissip
    flux = jnp.tanh(checkpoint)
    flux_rims = gather_rims(flux, row_source)
    advanced = checkpoint + time_step * apply_operator(
        flux, flux_rims, toward_down, toward_up, center, lateral
    )
    tanh_adv = jnp.tanh(advanced)
    section_slope = 2.0 - tanh_adv * tanh_adv
    line_points = checkpoint.shape[1]
    stations = checkpoint.shape[2]
    span_cells = checkpoint.shape[3]
    blocks = line_inverse.shape[1]
    block_points = line_points // blocks
    rounded = adjoint.astype(jnp.bfloat16).reshape(5, blocks, block_points, stations, span_cells)
    inverse = line_inverse.reshape(stations, blocks, 5, block_points, 5, block_points)
    carried = jnp.einsum(
        "sbclem,cblsp->ebmsp", inverse, rounded, preferred_element_type=jnp.float32
    ).reshape(5, line_points, stations, span_cells)
    weighted = section_slope * carried
    weight_rims = gather_rims(weighted, row_source)
    tangent = 1.0 - flux * flux
    return weighted + time_step * tangent * apply_operator(
        weighted, weight_rims, toward_up, toward_down, center, lateral
    )


def solution(mesh):
    return jax.shard_map(
        local,
        mesh=mesh,
        in_specs=(
            P(None, None, "stream", "span"),
            P(None, None, "stream", "span"),
            P("stream", None, None, None),
            P(),
        ),
        out_specs=P(None, None, "stream", "span"),
        check_vma=False,
    )
```

profile of v0, /device:TPU:17, one launch (start us, length us, event | category | flops | bytes accessed | tf_op | source)
XLA Modules:
  0.0 137.7 jit_solution(5082046438657520871)
XLA Ops:
  0.0 1.9 %tanh_bitcast_fusion = (f32[5,192,1,128]{3,1,2,0:T(8,128)}, f32[5,192,1,128]{3,1,0,2:T(8,128)S(1)}) fusion(f32[5,192,1,128]{3,1,0,2:T(8,128)} %bitcast.140), kind=kLoop, calls=%fused_computation.111 | loop fusion | bytes 1474560 | tf_op jit(solution)/shard_map/tanh | solution.py:102
  1.9 1.1 collective-permute-start
  3.6 4.8 %reduce-window.6 = s32[4,4,2,128]{3,2,1,0:T(2,128)S(1)} reduce-window(s32[4,4,2,128]{3,2,1,0:T(2,128)S(1)} %reshape.163, s32[]{:T(128)} %constant.84.clone.1), window={size=1x1x1x128 pad=0_0x0_0x0_0x127_0}, to_apply=%region_0.1 | reduce-window | flops 520192 | bytes 32772 | tf_op jit(solution)/shard_map/reduce-window
  9.6 2.5 %reshape.161 = bf16[3,5,64,5,64]{4,3,2,1,0:T(8,128)(2,1)S(1)} reshape(bf16[1,3,320,320]{3,2,1,0:T(8,128)(2,1)} %param.11) | data formatting | bytes 1228800 | tf_op jit(solution)/shard_map/reshape.24
  12.0 1.4 convert_element_type.6
  13.4 0.7 copy.138
  14.8 2.2 %fusion.2 = f32[5,3,64,1,128]{4,2,0,1,3:T(8,128)} fusion(bf16[3,5,64,5,64]{4,3,2,1,0:T(8,128)(2,1)S(1)} %reshape.161, bf16[5,3,64,128,1]{3,2,1,0,4:T(8,128)(2,1)} %bitcast.148), kind=kOutput, calls=%fused_computation.12 | convolution fusion | flops 78643200 | bytes 1351680 | tf_op jit(solution)/shard_map/sbclem,cblsp->ebmsp/dot_general | solution.py:116
  17.0 7.5 %collective-permute-done.1 = f32[5,192,1,128]{3,1,2,0:T(8,128)S(1)} collective-permute-done((f32[5,192,1,128]{3,1,2,0:T(8,128)}, f32[5,192,1,128]{3,1,2,0:T(8,128)S(1)}, u32[]{:S(2)}, u32[]{:S(2)}) %collective-permute-start.1) | collective-permute-done | bytes 491552 | tf_op jit(solution)/shard_map/ppermute | solution.py:18
  24.8 0.9 gather_fusion.2
  25.7 1.2 select_bitcast_fusion.2
  26.9 5.3 %all-to-all-start.1 = ((f32[5,192,128]{2,0,1:T(8,128)}), f32[5,192,128]{2,0,1:T(8,128)}, u32[]{:S(2)}, u32[]{:S(2)}) async-start(f32[5,192,128]{2,0,1:T(8,128)} %select_bitcast_fusion.2), calls=%async_computation.1 | async-start | bytes 1572864 | tf_op jit(solution)/shard_map/all_to_all | solution.py:57
  32.6 1.8 %gather_fusion = f32[192,5,128]{2,1,0:T(8,128)} fusion(f32[5,192,128]{2,0,1:T(8,128)S(1)} %copy.100, s32[1024]{0:T(1024)S(1)} %pad_clamp_fusion.3), kind=kCustom, calls=%fused_computation.clone | custom fusion | bytes 983808 | tf_op jit(solution)/shard_map/jit(_take)/gather | solution.py:55
  34.5 1.0 copy-done.7
  35.5 1.2 select_bitcast_fusion.3
  36.7 6.4 %all-to-all-done.1 = f32[5,192,128]{2,0,1:T(8,128)} async-done(((f32[5,192,128]{2,0,1:T(8,128)}), f32[5,192,128]{2,0,1:T(8,128)}, u32[]{:S(2)}, u32[]{:S(2)}) %all-to-all-start.1) | async-done | bytes 491552 | tf_op jit(solution)/shard_map/all_to_all | solution.py:57
  43.1 5.0 %all-to-all-start = ((f32[5,192,128]{2,0,1:T(8,128)}), f32[5,192,128]{2,0,1:T(8,128)}, u32[]{:S(2)}, u32[]{:S(2)}) async-start(f32[5,192,128]{2,0,1:T(8,128)} %select_bitcast_fusion.3), calls=%async_computation | async-start | bytes 1572864 | tf_op jit(solution)/shard_map/all_to_all | solution.py:58
  48.2 1.7 %fusion.39 = (f32[5,192,3,1]{3,1,0,2:T(8,128)S(1)}, f32[5,192,3,1]{3,1,0,2:T(8,128)}) fusion(f32[5,192,3,128]{3,1,0,2:T(8,128)S(1)} %pad_maximum_fusion), kind=kLoop, calls=%fused_computation.113 | loop fusion | bytes 46080 | tf_op jit(solution)/shard_map/slice | solution.py:19
  49.8 2.0 %copy.110 = f32[5,192,3,1]{1,3,2,0:T(1,128)S(1)} copy(f32[5,192,3,1]{3,1,0,2:T(8,128)} %get-tuple-element.11) | data formatting | bytes 23040 | tf_op jit(solution)/shard_map/slice | solution.py:21
  51.9 0.6 copy.108
  52.5 1.7 %collective-permute-start.2 = (f32[5,192,3,1]{1,3,2,0:T(1,128)S(1)}, f32[5,192,3,1]{1,3,2,0:T(1,128)S(1)}, u32[]{:S(2)}, u32[]{:S(2)}) collective-permute-start(f32[5,192,3,1]{1,3,2,0:T(1,128)S(1)} %copy.108), channel_id=1, source_target_pairs={{0,1},{1,2},{2,3},{3,0},{4,5},{5,6},{6,7},{7,4},{8,9},{9,10},{10,1... | collective-permute-start | bytes 34568 | tf_op jit(solution)/shard_map/ppermute | solution.py:18
  54.2 0.8 copy.117
  55.0 4.7 %collective-permute-done.3 = f32[5,192,3,1]{1,3,2,0:T(1,128)S(1)} collective-permute-done((f32[5,192,3,1]{1,3,2,0:T(1,128)S(1)}, f32[5,192,3,1]{1,3,2,0:T(1,128)S(1)}, u32[]{:S(2)}, u32[]{:S(2)}) %collective-permute-start.3) | collective-permute-done | bytes 11552 | tf_op jit(solution)/shard_map/ppermute | solution.py:21
  59.7 0.5 copy.111
  60.3 0.5 copy.109
  60.8 2.7 %gather_fusion.3 = f32[192,5,128]{2,1,0:T(8,128)} fusion(f32[5,192,128]{2,0,1:T(8,128)} %all-to-all-done.1, s32[1024]{0:T(1024)S(1)} %pad_clamp_fusion), kind=kCustom, calls=%fused_computation.3.clone | custom fusion | bytes 983808 | tf_op jit(solution)/shard_map/jit(_take)/gather | solution.py:60
  63.5 2.7 %gather_fusion.1 = f32[192,5,128]{2,1,0:T(8,128)} fusion(f32[5,192,128]{2,0,1:T(8,128)} %all-to-all-done, s32[1024]{0:T(1024)S(1)} %pad_clamp_fusion.2), kind=kCustom, calls=%fused_computation.1.clone | custom fusion | bytes 983808 | tf_op jit(solution)/shard_map/jit(_take)/gather | solution.py:66
  66.3 3.8 %fusion.7 = f32[5,192,1,128]{3,1,2,0:T(8,128)} fusion(f32[5,192,1,128]{3,1,2,0:T(8,128)} %bitcast.147, f32[5,192,1,128]{3,1,0,2:T(8,128)S(1)} %bitcast.141, f32[5,192,1,128]{3,1,0,2:T(8,128)} %copy-done.1, f32[5,192,3,1]{3,1,0,2:T(8,128)S(1)} %copy.111, f32[5,192,1,128]{3,1,0,2:T(8,128)} %bitcast.144, f32[5,192,1,128]{3,1,0,2:T(8,128)} %bitcast.146, ...), kind=kLoop, calls=%fused_computation.23 | loop fusion | flops 3317760 | bytes 3955668 | tf_op jit(solution)/shard_map/mul | solution.py:119
  70.1 2.1 %collective-permute-start.5 = (f32[5,192,1,128]{3,1,2,0:T(8,128)}, f32[5,192,1,128]{3,1,2,0:T(8,128)S(1)}, u32[]{:S(2)}, u32[]{:S(2)}) collective-permute-start(f32[5,192,1,128]{3,1,2,0:T(8,128)} %fusion.7), channel_id=1, source_target_pairs={{0,4},{4,8},{8,12},{12,16},{16,20},{20,24},{24,28},{28,0},{1,5},{5... | collective-permute-start | bytes 1474568 | tf_op jit(solution)/shard_map/ppermute | solution.py:18
  72.5 21.5 %collective-permute-done.5 = f32[5,192,1,128]{3,1,2,0:T(8,128)S(1)} collective-permute-done((f32[5,192,1,128]{3,1,2,0:T(8,128)}, f32[5,192,1,128]{3,1,2,0:T(8,128)S(1)}, u32[]{:S(2)}, u32[]{:S(2)}) %collective-permute-start.5) | collective-permute-done | bytes 491552 | tf_op jit(solution)/shard_map/ppermute | solution.py:18
  94.3 0.9 gather_fusion.6
  95.2 1.2 select_bitcast_fusion
  96.4 3.7 %all-to-all-start.3 = ((f32[5,192,128]{2,0,1:T(8,128)}), f32[5,192,128]{2,0,1:T(8,128)S(1)}, u32[]{:S(2)}, u32[]{:S(2)}) async-start(f32[5,192,128]{2,0,1:T(8,128)} %select_bitcast_fusion), calls=%async_computation.3 | async-start | bytes 1572864 | tf_op jit(solution)/shard_map/all_to_all | solution.py:57
  100.1 1.2 copy.121
  101.4 1.8 %gather_fusion.4 = f32[192,5,128]{2,1,0:T(8,128)S(1)} fusion(f32[5,192,128]{2,0,1:T(8,128)} %copy.121, s32[1024]{0:T(1024)S(1)} %pad_clamp_fusion.3), kind=kCustom, calls=%fused_computation.4.clone | custom fusion | bytes 983808 | tf_op jit(solution)/shard_map/jit(_take)/gather | solution.py:55
  103.2 1.2 select_bitcast_fusion.1
  104.4 6.5 %all-to-all-done.3 = f32[5,192,128]{2,0,1:T(8,128)S(1)} async-done(((f32[5,192,128]{2,0,1:T(8,128)}), f32[5,192,128]{2,0,1:T(8,128)S(1)}, u32[]{:S(2)}, u32[]{:S(2)}) %all-to-all-start.3) | async-done | bytes 491552 | tf_op jit(solution)/shard_map/all_to_all | solution.py:57
  110.9 5.0 %all-to-all-start.2 = ((f32[5,192,128]{2,0,1:T(8,128)}), f32[5,192,128]{2,0,1:T(8,128)}, u32[]{:S(2)}, u32[]{:S(2)}) async-start(f32[5,192,128]{2,0,1:T(8,128)} %select_bitcast_fusion.1), calls=%async_computation.2 | async-start | bytes 1572864 | tf_op jit(solution)/shard_map/all_to_all | solution.py:58
  115.9 1.1 pad_maximum_fusion.1
  117.1 0.5 fusion.38
  117.6 0.6 copy.129
  118.3 0.6 copy.127
  118.8 1.7 %collective-permute-start.6 = (f32[5,192,3,1]{1,3,2,0:T(1,128)S(1)}, f32[5,192,3,1]{1,3,2,0:T(1,128)S(1)}, u32[]{:S(2)}, u32[]{:S(2)}) collective-permute-start(f32[5,192,3,1]{1,3,2,0:T(1,128)S(1)} %copy.127), channel_id=1, source_target_pairs={{0,1},{1,2},{2,3},{3,0},{4,5},{5,6},{6,7},{7,4},{8,9},{9,10},{10,1... | collective-permute-start | bytes 34568 | tf_op jit(solution)/shard_map/ppermute | solution.py:18
  120.5 6.9 %collective-permute-done.7 = f32[5,192,3,1]{1,3,2,0:T(1,128)S(1)} collective-permute-done((f32[5,192,3,1]{1,3,2,0:T(1,128)S(1)}, f32[5,192,3,1]{1,3,2,0:T(1,128)S(1)}, u32[]{:S(2)}, u32[]{:S(2)}) %collective-permute-start.7) | collective-permute-done | bytes 11552 | tf_op jit(solution)/shard_map/ppermute | solution.py:21
  127.5 0.5 copy.130
  128.0 0.5 copy.128
  128.5 2.7 %gather_fusion.7 = f32[192,5,128]{2,1,0:T(8,128)} fusion(f32[5,192,128]{2,0,1:T(8,128)} %copy-done.6, s32[1024]{0:T(1024)S(1)} %pad_clamp_fusion), kind=kCustom, calls=%fused_computation.7.clone | custom fusion | bytes 983808 | tf_op jit(solution)/shard_map/jit(_take)/gather | solution.py:60
  131.2 2.7 %gather_fusion.5 = f32[192,5,128]{2,1,0:T(8,128)} fusion(f32[5,192,128]{2,0,1:T(8,128)} %all-to-all-done.2, s32[1024]{0:T(1024)S(1)} %pad_clamp_fusion.2), kind=kCustom, calls=%fused_computation.5.clone | custom fusion | bytes 983808 | tf_op jit(solution)/shard_map/jit(_take)/gather | solution.py:66
  134.0 3.7 %fusion.20 = f32[5,192,1,128]{3,1,2,0:T(8,128)} fusion(f32[5,192,1,128]{3,1,2,0:T(8,128)} %fusion.7, f32[5,192,3,1]{3,1,2,0:T(8,128)S(1)} %copy.130, f32[5,192,1,128]{3,1,2,0:T(8,128)} %copy-done.5, f32[5,192,1,128]{3,1,2,0:T(8,128)} %copy-done.4, f32[5,192,3,1]{3,1,2,0:T(8,128)S(1)} %copy.128, f32[192,5,128]{2,1,0:T(8,128)} %gather_fusion.7, ...), kind=kLoop, calls=%fused_computation.37 | loop fusion | flops 3317760 | bytes 3464148 | tf_op jit(solution)/shard_map/add | solution.py:122
  (81 shorter events, 3.9 us)
Async XLA Ops:
  0.0 3.4 %copy-start.9 = (s32[768]{0:T(1024)S(1)}, s32[768]{0:T(1024)}, u32[]{:S(2)}) copy-start(s32[768]{0:T(1024)} %param.12) | copy-start | bytes 9220
  1.9 32.5 %copy-start.1 = (f32[5,192,1,128]{3,1,0,2:T(8,128)}, f32[5,192,1,128]{3,1,0,2:T(8,128)S(1)}, u32[]{:S(2)}) copy-start(f32[5,192,1,128]{3,1,0,2:T(8,128)S(1)} %get-tuple-element.13) | copy-start | bytes 1474564
  1.9 30.3 %collective-permute-start = (f32[5,192,1,128]{3,1,2,0:T(8,128)}, f32[5,192,1,128]{3,1,2,0:T(8,128)S(1)}, u32[]{:S(2)}, u32[]{:S(2)}) collective-permute-start(f32[5,192,1,128]{3,1,2,0:T(8,128)} %get-tuple-element.12), channel_id=1, source_target_pairs={{4,0},{8,4},{12,8},{16,12},{20,16},{24,20},{28,24},{0,28},{5,1},{9... | collective-permute-start | bytes 1474568 | tf_op jit(solution)/shard_map/ppermute | solution.py:21
  3.0 21.5 %collective-permute-start.1 = (f32[5,192,1,128]{3,1,2,0:T(8,128)}, f32[5,192,1,128]{3,1,2,0:T(8,128)S(1)}, u32[]{:S(2)}, u32[]{:S(2)}) collective-permute-start(f32[5,192,1,128]{3,1,2,0:T(8,128)} %get-tuple-element.12), channel_id=1, source_target_pairs={{0,4},{4,8},{8,12},{12,16},{16,20},{20,24},{24,28},{28,0},{1,5},{5... | collective-permute-start | bytes 1474568 | tf_op jit(solution)/shard_map/ppermute | solution.py:18
  24.5 9.9 %copy-start.3 = (f32[5,192,1,128]{3,1,2,0:T(8,128)}, f32[5,192,1,128]{3,1,2,0:T(8,128)S(1)}, u32[]{:S(2)}) copy-start(f32[5,192,1,128]{3,1,2,0:T(8,128)S(1)} %collective-permute-done.1) | copy-start | bytes 1474564
  26.9 16.2 %all-to-all-start.1 = ((f32[5,192,128]{2,0,1:T(8,128)}), f32[5,192,128]{2,0,1:T(8,128)}, u32[]{:S(2)}, u32[]{:S(2)}) async-start(f32[5,192,128]{2,0,1:T(8,128)} %select_bitcast_fusion.2), calls=%async_computation.1 | async-start | bytes 1572864 | tf_op jit(solution)/shard_map/all_to_all | solution.py:57
  32.3 2.2 %copy-start.2 = (f32[5,192,1,128]{3,1,2,0:T(8,128)}, f32[5,192,1,128]{3,1,2,0:T(8,128)S(1)}, u32[]{:S(2)}) copy-start(f32[5,192,1,128]{3,1,2,0:T(8,128)S(1)} %collective-permute-done) | copy-start | bytes 1474564
  34.4 1.1 copy-start.7
  43.1 20.4 %all-to-all-start = ((f32[5,192,128]{2,0,1:T(8,128)}), f32[5,192,128]{2,0,1:T(8,128)}, u32[]{:S(2)}, u32[]{:S(2)}) async-start(f32[5,192,128]{2,0,1:T(8,128)} %select_bitcast_fusion.3), calls=%async_computation | async-start | bytes 1572864 | tf_op jit(solution)/shard_map/all_to_all | solution.py:58
  49.8 4.4 %copy-start.8 = (f32[5,3,64,1,128]{4,2,0,1,3:T(8,128)S(1)}, f32[5,3,64,1,128]{4,2,0,1,3:T(8,128)}, u32[]{:S(2)}) copy-start(f32[5,3,64,1,128]{4,2,0,1,3:T(8,128)} %fusion.2) | copy-start | bytes 1474564
  51.8 7.9 %collective-permute-start.3 = (f32[5,192,3,1]{1,3,2,0:T(1,128)S(1)}, f32[5,192,3,1]{1,3,2,0:T(1,128)S(1)}, u32[]{:S(2)}, u32[]{:S(2)}) collective-permute-start(f32[5,192,3,1]{1,3,2,0:T(1,128)S(1)} %copy.110), channel_id=1, source_target_pairs={{1,0},{2,1},{3,2},{0,3},{5,4},{6,5},{7,6},{4,7},{9,8},{10,9},{11,1... | collective-permute-start | bytes 34568 | tf_op jit(solution)/shard_map/ppermute | solution.py:21
  52.5 7.8 %collective-permute-start.2 = (f32[5,192,3,1]{1,3,2,0:T(1,128)S(1)}, f32[5,192,3,1]{1,3,2,0:T(1,128)S(1)}, u32[]{:S(2)}, u32[]{:S(2)}) collective-permute-start(f32[5,192,3,1]{1,3,2,0:T(1,128)S(1)} %copy.108), channel_id=1, source_target_pairs={{0,1},{1,2},{2,3},{3,0},{4,5},{5,6},{6,7},{7,4},{8,9},{9,10},{10,1... | collective-permute-start | bytes 34568 | tf_op jit(solution)/shard_map/ppermute | solution.py:18
  60.2 6.1 %copy-start = (f32[5,192,1,128]{3,2,1,0:T(1,128)S(1)}, f32[5,192,1,128]{3,2,1,0:T(1,128)}, u32[]{:S(2)}) copy-start(f32[5,192,1,128]{3,2,1,0:T(1,128)} %param.9) | copy-start | bytes 1474564
  60.2 6.1 %copy-start.10 = (f32[5]{0:T(128)S(1)}, f32[5]{0:T(128)}, u32[]{:S(2)}) copy-start(f32[5]{0:T(128)} %constant.95.clone) | copy-start | bytes 64
  60.2 6.0 %copy-start.11 = (f32[5]{0:T(128)S(1)}, f32[5]{0:T(128)}, u32[]{:S(2)}) copy-start(f32[5]{0:T(128)} %constant.105) | copy-start | bytes 64
  60.2 6.0 %copy-start.12 = (f32[5]{0:T(128)S(1)}, f32[5]{0:T(128)}, u32[]{:S(2)}) copy-start(f32[5]{0:T(128)} %constant.104) | copy-start | bytes 64
  60.2 6.0 %copy-start.13 = (f32[5]{0:T(128)S(1)}, f32[5]{0:T(128)}, u32[]{:S(2)}) copy-start(f32[5]{0:T(128)} %constant.102) | copy-start | bytes 64
  70.1 23.8 %collective-permute-start.5 = (f32[5,192,1,128]{3,1,2,0:T(8,128)}, f32[5,192,1,128]{3,1,2,0:T(8,128)S(1)}, u32[]{:S(2)}, u32[]{:S(2)}) collective-permute-start(f32[5,192,1,128]{3,1,2,0:T(8,128)} %fusion.7), channel_id=1, source_target_pairs={{0,4},{4,8},{8,12},{12,16},{16,20},{20,24},{24,28},{28,0},{1,5},{5... | collective-permute-start | bytes 1474568 | tf_op jit(solution)/shard_map/ppermute | solution.py:18
  72.2 27.9 %collective-permute-start.4 = (f32[5,192,1,128]{3,1,2,0:T(8,128)}, f32[5,192,1,128]{3,1,2,0:T(8,128)S(1)}, u32[]{:S(2)}, u32[]{:S(2)}) collective-permute-start(f32[5,192,1,128]{3,1,2,0:T(8,128)} %fusion.7), channel_id=1, source_target_pairs={{4,0},{8,4},{12,8},{16,12},{20,16},{24,20},{28,24},{0,28},{5,1},{9... | collective-permute-start | bytes 1474568 | tf_op jit(solution)/shard_map/ppermute | solution.py:21
  94.0 22.0 %copy-start.4 = (f32[5,192,1,128]{3,1,2,0:T(8,128)}, f32[5,192,1,128]{3,1,2,0:T(8,128)S(1)}, u32[]{:S(2)}) copy-start(f32[5,192,1,128]{3,1,2,0:T(8,128)S(1)} %collective-permute-done.5) | copy-start | bytes 1474564
  96.4 14.5 %all-to-all-start.3 = ((f32[5,192,128]{2,0,1:T(8,128)}), f32[5,192,128]{2,0,1:T(8,128)S(1)}, u32[]{:S(2)}, u32[]{:S(2)}) async-start(f32[5,192,128]{2,0,1:T(8,128)} %select_bitcast_fusion), calls=%async_computation.3 | async-start | bytes 1572864 | tf_op jit(solution)/shard_map/all_to_all | solution.py:57
  100.1 15.8 %copy-start.5 = (f32[5,192,1,128]{3,1,2,0:T(8,128)}, f32[5,192,1,128]{3,1,2,0:T(8,128)S(1)}, u32[]{:S(2)}) copy-start(f32[5,192,1,128]{3,1,2,0:T(8,128)S(1)} %collective-permute-done.4) | copy-start | bytes 1474564
  110.9 5.0 %copy-start.6 = (f32[5,192,128]{2,0,1:T(8,128)}, f32[5,192,128]{2,0,1:T(8,128)S(1)}, u32[]{:S(2)}) copy-start(f32[5,192,128]{2,0,1:T(8,128)S(1)} %all-to-all-done.3) | copy-start | bytes 1474564
  110.9 20.3 %all-to-all-start.2 = ((f32[5,192,128]{2,0,1:T(8,128)}), f32[5,192,128]{2,0,1:T(8,128)}, u32[]{:S(2)}, u32[]{:S(2)}) async-start(f32[5,192,128]{2,0,1:T(8,128)} %select_bitcast_fusion.1), calls=%async_computation.2 | async-start | bytes 1572864 | tf_op jit(solution)/shard_map/all_to_all | solution.py:58
  118.2 9.3 %collective-permute-start.7 = (f32[5,192,3,1]{1,3,2,0:T(1,128)S(1)}, f32[5,192,3,1]{1,3,2,0:T(1,128)S(1)}, u32[]{:S(2)}, u32[]{:S(2)}) collective-permute-start(f32[5,192,3,1]{1,3,2,0:T(1,128)S(1)} %copy.129), channel_id=1, source_target_pairs={{1,0},{2,1},{3,2},{0,3},{5,4},{6,5},{7,6},{4,7},{9,8},{10,9},{11,1... | collective-permute-start | bytes 34568 | tf_op jit(solution)/shard_map/ppermute | solution.py:21
  118.8 9.1 %collective-permute-start.6 = (f32[5,192,3,1]{1,3,2,0:T(1,128)S(1)}, f32[5,192,3,1]{1,3,2,0:T(1,128)S(1)}, u32[]{:S(2)}, u32[]{:S(2)}) collective-permute-start(f32[5,192,3,1]{1,3,2,0:T(1,128)S(1)} %copy.127), channel_id=1, source_target_pairs={{0,1},{1,2},{2,3},{3,0},{4,5},{5,6},{6,7},{7,4},{8,9},{9,10},{10,1... | collective-permute-start | bytes 34568 | tf_op jit(solution)/shard_map/ppermute | solution.py:18
where the time goes:
time: 140 us; the launch traced here: 138 us
  waiting for transfers between devices  53.5 us (38%)
  local copies, waits for them, and re-layouts  34.2 us (24%)
  starting transfers between devices  26.5 us (19%)
  other arithmetic  20.9 us (15%)
  matrix products  2.23 us (2%)
    ppermute x4, waiting for transfers between devices, with_halo(): lax.ppermute(lax.slice_in_dim(block, block.shape[dim] - width, None, axis...  29 us
    all_to_all x2, waiting for transfers between devices, plane_remap(): lax.all_to_all(outgoing[0], 'span', split_axis=1, concat_axis=1, tiled=True)  12.9 us
    ppermute x4, waiting for transfers between devices, with_halo(): lax.ppermute(lax.slice_in_dim(block, 0, width, axis=dim), axis, backward)  11.6 us
    all_to_all x2, starting transfers between devices, plane_remap(): lax.all_to_all(outgoing[1], 'span', split_axis=1, concat_axis=1, tiled=True)  10 us
    all_to_all x2, starting transfers between devices, plane_remap(): lax.all_to_all(outgoing[0], 'span', split_axis=1, concat_axis=1, tiled=True)  9.05 us
    ppermute x4, starting transfers between devices, with_halo(): lax.ppermute(lax.slice_in_dim(block, block.shape[dim] - width, None, axis...  5.88 us
    gather x2, local copies, waits for them, and re-layouts, plane_remap(): upper_mapped = jnp.take(got_upper, upper_pos, axis=1)  5.49 us
    gather x2, local copies, waits for them, and re-layouts, plane_remap(): lower_mapped = jnp.take(got_lower, own_dev * capacity + own_arrival, axis=1)  5.47 us
  transfers between devices with their start and end apart: 12, of which 6 were waited for; matrix products, arithmetic and copies ran while one was open for 30% of the time, Pallas kernels for 0%

commit v1 on v0

v1 whole, which is shorter than its diff:
```python
import jax
import jax.numpy as jnp
from jax import lax
from jax.experimental import pallas as pl
from jax.experimental.pallas import tpu as pltpu
from jax.sharding import PartitionSpec as P

time_step = 0.5
ADVECTION = (1.0, 0.6, 0.8, 1.2, 0.7)
DISSIPATION = (0.3, 0.25, 0.35, 0.3, 0.4)
SPREADING = (0.4, 0.3, 0.5, 0.35, 0.45)
NC = 5
LANES = 128
HALF = 64
AXES = ("stream", "span")
f32 = jnp.float32
bf16 = jnp.bfloat16


class Plan:
    def __init__(self, mesh, rows, blocks, block_rows):
        self.stream = mesh.shape["stream"]
        self.span = mesh.shape["span"]
        self.rows = rows
        self.blocks = blocks
        self.block_rows = block_rows
        self.pairs = self.stream // 2
        self.inlet = self.stream // 4
        assert self.stream % 4 == 0 and self.inlet % 2 == 0 and self.span % 2 == 0
        self.chips = self.span // 2
        self.capacity = rows // self.span
        self.part = self.capacity // 2
        self.part_pad = -(-self.part // 8) * 8
        self.packed = self.span * self.part_pad
        self.slots = 2 * self.packed
        self.swap_x = self.full({})
        boundaries = [z for z in range(self.pairs - 1) if z + 1 != self.inlet]
        self.swap_z = []
        for parity in (0, 1):
            moves = {}
            for z in boundaries:
                if z % 2 == parity:
                    for x in range(2):
                        for j in range(self.span):
                            a, b = self.at(z, x, j), self.at(z + 1, x, j)
                            moves[a], moves[b] = b, a
            if moves:
                self.swap_z.append(self.full(moves))
        self.swap_face = []
        for turn in range(self.chips):
            moves = {}
            for x in range(2):
                for j in range(self.span):
                    other = ((j // 2 + turn) % self.chips) * 2 + j % 2
                    a, b = self.at(self.inlet - 1, x, j), self.at(self.inlet, x, other)
                    moves[a], moves[b] = b, a
            self.swap_face.append(self.full(moves))
        every = [(z, j) for z in range(self.pairs) for j in range(self.span)]
        self.swap_x = self.full(
            {self.at(z, x, j): self.at(z, 1 - x, j) for z, j in every for x in range(2)}
        )
        moves = {}
        for z, j in every:
            a, b = self.at(z, 1, j), self.at(z, 0, (j + 1) % self.span)
            moves[a], moves[b] = b, a
        self.swap_span = self.full(moves)
        self.swap_core = self.full({})

    def at(self, z, x, j):
        return (2 * z + x) * self.span + j

    def full(self, moves):
        count = self.stream * self.span
        return [(d, moves.get(d, d ^ 1)) for d in range(count)]


def place():
    s = lax.axis_index("stream")
    return s // 2, lax.rem(s, 2), lax.axis_index("span")


def lane_ids(rows):
    return lax.broadcasted_iota(jnp.int32, (rows, LANES), 1)


def split2(values):
    high = values.astype(bf16)
    return high, (values - high.astype(f32)).astype(bf16)


def dot(a, b, dims=((1,), (0,))):
    return lax.dot_general(a, b, (dims, ((), ())), preferred_element_type=f32)


def pack(block, high):
    rows = block.shape[0] // 2
    return jnp.where(
        lane_ids(rows) < HALF,
        pltpu.roll(block[:rows], HALF * high, 1),
        pltpu.roll(block[rows:], HALF * (1 - high), 1),
    )


def unpack(packed, high):
    return jnp.concatenate(
        [pltpu.roll(packed, HALF * high, 1), pltpu.roll(packed, HALF * (1 - high), 1)], axis=0
    )


def pack_kernel(block_ref, out_ref):
    _, x, _ = place()
    for c in range(NC):
        out_ref[c] = pack(block_ref[c], 1 - x)


def slot_kernel(plan, source_ref, put_ref, get_ref):
    rows, span, chips = plan.rows, plan.span, plan.chips
    z, _, j = place()
    source = source_ref[...]
    own_chip, own_core = j // 2, lax.rem(j, 2)

    def order(other, sign):
        core = jnp.where(other % 2 == own_core, 0, 1)
        turn = lax.rem(sign * (other // 2 - own_chip) + chips, chips)
        return ((core * chips + turn) * plan.part_pad).astype(f32)

    before = (
        lax.broadcasted_iota(jnp.int32, (rows, rows), 0)
        < lax.broadcasted_iota(jnp.int32, (rows, rows), 1)
    )
    before = jnp.where(before, 1.0, 0.0).astype(bf16)
    sub = lax.broadcasted_iota(jnp.int32, (rows, rows), 0)
    lane = lax.broadcasted_iota(jnp.int32, (rows, rows), 1)
    arrival = jnp.zeros(source.shape, f32)
    base = jnp.zeros(source.shape, f32)
    for d in range(span):
        here = jnp.where((source >= d * rows) & (source < (d + 1) * rows), 1.0, 0.0)
        arrival += here * dot(here.astype(bf16), before)
        base += here * order(d, -1)
    late = jnp.where(arrival >= plan.part, 1.0, 0.0)
    within = arrival + late * (plan.packed - plan.part)
    own = lax.broadcasted_iota(jnp.int32, source.shape, 0) == j
    stator_row = jnp.sum(jnp.where(own, base + within, 0.0), axis=0, keepdims=True)
    total = jnp.zeros((rows, rows), f32)
    for d in range(span):
        match = source[d : d + 1] - j * rows == sub
        total += jnp.where(match, within[d : d + 1] + order(d, 1), 0.0)
    rotor_col = jnp.sum(total, axis=1, keepdims=True)
    same = sub == lane
    stator_col = jnp.sum(jnp.where(same, stator_row, 0.0), axis=1, keepdims=True)
    rotor_row = jnp.sum(jnp.where(same, rotor_col, 0.0), axis=0, keepdims=True)
    stator = z == plan.inlet
    col = jnp.where(stator, stator_col, rotor_col).astype(jnp.int32)
    row = jnp.where(stator, stator_row, rotor_row).astype(jnp.int32)
    put = lax.broadcasted_iota(jnp.int32, (plan.slots, rows), 0) == row
    get = lax.broadcasted_iota(jnp.int32, (rows, plan.slots), 1) == col
    put_ref[...] = jnp.where(put, 1.0, 0.0).astype(bf16)
    get_ref[...] = jnp.where(get, 1.0, 0.0).astype(bf16)


def carried_kernel(plan, adjoint_ref, inverse_ref, carried_ref, out_ref):
    size = plan.block_rows
    for b in range(plan.blocks):
        rounded = jnp.concatenate(
            [adjoint_ref[c, b * size : (b + 1) * size].astype(bf16) for c in range(NC)], axis=0
        )
        product = dot(inverse_ref[b], rounded, ((0,), (0,)))
        for c in range(NC):
            carried_ref[c, b * size : (b + 1) * size] = product[c * size : (c + 1) * size]
    _, x, _ = place()
    for c in range(NC):
        out_ref[c] = pack(carried_ref[c], 1 - x)


def edge_pick(c, low, value_rows=16):
    row = lax.broadcasted_iota(jnp.int32, (value_rows, LANES), 0)
    lane = lax.broadcasted_iota(jnp.int32, (value_rows, LANES), 1)
    hit = ((row == c) & (lane == low)) | ((row == 8 + c) & (lane == low + HALF))
    return jnp.where(hit, 1.0, 0.0).astype(bf16)


def send_parts(plan, field, put_ref, z_refs, face_ref, span_ref, x_ref):
    z, x, _ = place()
    odd = lax.rem(z, 2)
    rotor = z < plan.inlet
    lane = lane_ids(plan.rows)
    keep = jnp.logical_xor(lane < HALF, rotor)
    put = put_ref[...]
    span_edge = jnp.zeros((16, plan.rows), f32)
    x_edge = jnp.zeros((16, plan.rows), f32)
    for c in range(NC):
        block = field(c)
        for parity, ref in enumerate(z_refs):
            ref[c] = pack(block, 1 - odd if parity == 0 else odd)
        both = jnp.where(keep, block, pltpu.roll(block, HALF, 1))
        moved = dot(put, jnp.concatenate(split2(both), axis=1))
        moved = moved[:, :LANES] + moved[:, LANES:]
        packed = jnp.where(lane_ids(plan.packed) < HALF, moved[: plan.packed], moved[plan.packed :])
        for core in range(2):
            for turn in range(plan.chips):
                at = (core * plan.chips + turn) * plan.part_pad
                face_ref[core, turn, c] = packed[at : at + plan.part_pad]
        high, low = split2(block)
        nt = ((1,), (1,))
        pick_span, pick_x = edge_pick(c, 63 * x), edge_pick(c, 63 * (1 - x))
        span_edge += dot(pick_span, high, nt) + dot(pick_span, low, nt)
        x_edge += dot(pick_x, high, nt) + dot(pick_x, low, nt)
    span_ref[...] = span_edge
    x_ref[...] = x_edge


def stencil(plan, c, block, got, get, coef_down, coef_up):
    z_refs, face_refs, edge_high, edge_low = got
    z, x, _ = place()
    odd = lax.rem(z, 2)
    lane = lane_ids(plan.rows)
    low = lane < HALF
    packed = jnp.concatenate(
        [face_refs[t][core, c] for core in range(2) for t in range(plan.chips)], axis=0
    )
    turned = pltpu.roll(packed, HALF, 1)
    low_p = lane_ids(plan.packed) < HALF
    both = jnp.concatenate(
        [jnp.where(low_p, packed, turned), jnp.where(low_p, turned, packed)], axis=0
    )
    other = dot(get, jnp.concatenate(split2(both), axis=1))
    other = other[:, :LANES] + other[:, LANES:]
    at_face = (z == plan.inlet) | (z == plan.inlet - 1)
    at_end = (z == 0) | (z == plan.pairs - 1)
    if len(z_refs) > 1:
        second = unpack(z_refs[1][c], odd)
        other = jnp.where(at_face, other, jnp.where(at_end, 0.0, second))
    else:
        other = jnp.where(at_face, other, 0.0)
    halo = jnp.where(jnp.logical_xor(low, odd == 1), other, unpack(z_refs[0][c], 1 - odd))
    across = pltpu.roll(block, HALF, 1)
    upstream = jnp.where(low, halo, across)
    downstream = jnp.where(low, across, halo)
    spots = jnp.concatenate([edge_pick(c, 63 * x), edge_pick(c, 63 * (1 - x))], axis=0)
    tn = ((0,), (0,))
    ghost = dot(edge_high, spots, tn) + dot(edge_low, spots, tn)
    cell = jnp.bitwise_and(lane, HALF - 1)
    left = jnp.where(cell == 0, 0.0, pltpu.roll(block, 1, 1))
    right = jnp.where(cell == HALF - 1, 0.0, pltpu.roll(block, LANES - 1, 1))
    lateral_sum = left + right + ghost - 2.0 * block
    return (
        coef_down * downstream
        + coef_up * upstream
        - 2.0 * DISSIPATION[c] * block
        + SPREADING[c] * lateral_sum
    )


def paired(plan, own, arrived, x):
    return jnp.where(jnp.logical_xor(lane_ids(plan.rows) < HALF, x == 1), own, unpack(arrived, 1 - x))


def coefficients(c):
    down = -0.5 * ADVECTION[c] + DISSIPATION[c]
    up = 0.5 * ADVECTION[c] + DISSIPATION[c]
    return down, up


def first_kernel(plan, block_ref, arrived_ref, put_ref, state_ref, flux_ref, *outs):
    _, x, _ = place()

    def field(c):
        state = paired(plan, block_ref[c], arrived_ref[c], x)
        flux = jnp.tanh(state)
        state_ref[c] = state
        flux_ref[c] = flux
        return flux

    count = len(plan.swap_z)
    send_parts(plan, field, put_ref, outs[:count], *outs[count:])


def arrived_parts(plan, refs):
    count = len(plan.swap_z)
    z_refs, refs = refs[:count], refs[count:]
    face_refs, refs = refs[: plan.chips], refs[plan.chips :]
    edges = jnp.concatenate([refs[0][...], refs[1][...]], axis=0)
    return (z_refs, face_refs) + split2(edges), refs[2:]


def second_kernel(plan, state_ref, flux_ref, carried_ref, arrived_ref, put_ref, get_ref, *refs):
    _, x, _ = place()
    got, refs = arrived_parts(plan, refs)
    weighted_ref, refs = refs[0], refs[1:]
    get = get_ref[...]

    def field(c):
        down, up = coefficients(c)
        change = stencil(plan, c, flux_ref[c], got, get, down, up)
        slope = jnp.tanh(state_ref[c] + time_step * change)
        slope = 2.0 - slope * slope
        weighted = slope * paired(plan, carried_ref[c], arrived_ref[c], x)
        weighted_ref[c] = weighted
        return weighted

    count = len(plan.swap_z)
    send_parts(plan, field, put_ref, refs[:count], *refs[count:])


def third_kernel(plan, weighted_ref, flux_ref, get_ref, *refs):
    _, x, _ = place()
    got, refs = arrived_parts(plan, refs)
    result_ref, out_ref = refs
    get = get_ref[...]
    for c in range(NC):
        down, up = coefficients(c)
        weighted, flux = weighted_ref[c], flux_ref[c]
        change = stencil(plan, c, weighted, got, get, up, down)
        result = weighted + time_step * (1.0 - flux * flux) * change
        result_ref[c] = result
        out_ref[c] = pack(result, 1 - x)


def last_kernel(plan, result_ref, arrived_ref, out_ref):
    _, x, _ = place()
    for c in range(NC):
        out_ref[c] = paired(plan, result_ref[c], arrived_ref[c], x)


def call(kernel, outs, *args):
    whole = pl.BlockSpec(memory_space=pltpu.VMEM)
    return pl.pallas_call(
        kernel,
        out_shape=[jax.ShapeDtypeStruct(shape, dtype) for shape, dtype in outs],
        in_specs=[whole] * len(args),
        out_specs=[whole] * len(outs),
        compiler_params=pltpu.CompilerParams(vmem_limit_bytes=32 * 2**20),
    )(*args)


def bind(kernel, plan):
    def bound(*refs):
        kernel(plan, *refs)

    return bound


def exchange(plan, parts):
    count = len(plan.swap_z)
    face, span_edge, x_edge = parts[count:]
    crossed = lax.ppermute(face[1], AXES, plan.swap_core)
    z_got = [lax.ppermute(part, AXES, perm) for part, perm in zip(parts, plan.swap_z)]
    face_got = [
        lax.ppermute(jnp.stack([face[0, t], crossed[t]]), AXES, plan.swap_face[t])
        for t in range(plan.chips)
    ]
    span_got = lax.ppermute(span_edge, AXES, plan.swap_span)
    x_got = lax.ppermute(x_edge, AXES, plan.swap_x)
    return z_got + face_got + [span_got, x_got]


def solution(mesh):
    def local(checkpoint, adjoint, line_inverse, row_source):
        rows = checkpoint.shape[1]
        blocks = line_inverse.shape[1]
        plan = Plan(mesh, rows, blocks, rows // blocks)
        full, half = (NC, rows, LANES), (NC, rows // 2, LANES)
        checkpoint = checkpoint.reshape(full)
        adjoint = adjoint.reshape(full)
        inverse = line_inverse.reshape(line_inverse.shape[1:])
        source = row_source.reshape(plan.span, rows)
        source = jnp.pad(source, ((0, -plan.span % 8), (0, 0)), constant_values=-1)
        parts = (
            [(half, f32)] * len(plan.swap_z)
            + [((2, plan.chips, NC, plan.part_pad, LANES), f32)]
            + [((16, rows), f32)] * 2
        )
        (mine,) = call(pack_kernel, [(half, f32)], checkpoint)
        state_got = lax.ppermute(mine, AXES, plan.swap_x)
        carried, mine = call(
            bind(carried_kernel, plan), [(full, f32), (half, f32)], adjoint, inverse
        )
        carried_got = lax.ppermute(mine, AXES, plan.swap_x)
        put, get = call(
            bind(slot_kernel, plan),
            [((plan.slots, rows), bf16), ((rows, plan.slots), bf16)],
            source,
        )
        state, flux, *sent = call(
            bind(first_kernel, plan), [(full, f32)] * 2 + parts, checkpoint, state_got, put
        )
        got = exchange(plan, sent)
        weighted, *sent = call(
            bind(second_kernel, plan),
            [(full, f32)] + parts,
            *(state, flux, carried, carried_got, put, get),
            *got,
        )
        got = exchange(plan, sent)
        result, mine = call(
            bind(third_kernel, plan), [(full, f32), (half, f32)], weighted, flux, get, *got
        )
        result_got = lax.ppermute(mine, AXES, plan.swap_x)
        (out,) = call(bind(last_kernel, plan), [(full, f32)], result, result_got)
        return out.reshape(NC, rows, 1, LANES)

    return jax.shard_map(
        local,
        mesh=mesh,
        in_specs=(
            P(None, None, "stream", "span"),
            P(None, None, "stream", "span"),
            P("stream", None, None, None),
            P(),
        ),
        out_specs=P(None, None, "stream", "span"),
        check_vma=False,
    )
```

time: 140 us -> 43.9 us (0.31)
  the two profiles are of different devices: /device:TPU:17 before, /device:TPU:0 now
where the time goes in v1:
time: 43.9 us; the launch traced here: 43.7 us
  waiting for transfers between devices  17.8 us (41%)
  starting transfers between devices  17.2 us (39%)
  Pallas kernels  6.33 us (14%)
  local copies, waits for them, and re-layouts  2.21 us (5%)
    pallas_call x7, Pallas kernels, call(): pl.pallas_call(kernel, out_shape=[jax.ShapeDtypeStruct(shape, dtype) for...  6.33 us
    ppermute x1, waiting for transfers between devices, local(): result_got = lax.ppermute(mine, AXES, plan.swap_x)  6.23 us
    ppermute x2, starting transfers between devices, exchange(): lax.ppermute(part, AXES, perm)  6.21 us
    ppermute x2, waiting for transfers between devices, exchange(): span_got = lax.ppermute(span_edge, AXES, plan.swap_span)  4.05 us
    ppermute x1, waiting for transfers between devices, local(): state_got = lax.ppermute(mine, AXES, plan.swap_x)  3.82 us
    ppermute x2, starting transfers between devices, exchange(): span_got = lax.ppermute(span_edge, AXES, plan.swap_span)  3.5 us
    ppermute x1, starting transfers between devices, local(): state_got = lax.ppermute(mine, AXES, plan.swap_x)  3 us
    ppermute x2, waiting for transfers between devices, exchange(): x_got = lax.ppermute(x_edge, AXES, plan.swap_x)  2.85 us
  transfers between devices with their start and end apart: 15, of which 7 were waited for; matrix products, arithmetic and copies ran while one was open for 0% of the time, Pallas kernels for 4%

profile of v1, /device:TPU:0, one launch (start us, length us, event | category | flops | bytes accessed | tf_op | source)
XLA Modules:
  0.0 43.7 jit_solution(8668885280200088234)
XLA Ops:
  0.0 0.0 copy-start
  0.0 1.0 %copy-done = f32[5,192,1,128]{3,2,1,0:T(1,128)S(1)} copy-done((f32[5,192,1,128]{3,2,1,0:T(1,128)S(1)}, f32[5,192,1,128]{3,2,1,0:T(1,128)}, u32[]{:S(2)}) %copy-start) | copy-done | bytes 491544
  1.0 0.0 copy-start.2
  1.0 0.2 shard_map.46
  1.2 3.0 %collective-permute-start = (f32[5,96,128]{2,1,0:T(8,128)S(1)}, f32[5,96,128]{2,1,0:T(8,128)S(1)}, u32[]{:S(2)}, u32[]{:S(2)}) collective-permute-start(f32[5,96,128]{2,1,0:T(8,128)S(1)} %shard_map.46), channel_id=1, source_target_pairs={{0,4},{1,5},{2,6},{3,7},{4,0},{5,1},{6,2},{7,3},{8,12},{9,13},{10,... | collective-permute-start | bytes 737288 | tf_op jit(solution)/shard_map/ppermute | solution.py:374
  4.2 0.0 copy-done.2
  4.2 0.0 copy-start.3
  4.2 1.0 %copy-done.3 = f32[5,192,1,128]{3,2,1,0:T(1,128)S(1)} copy-done((f32[5,192,1,128]{3,2,1,0:T(1,128)S(1)}, f32[5,192,1,128]{3,2,1,0:T(1,128)}, u32[]{:S(2)}) %copy-start.3) | copy-done | bytes 491544
  5.3 0.0 copy-start.4
  5.3 0.0 copy-start.1
  5.3 0.5 %shard_map.49 = (f32[5,192,128]{2,1,0:T(8,128)S(1)}, f32[5,96,128]{2,1,0:T(8,128)S(1)}) custom-call(f32[5,192,128]{2,1,0:T(8,128)S(1)} %bitcast.21, bf16[3,320,320]{2,1,0:T(8,128)(2,1)S(1)} %bitcast.20), custom_call_target="tpu_custom_call" | custom-call | tf_op jit(solution)/shard_map/pallas_call | solution.py:327
  5.8 0.9 %collective-permute-start.1 = (f32[5,96,128]{2,1,0:T(8,128)S(1)}, f32[5,96,128]{2,1,0:T(8,128)S(1)}, u32[]{:S(2)}, u32[]{:S(2)}) collective-permute-start(f32[5,96,128]{2,1,0:T(8,128)S(1)} %get-tuple-element.26), channel_id=1, source_target_pairs={{0,4},{1,5},{2,6},{3,7},{4,0},{5,1},{6,2},{7,3},{8,12},{9,13},{10,... | collective-permute-start | bytes 737288 | tf_op jit(solution)/shard_map/ppermute | solution.py:378
  6.7 0.0 copy-done.4
  6.7 0.1 reshape.16
  6.8 0.4 shard_map.47
  7.2 3.8 %collective-permute-done.refs_1_ = f32[5,96,128]{2,1,0:T(8,128)S(1)} collective-permute-done((f32[5,96,128]{2,1,0:T(8,128)S(1)}, f32[5,96,128]{2,1,0:T(8,128)S(1)}, u32[]{:S(2)}, u32[]{:S(2)}) %collective-permute-start) | collective-permute-done | bytes 245792 | tf_op jit(solution)/shard_map/ppermute | solution.py:374
  11.0 0.0 copy-done.1
  11.0 0.9 %shard_map.48 = (f32[5,192,128]{2,1,0:T(8,128)S(1)}, f32[5,192,128]{2,1,0:T(8,128)S(1)}, f32[5,96,128]{2,1,0:T(8,128)S(1)}, f32[2,2,5,24,128]{4,3,2,1,0:T(8,128)...) custom-call(f32[5,192,128]{2,1,0:T(8,128)S(1)} %bitcast.19, f32[5,96,128]{2,1,0:T(8,128)S(1)} %collective-permute-done.refs_1_, ...), custom_call_target="tpu_custom_call" | custom-call | tf_op jit(solution)/shard_map/pallas_call | solution.py:327
  11.9 0.1 collective-permute-start.3
  12.0 2.2 %collective-permute-start.2 = (f32[5,96,128]{2,1,0:T(8,128)S(1)}, f32[5,96,128]{2,1,0:T(8,128)S(1)}, u32[]{:S(2)}, u32[]{:S(2)}) collective-permute-start(f32[5,96,128]{2,1,0:T(8,128)S(1)} %get-tuple-element.28), channel_id=1, source_target_pairs={{0,8},{1,9},{2,10},{3,11},{4,12},{5,13},{6,14},{7,15},{8,0},{9,1},... | collective-permute-start | bytes 737288 | tf_op jit(solution)/shard_map/ppermute | solution.py:347
  14.2 0.0 collective-permute-done.3
  14.3 0.2 collective-permute-start.4
  14.5 0.4 collective-permute-start.5
  14.9 2.2 %collective-permute-start.6 = (f32[16,192]{1,0:T(8,128)S(1)}, f32[16,192]{1,0:T(8,128)S(1)}, u32[]{:S(2)}, u32[]{:S(2)}) collective-permute-start(f32[16,192]{1,0:T(8,128)S(1)} %get-tuple-element.30), channel_id=1, source_target_pairs={{0,7},{1,4},{2,5},{3,6},{4,1},{5,2},{6,3},{7,0},{8,15},{9,12},{10,... | collective-permute-start | bytes 36872 | tf_op jit(solution)/shard_map/ppermute | solution.py:352
  17.2 0.0 collective-permute-done.1.refs_3_
  17.2 0.0 collective-permute-start.7
  17.2 1.8 %collective-permute-done.6.refs_9_ = f32[16,192]{1,0:T(8,128)S(1)} collective-permute-done((f32[16,192]{1,0:T(8,128)S(1)}, f32[16,192]{1,0:T(8,128)S(1)}, u32[]{:S(2)}, u32[]{:S(2)}) %collective-permute-start.6) | collective-permute-done | bytes 12320 | tf_op jit(solution)/shard_map/ppermute | solution.py:352
  19.0 1.9 %collective-permute-done.7.refs_10_ = f32[16,192]{1,0:T(8,128)S(1)} collective-permute-done((f32[16,192]{1,0:T(8,128)S(1)}, f32[16,192]{1,0:T(8,128)S(1)}, u32[]{:S(2)}, u32[]{:S(2)}) %collective-permute-start.7) | collective-permute-done | bytes 12320 | tf_op jit(solution)/shard_map/ppermute | solution.py:353
  20.9 0.0 collective-permute-done.4.refs_7_
  20.9 0.0 collective-permute-done.5.refs_8_
  20.9 0.0 collective-permute-done.2.refs_6_
  20.9 2.2 %shard_map.50 = (f32[5,192,128]{2,1,0:T(8,128)S(1)}, f32[5,96,128]{2,1,0:T(8,128)S(1)}, f32[2,2,5,24,128]{4,3,2,1,0:T(8,128)S(1)}, f32[16,192]{1,0:T(8,128)S(1)}, f32[16,192]{1,0:T(8,128)S(1)}) custom-call(f32[5,192,128]{2,1,0:T(8,128)S(1)} %get-tuple-element.23.refs_0_, f32[5,192,128]{2,1,0:T(8,128)S(1)} %get-tuple-element.24.refs_1_, ...), custom_call_target="tpu_custom_call" | custom-call | tf_op jit(solution)/shard_map/pallas_call | solution.py:327
  23.1 0.1 collective-permute-start.9
  23.2 4.0 %collective-permute-start.8 = (f32[5,96,128]{2,1,0:T(8,128)S(1)}, f32[5,96,128]{2,1,0:T(8,128)S(1)}, u32[]{:S(2)}, u32[]{:S(2)}) collective-permute-start(f32[5,96,128]{2,1,0:T(8,128)S(1)} %get-tuple-element.33), channel_id=1, source_target_pairs={{0,8},{1,9},{2,10},{3,11},{4,12},{5,13},{6,14},{7,15},{8,0},{9,1},... | collective-permute-start | bytes 737288 | tf_op jit(solution)/shard_map/ppermute | solution.py:347
  27.2 0.0 collective-permute-done.9
  27.2 0.2 collective-permute-start.10
  27.5 0.4 collective-permute-start.11
  27.9 1.3 %collective-permute-start.12 = (f32[16,192]{1,0:T(8,128)S(1)}, f32[16,192]{1,0:T(8,128)S(1)}, u32[]{:S(2)}, u32[]{:S(2)}) collective-permute-start(f32[16,192]{1,0:T(8,128)S(1)} %get-tuple-element.35), channel_id=1, source_target_pairs={{0,7},{1,4},{2,5},{3,6},{4,1},{5,2},{6,3},{7,0},{8,15},{9,12},{10,... | collective-permute-start | bytes 36872 | tf_op jit(solution)/shard_map/ppermute | solution.py:352
  29.2 0.5 %collective-permute-start.13 = (f32[16,192]{1,0:T(8,128)S(1)}, f32[16,192]{1,0:T(8,128)S(1)}, u32[]{:S(2)}, u32[]{:S(2)}) collective-permute-start(f32[16,192]{1,0:T(8,128)S(1)} %get-tuple-element.36), channel_id=1, source_target_pairs={{0,4},{1,5},{2,6},{3,7},{4,0},{5,1},{6,2},{7,3},{8,12},{9,13},{10,... | collective-permute-start | bytes 36872 | tf_op jit(solution)/shard_map/ppermute | solution.py:353
  29.7 2.3 %collective-permute-done.12.refs_6_ = f32[16,192]{1,0:T(8,128)S(1)} collective-permute-done((f32[16,192]{1,0:T(8,128)S(1)}, f32[16,192]{1,0:T(8,128)S(1)}, u32[]{:S(2)}, u32[]{:S(2)}) %collective-permute-start.12) | collective-permute-done | bytes 12320 | tf_op jit(solution)/shard_map/ppermute | solution.py:352
  31.9 1.0 %collective-permute-done.13.refs_7_ = f32[16,192]{1,0:T(8,128)S(1)} collective-permute-done((f32[16,192]{1,0:T(8,128)S(1)}, f32[16,192]{1,0:T(8,128)S(1)}, u32[]{:S(2)}, u32[]{:S(2)}) %collective-permute-start.13) | collective-permute-done | bytes 12320 | tf_op jit(solution)/shard_map/ppermute | solution.py:353
  32.9 0.0 collective-permute-done.10.refs_4_
  32.9 0.0 collective-permute-done.11.refs_5_
  32.9 0.8 %collective-permute-done.8.refs_3_ = f32[5,96,128]{2,1,0:T(8,128)S(1)} collective-permute-done((f32[5,96,128]{2,1,0:T(8,128)S(1)}, f32[5,96,128]{2,1,0:T(8,128)S(1)}, u32[]{:S(2)}, u32[]{:S(2)}) %collective-permute-start.8) | collective-permute-done | bytes 245792 | tf_op jit(solution)/shard_map/ppermute | solution.py:347
  33.7 1.2 %shard_map.51 = (f32[5,192,128]{2,1,0:T(8,128)S(1)}, f32[5,96,128]{2,1,0:T(8,128)S(1)}) custom-call(f32[5,192,128]{2,1,0:T(8,128)S(1)} %get-tuple-element.32.refs_0_, f32[5,192,128]{2,1,0:T(8,128)S(1)} %get-tuple-element.24.refs_1_, bf16[192,192]{1,0:T(8,128)(2,1)S(1)} %get-tuple-element.27.refs_5_.refs_2_, ...), custom_call_target="tpu_custom_call" | custom-call | tf_op jit(solution)/shard_map/pallas_call | solution.py:327
  34.9 1.5 %collective-permute-start.14 = (f32[5,96,128]{2,1,0:T(8,128)S(1)}, f32[5,96,128]{2,1,0:T(8,128)S(1)}, u32[]{:S(2)}, u32[]{:S(2)}) collective-permute-start(f32[5,96,128]{2,1,0:T(8,128)S(1)} %get-tuple-element.38), channel_id=1, source_target_pairs={{0,4},{1,5},{2,6},{3,7},{4,0},{5,1},{6,2},{7,3},{8,12},{9,13},{10,... | collective-permute-start | bytes 737288 | tf_op jit(solution)/shard_map/ppermute | solution.py:398
  36.5 6.2 %collective-permute-done.14.refs_1_ = f32[5,96,128]{2,1,0:T(8,128)S(1)} collective-permute-done((f32[5,96,128]{2,1,0:T(8,128)S(1)}, f32[5,96,128]{2,1,0:T(8,128)S(1)}, u32[]{:S(2)}, u32[]{:S(2)}) %collective-permute-start.14) | collective-permute-done | bytes 245792 | tf_op jit(solution)/shard_map/ppermute | solution.py:398
  42.7 1.0 %shard_map.52 = f32[5,192,128]{2,1,0:T(8,128)} custom-call(f32[5,192,128]{2,1,0:T(8,128)S(1)} %get-tuple-element.37.refs_0_, f32[5,96,128]{2,1,0:T(8,128)S(1)} %collective-permute-done.14.refs_1_), custom_call_target="tpu_custom_call" | custom-call | tf_op jit(solution)/shard_map/pallas_call | solution.py:327
  (11 shorter events, 0.1 us)
Async XLA Ops:
  0.0 1.0 %copy-start = (f32[5,192,1,128]{3,2,1,0:T(1,128)S(1)}, f32[5,192,1,128]{3,2,1,0:T(1,128)}, u32[]{:S(2)}) copy-start(f32[5,192,1,128]{3,2,1,0:T(1,128)} %param.4) | copy-start | bytes 1474564
  1.0 3.2 %copy-start.2 = (bf16[1,3,320,320]{3,2,1,0:T(8,128)(2,1)S(1)}, bf16[1,3,320,320]{3,2,1,0:T(8,128)(2,1)}, u32[]{:S(2)}) copy-start(bf16[1,3,320,320]{3,2,1,0:T(8,128)(2,1)} %param.6) | copy-start | bytes 1843204
  1.2 9.8 %collective-permute-start = (f32[5,96,128]{2,1,0:T(8,128)S(1)}, f32[5,96,128]{2,1,0:T(8,128)S(1)}, u32[]{:S(2)}, u32[]{:S(2)}) collective-permute-start(f32[5,96,128]{2,1,0:T(8,128)S(1)} %shard_map.46), channel_id=1, source_target_pairs={{0,4},{1,5},{2,6},{3,7},{4,0},{5,1},{6,2},{7,3},{8,12},{9,13},{10,... | collective-permute-start | bytes 737288 | tf_op jit(solution)/shard_map/ppermute | solution.py:374
  4.2 1.0 %copy-start.3 = (f32[5,192,1,128]{3,2,1,0:T(1,128)S(1)}, f32[5,192,1,128]{3,2,1,0:T(1,128)}, u32[]{:S(2)}) copy-start(f32[5,192,1,128]{3,2,1,0:T(1,128)} %param.5) | copy-start | bytes 1474564
  5.3 1.4 %copy-start.4 = (s32[768]{0:T(1024)S(1)}, s32[768]{0:T(1024)}, u32[]{:S(2)}) copy-start(s32[768]{0:T(1024)} %param.7) | copy-start | bytes 9220
  5.3 5.7 %copy-start.1 = (f32[5,192,1,128]{3,2,1,0:T(1,128)S(1)}, f32[5,192,1,128]{3,2,1,0:T(1,128)}, u32[]{:S(2)}) copy-start(f32[5,192,1,128]{3,2,1,0:T(1,128)} %param.4) | copy-start | bytes 1474564
  5.8 11.4 %collective-permute-start.1 = (f32[5,96,128]{2,1,0:T(8,128)S(1)}, f32[5,96,128]{2,1,0:T(8,128)S(1)}, u32[]{:S(2)}, u32[]{:S(2)}) collective-permute-start(f32[5,96,128]{2,1,0:T(8,128)S(1)} %get-tuple-element.26), channel_id=1, source_target_pairs={{0,4},{1,5},{2,6},{3,7},{4,0},{5,1},{6,2},{7,3},{8,12},{9,13},{10,... | collective-permute-start | bytes 737288 | tf_op jit(solution)/shard_map/ppermute | solution.py:378
  11.9 2.3 %collective-permute-start.3 = (f32[2,5,24,128]{3,2,1,0:T(8,128)S(1)}, f32[2,5,24,128]{3,2,1,0:T(8,128)S(1)}, u32[]{:S(2)}, u32[]{:S(2)}) collective-permute-start(f32[2,5,24,128]{3,2,1,0:T(8,128)S(1)} %slice_bitcast_fusion.1), channel_id=1, source_target_pairs={{0,1},{1,0},{2,3},{3,2},{4,5},{5,4},{6,7},{7,6},{8,9},{9,8},{10,11... | collective-permute-start | bytes 368648 | tf_op jit(solution)/shard_map/ppermute | solution.py:346
  12.0 8.9 %collective-permute-start.2 = (f32[5,96,128]{2,1,0:T(8,128)S(1)}, f32[5,96,128]{2,1,0:T(8,128)S(1)}, u32[]{:S(2)}, u32[]{:S(2)}) collective-permute-start(f32[5,96,128]{2,1,0:T(8,128)S(1)} %get-tuple-element.28), channel_id=1, source_target_pairs={{0,8},{1,9},{2,10},{3,11},{4,12},{5,13},{6,14},{7,15},{8,0},{9,1},... | collective-permute-start | bytes 737288 | tf_op jit(solution)/shard_map/ppermute | solution.py:347
  14.3 6.6 %collective-permute-start.4 = (f32[2,5,24,128]{3,2,1,0:T(8,128)S(1)}, f32[2,5,24,128]{3,2,1,0:T(8,128)S(1)}, u32[]{:S(2)}, u32[]{:S(2)}) collective-permute-start(f32[2,5,24,128]{3,2,1,0:T(8,128)S(1)} %pad_maximum_fusion), channel_id=1, source_target_pairs={{0,1},{1,0},{2,3},{3,2},{4,5},{5,4},{6,7},{7,6},{8,16},{9,17},{10,... | collective-permute-start | bytes 368648 | tf_op jit(solution)/shard_map/ppermute | solution.py:349
  14.5 6.4 %collective-permute-start.5 = (f32[2,5,24,128]{3,2,1,0:T(8,128)S(1)}, f32[2,5,24,128]{3,2,1,0:T(8,128)S(1)}, u32[]{:S(2)}, u32[]{:S(2)}) collective-permute-start(f32[2,5,24,128]{3,2,1,0:T(8,128)S(1)} %pad_maximum_fusion.1), channel_id=1, source_target_pairs={{0,1},{1,0},{2,3},{3,2},{4,5},{5,4},{6,7},{7,6},{8,18},{9,19},{10,... | collective-permute-start | bytes 368648 | tf_op jit(solution)/shard_map/ppermute | solution.py:349
  14.9 4.1 %collective-permute-start.6 = (f32[16,192]{1,0:T(8,128)S(1)}, f32[16,192]{1,0:T(8,128)S(1)}, u32[]{:S(2)}, u32[]{:S(2)}) collective-permute-start(f32[16,192]{1,0:T(8,128)S(1)} %get-tuple-element.30), channel_id=1, source_target_pairs={{0,7},{1,4},{2,5},{3,6},{4,1},{5,2},{6,3},{7,0},{8,15},{9,12},{10,... | collective-permute-start | bytes 36872 | tf_op jit(solution)/shard_map/ppermute | solution.py:352
  17.2 3.7 %collective-permute-start.7 = (f32[16,192]{1,0:T(8,128)S(1)}, f32[16,192]{1,0:T(8,128)S(1)}, u32[]{:S(2)}, u32[]{:S(2)}) collective-permute-start(f32[16,192]{1,0:T(8,128)S(1)} %get-tuple-element.31), channel_id=1, source_target_pairs={{0,4},{1,5},{2,6},{3,7},{4,0},{5,1},{6,2},{7,3},{8,12},{9,13},{10,... | collective-permute-start | bytes 36872 | tf_op jit(solution)/shard_map/ppermute | solution.py:353
  23.1 4.1 %collective-permute-start.9 = (f32[2,5,24,128]{3,2,1,0:T(8,128)S(1)}, f32[2,5,24,128]{3,2,1,0:T(8,128)S(1)}, u32[]{:S(2)}, u32[]{:S(2)}) collective-permute-start(f32[2,5,24,128]{3,2,1,0:T(8,128)S(1)} %slice_bitcast_fusion), channel_id=1, source_target_pairs={{0,1},{1,0},{2,3},{3,2},{4,5},{5,4},{6,7},{7,6},{8,9},{9,8},{10,11... | collective-permute-start | bytes 368648 | tf_op jit(solution)/shard_map/ppermute | solution.py:346
  23.2 10.5 %collective-permute-start.8 = (f32[5,96,128]{2,1,0:T(8,128)S(1)}, f32[5,96,128]{2,1,0:T(8,128)S(1)}, u32[]{:S(2)}, u32[]{:S(2)}) collective-permute-start(f32[5,96,128]{2,1,0:T(8,128)S(1)} %get-tuple-element.33), channel_id=1, source_target_pairs={{0,8},{1,9},{2,10},{3,11},{4,12},{5,13},{6,14},{7,15},{8,0},{9,1},... | collective-permute-start | bytes 737288 | tf_op jit(solution)/shard_map/ppermute | solution.py:347
  27.2 5.7 %collective-permute-start.10 = (f32[2,5,24,128]{3,2,1,0:T(8,128)S(1)}, f32[2,5,24,128]{3,2,1,0:T(8,128)S(1)}, u32[]{:S(2)}, u32[]{:S(2)}) collective-permute-start(f32[2,5,24,128]{3,2,1,0:T(8,128)S(1)} %pad_maximum_fusion.2), channel_id=1, source_target_pairs={{0,1},{1,0},{2,3},{3,2},{4,5},{5,4},{6,7},{7,6},{8,16},{9,17},{10,... | collective-permute-start | bytes 368648 | tf_op jit(solution)/shard_map/ppermute | solution.py:349
  27.5 5.4 %collective-permute-start.11 = (f32[2,5,24,128]{3,2,1,0:T(8,128)S(1)}, f32[2,5,24,128]{3,2,1,0:T(8,128)S(1)}, u32[]{:S(2)}, u32[]{:S(2)}) collective-permute-start(f32[2,5,24,128]{3,2,1,0:T(8,128)S(1)} %pad_maximum_fusion.3), channel_id=1, source_target_pairs={{0,1},{1,0},{2,3},{3,2},{4,5},{5,4},{6,7},{7,6},{8,18},{9,19},{10,... | collective-permute-start | bytes 368648 | tf_op jit(solution)/shard_map/ppermute | solution.py:349
  27.9 4.1 %collective-permute-start.12 = (f32[16,192]{1,0:T(8,128)S(1)}, f32[16,192]{1,0:T(8,128)S(1)}, u32[]{:S(2)}, u32[]{:S(2)}) collective-permute-start(f32[16,192]{1,0:T(8,128)S(1)} %get-tuple-element.35), channel_id=1, source_target_pairs={{0,7},{1,4},{2,5},{3,6},{4,1},{5,2},{6,3},{7,0},{8,15},{9,12},{10,... | collective-permute-start | bytes 36872 | tf_op jit(solution)/shard_map/ppermute | solution.py:352
  29.2 3.7 %collective-permute-start.13 = (f32[16,192]{1,0:T(8,128)S(1)}, f32[16,192]{1,0:T(8,128)S(1)}, u32[]{:S(2)}, u32[]{:S(2)}) collective-permute-start(f32[16,192]{1,0:T(8,128)S(1)} %get-tuple-element.36), channel_id=1, source_target_pairs={{0,4},{1,5},{2,6},{3,7},{4,0},{5,1},{6,2},{7,3},{8,12},{9,13},{10,... | collective-permute-start | bytes 36872 | tf_op jit(solution)/shard_map/ppermute | solution.py:353
  34.9 7.8 %collective-permute-start.14 = (f32[5,96,128]{2,1,0:T(8,128)S(1)}, f32[5,96,128]{2,1,0:T(8,128)S(1)}, u32[]{:S(2)}, u32[]{:S(2)}) collective-permute-start(f32[5,96,128]{2,1,0:T(8,128)S(1)} %get-tuple-element.38), channel_id=1, source_target_pairs={{0,4},{1,5},{2,6},{3,7},{4,0},{5,1},{6,2},{7,3},{8,12},{9,13},{10,... | collective-permute-start | bytes 737288 | tf_op jit(solution)/shard_map/ppermute | solution.py:398

commit v2 on v1

v2 whole, which is shorter than its diff:
```python
import jax
import jax.numpy as jnp
from jax import lax
from jax.experimental import pallas as pl
from jax.experimental.pallas import tpu as pltpu
from jax.sharding import PartitionSpec as P

time_step = 0.5
ADVECTION = (1.0, 0.6, 0.8, 1.2, 0.7)
DISSIPATION = (0.3, 0.25, 0.35, 0.3, 0.4)
SPREADING = (0.4, 0.3, 0.5, 0.35, 0.45)
NC = 5
LANES = 128
HALF = 64
AXES = ("stream", "span")
f32 = jnp.float32
bf16 = jnp.bfloat16
GHOST_FLOPS = 10**10


class Plan:
    def __init__(self, mesh, rows, blocks):
        self.stream = mesh.shape["stream"]
        self.span = mesh.shape["span"]
        self.rows = rows
        self.blocks = blocks
        self.block_rows = rows // blocks
        self.pairs = self.stream // 2
        self.inlet = self.stream // 4
        assert self.stream % 4 == 0 and self.inlet % 2 == 0 and self.span % 2 == 0
        self.chips = self.span // 2
        self.capacity = rows // self.span
        self.part = self.capacity // 2
        self.part_pad = -(-self.part // 8) * 8
        self.packed = self.span * self.part_pad
        self.slots = 2 * self.packed
        self.edge_rows = 8 * -(-rows // LANES)
        zs, js = range(self.pairs), range(self.span)
        self.swap_core = self.full({})
        self.swap_x = self.full(
            {self.at(z, x, j): self.at(z, 1 - x, j) for z in zs for j in js for x in range(2)}
        )
        self.swap_z = []
        for parity in (0, 1):
            moves = {}
            for z in zs[:-1]:
                if z % 2 == parity and z + 1 != self.inlet:
                    for x in range(2):
                        for j in js:
                            self.trade(moves, self.at(z, x, j), self.at(z + 1, x, j))
            if moves:
                self.swap_z.append(self.full(moves))
        self.swap_face, self.straight, self.diag = [], [], []
        for turn in range(self.chips):
            face, straight, diag = {}, {}, {}
            for j in js:
                for z in zs[:-1]:
                    up = down = j
                    if z + 1 == self.inlet:
                        up = (j // 2 + turn) % self.chips * 2 + j % 2
                        down = (j // 2 - turn) % self.chips * 2 + j % 2
                        for x in range(2):
                            self.trade(face, self.at(z, x, j), self.at(z + 1, x, up))
                    straight[self.at(z, 0, j)] = self.at(z + 1, 0, up)
                    straight[self.at(z + 1, 1, j)] = self.at(z, 1, down)
                    self.trade(diag, self.at(z, 1, j), self.at(z + 1, 0, up))
                last = self.pairs - 1
                straight[self.at(last, 0, j)] = self.at(last, 1, j)
                straight[self.at(0, 1, j)] = self.at(0, 0, j)
            self.swap_face.append(self.full(face))
            self.straight.append(self.full(straight))
            self.diag.append(self.full(diag))
        outward, inward, cross = {}, {}, {}
        for z in zs:
            for j in js:
                after, before = (j + 1) % self.span, (j - 1) % self.span
                outward[self.at(z, 0, j)] = self.at(z, 0, after)
                outward[self.at(z, 1, j)] = self.at(z, 1, before)
                inward[self.at(z, 0, j)] = self.at(z, 0, before)
                inward[self.at(z, 1, j)] = self.at(z, 1, after)
                self.trade(cross, self.at(z, 1, j), self.at(z, 0, after))
        self.outward, self.inward, self.cross = map(self.full, (outward, inward, cross))

    def at(self, z, x, j):
        return (2 * z + x) * self.span + j

    def trade(self, moves, a, b):
        moves[a], moves[b] = b, a

    def full(self, moves):
        return [(d, moves.get(d, d ^ 1)) for d in range(self.stream * self.span)]


def place():
    s = lax.axis_index("stream")
    return s // 2, lax.rem(s, 2), lax.axis_index("span")


def is_low(rows):
    return lax.broadcasted_iota(jnp.int32, (rows, LANES), 1) < HALF


def split2(values):
    high = values.astype(bf16)
    return high, (values - high.astype(f32)).astype(bf16)


def dot(a, b, dims=((1,), (0,))):
    return lax.dot_general(a, b, (dims, ((), ())), preferred_element_type=f32)


def permuted(matrix, block):
    both = dot(matrix, jnp.concatenate(split2(block), axis=1))
    return both[:, :LANES] + both[:, LANES:]


def half_turn(block):
    return pltpu.roll(block, HALF, 1)


def pack(block, high):
    rows = block.shape[0] // 2
    return jnp.where(
        is_low(rows),
        pltpu.roll(block[:rows], HALF * high, 1),
        pltpu.roll(block[rows:], HALF * (1 - high), 1),
    )


def unpack(packed, high):
    return jnp.concatenate(
        [pltpu.roll(packed, HALF * high, 1), pltpu.roll(packed, HALF * (1 - high), 1)], axis=0
    )


def unpack2(for_low, for_high):
    low = is_low(for_low.shape[0])
    return jnp.concatenate(
        [
            jnp.where(low, for_low, half_turn(for_high)),
            jnp.where(low, half_turn(for_low), for_high),
        ],
        axis=0,
    )


def padded(plan, half):
    gap = plan.packed - half.shape[0]
    return jnp.concatenate([half, jnp.zeros((gap, LANES), f32)], axis=0) if gap else half


def spread(plan, block):
    half = plan.rows // 2
    if plan.packed == half:
        return block
    return jnp.concatenate([padded(plan, block[:half]), padded(plan, block[half:])], axis=0)


def gathered(plan, slots):
    half = plan.rows // 2
    if plan.packed == half:
        return slots
    return jnp.concatenate([slots[:half], slots[plan.packed : plan.packed + half]], axis=0)


def pairing(plan, own, arrived, x):
    return jnp.where(jnp.logical_xor(is_low(plan.rows), x == 1), own, unpack(arrived, 1 - x))


def picks(lanes):
    shape = (8 * len(lanes), NC * LANES)
    row = lax.broadcasted_iota(jnp.int32, shape, 0)
    lane = lax.broadcasted_iota(jnp.int32, shape, 1)
    hit = row < 0
    for i, at in enumerate(lanes):
        for c in range(NC):
            hit = hit | ((row == 8 * i + c) & (lane == c * LANES + at))
    return jnp.where(hit, 1.0, 0.0).astype(bf16)


def edges_of(blocks, lanes):
    blocks = jnp.concatenate([block.astype(bf16) for block in blocks], axis=1)
    return dot(picks(lanes), blocks, ((1,), (1,)))


def edges_at(edges, lanes):
    return dot(edges.astype(bf16), picks(lanes), ((0,), (0,)))


def put_edge(plan, out_ref, i, edge):
    at = NC * plan.rows // 2 + i * plan.edge_rows
    for start in range(0, plan.rows, LANES):
        width = min(LANES, plan.rows - start)
        out_ref[at : at + 8, :width] = edge[:, start : start + width]
        if width < LANES:
            out_ref[at : at + 8, width:] = jnp.zeros((8, LANES - width), f32)
        at += 8


def get_edge(plan, ref, i):
    at = NC * plan.rows // 2 + i * plan.edge_rows
    parts = []
    for start in range(0, plan.rows, LANES):
        parts.append(ref[at : at + 8, : min(LANES, plan.rows - start)])
        at += 8
    return jnp.concatenate(parts, axis=1)


def lateral(block):
    cell = lax.broadcasted_iota(jnp.int32, block.shape, 1) & (HALF - 1)
    left = jnp.where(cell == 0, 0.0, pltpu.roll(block, 1, 1))
    right = jnp.where(cell == HALF - 1, 0.0, pltpu.roll(block, LANES - 1, 1))
    return left + right - 2.0 * block


def coefficients(c):
    down = -0.5 * ADVECTION[c] + DISSIPATION[c]
    up = 0.5 * ADVECTION[c] + DISSIPATION[c]
    return down, up


def pack_kernel(block_ref, out_ref):
    _, x, _ = place()
    for c in range(NC):
        out_ref[c] = pack(block_ref[c], 1 - x)


def slot_kernel(plan, source_ref, put_ref, get_ref):
    rows, span, chips = plan.rows, plan.span, plan.chips
    z, _, j = place()
    source = source_ref[...]
    own_chip, own_core = j // 2, lax.rem(j, 2)

    def order(other, sign):
        core = jnp.where(other % 2 == own_core, 0, 1)
        turn = lax.rem(sign * (other // 2 - own_chip) + chips, chips)
        return ((core * chips + turn) * plan.part_pad).astype(f32)

    sub = lax.broadcasted_iota(jnp.int32, (rows, rows), 0)
    lane = lax.broadcasted_iota(jnp.int32, (rows, rows), 1)
    before = jnp.where(sub < lane, 1.0, 0.0).astype(bf16)
    arrival = jnp.zeros(source.shape, f32)
    base = jnp.zeros(source.shape, f32)
    for d in range(span):
        here = jnp.where((source >= d * rows) & (source < (d + 1) * rows), 1.0, 0.0)
        arrival += here * dot(here.astype(bf16), before)
        base += here * order(d, -1)
    late = jnp.where(arrival >= plan.part, 1.0, 0.0)
    within = arrival + late * (plan.packed - plan.part)
    own = lax.broadcasted_iota(jnp.int32, source.shape, 0) == j
    stator_row = jnp.sum(jnp.where(own, base + within, 0.0), axis=0, keepdims=True)
    total = jnp.zeros((rows, rows), f32)
    for d in range(span):
        match = source[d : d + 1] - j * rows == sub
        total += jnp.where(match, within[d : d + 1] + order(d, 1), 0.0)
    rotor_col = jnp.sum(total, axis=1, keepdims=True)
    same = sub == lane
    stator_col = jnp.sum(jnp.where(same, stator_row, 0.0), axis=1, keepdims=True)
    rotor_row = jnp.sum(jnp.where(same, rotor_col, 0.0), axis=0, keepdims=True)
    stator = z == plan.inlet
    col = jnp.where(stator, stator_col, rotor_col).astype(jnp.int32)
    row = jnp.where(stator, stator_row, rotor_row).astype(jnp.int32)
    put = lax.broadcasted_iota(jnp.int32, (plan.slots, rows), 0) == row
    get = lax.broadcasted_iota(jnp.int32, (rows, plan.slots), 1) == col
    put_ref[...] = jnp.where(put, 1.0, 0.0).astype(bf16)
    get_ref[...] = jnp.where(get, 1.0, 0.0).astype(bf16)


def carried_kernel(plan, adjoint_ref, inverse_ref, carried_ref):
    size = plan.block_rows
    for b in range(plan.blocks):
        rounded = jnp.concatenate(
            [adjoint_ref[c, b * size : (b + 1) * size].astype(bf16) for c in range(NC)], axis=0
        )
        product = dot(inverse_ref[b], rounded, ((0,), (0,)))
        for c in range(NC):
            carried_ref[c, b * size : (b + 1) * size] = product[c * size : (c + 1) * size]


def edge_kernel(plan, block_ref, outward_ref, inward_ref, partner_ref, own_ref):
    _, x, _ = place()
    blocks = [jnp.tanh(block_ref[c]) for c in range(NC)]
    edges = edges_of(blocks, [127 * (1 - x), 127 * x, 63 + x, 64 - x])
    for i, ref in enumerate((outward_ref, inward_ref, partner_ref, own_ref)):
        ref[...] = edges[8 * i : 8 * i + 8]


def share_kernel(plan, carried_ref, partner_ref, inward_ref, *refs):
    out_ref = refs[-1]
    _, x, _ = place()
    half = plan.rows // 2
    for c in range(NC):
        out_ref[c * half : (c + 1) * half] = pack(carried_ref[c], 1 - x)
    put_edge(plan, out_ref, 0, partner_ref[...])
    put_edge(plan, out_ref, 1, inward_ref[...])


def in_slots(plan, block, put):
    z, _, _ = place()
    low = is_low(plan.slots)
    face = jnp.logical_or(
        jnp.logical_and(low, z == plan.inlet),
        jnp.logical_and(jnp.logical_not(low), z == plan.inlet - 1),
    )
    return jnp.where(face, permuted(put, block), spread(plan, block))


def sending(plan, slots):
    turned = half_turn(slots)
    low, n = is_low(plan.packed), plan.packed
    to_before = jnp.where(low, slots[:n], turned[n:])
    to_after = jnp.where(low, turned[:n], slots[n:])
    return to_before, to_after


def put_parts(plan, ref, c, packed):
    for core in range(2):
        for turn in range(plan.chips):
            at = (core * plan.chips + turn) * plan.part_pad
            ref[core, turn, c] = packed[at : at + plan.part_pad]


def get_parts(plan, refs, c):
    parts = [refs[t][core, c] for core in range(2) for t in range(plan.chips)]
    return jnp.concatenate(parts, axis=0)


def first_kernel(plan, block_ref, arrived_ref, put_ref, flux_ref, face_ref, *z_refs):
    z, x, _ = place()
    odd = lax.rem(z, 2) == 1
    put = put_ref[...]
    half = plan.rows // 2
    for c in range(NC):
        flux = jnp.tanh(pairing(plan, block_ref[c], arrived_ref[c], x))
        flux_ref[c] = flux
        to_before, to_after = sending(plan, in_slots(plan, flux, put))
        swap = jnp.where(odd, to_before, to_after)
        other = jnp.where(odd, to_after, to_before)
        z_refs[0][c] = swap[:half]
        if len(z_refs) > 1:
            z_refs[1][c] = other[:half]
        put_parts(plan, face_ref, c, other)


def local_kernel(
    plan, block_ref, arrived_ref, flux_ref, carried_ref, share_ref, *refs
):
    outward_ref, own_ref, base_ref, pair_ref, tangent_ref = refs
    _, x, _ = place()
    half = plan.rows // 2
    low = is_low(plan.rows)
    forwarded, partner = get_edge(plan, share_ref, 1), get_edge(plan, share_ref, 0)
    edges = jnp.concatenate([outward_ref[...], forwarded, partner, own_ref[...]], axis=0)
    ghosts = edges_at(edges, [127 * x, 64 - x, 127 * (1 - x), 63 + x])
    for c in range(NC):
        own, flux = block_ref[c], flux_ref[c]
        state = pairing(plan, own, arrived_ref[c], x)
        down, up = coefficients(c)
        ghost = ghosts[:, c * LANES : (c + 1) * LANES]
        change = (
            jnp.where(low, down, up) * half_turn(flux)
            - 2.0 * DISSIPATION[c] * flux
            + SPREADING[c] * (lateral(flux) + ghost)
        )
        base_ref[c] = state + time_step * change
        share = share_ref[c * half : (c + 1) * half]
        pair_ref[c] = pairing(plan, carried_ref[c], share, x)
        flux = jnp.tanh(own)
        tangent_ref[c] = time_step * (1.0 - flux * flux)


def second_kernel(plan, base_ref, pair_ref, flux_ref, get_ref, put_ref, *refs):
    chips, count = plan.chips, len(plan.swap_z)
    face_refs, z_refs = refs[:chips], refs[chips : chips + count]
    weighted_ref, slots_ref, core_ref, partial_ref = refs[chips + count :]
    z, x, _ = place()
    odd = lax.rem(z, 2) == 1
    low = is_low(plan.rows)
    swapped = jnp.logical_xor(low, jnp.logical_not(odd))
    at_face = jnp.logical_or(z == plan.inlet, z == plan.inlet - 1)
    at_end = jnp.logical_or(z == 0, z == plan.pairs - 1)
    put, get = put_ref[...], get_ref[...]
    for c in range(NC):
        face = get_parts(plan, face_refs, c)
        near = padded(plan, z_refs[0][c])
        slots = unpack2(jnp.where(odd, near, face), jnp.where(odd, face, near))
        moved = permuted(get, slots)
        if count > 1:
            far = padded(plan, z_refs[1][c])
            slots = unpack2(jnp.where(odd, near, far), jnp.where(odd, far, near))
        slots = gathered(plan, slots)
        other = jnp.where(at_face, moved, jnp.where(at_end, 0.0, slots))
        halo = jnp.where(swapped, slots, other)
        down, up = coefficients(c)
        slope = jnp.tanh(base_ref[c] + time_step * jnp.where(low, up, down) * halo)
        weighted = (2.0 - slope * slope) * pair_ref[c]
        weighted_ref[c] = weighted
        flux = flux_ref[c]
        change = (
            jnp.where(low, up, down) * half_turn(weighted)
            - 2.0 * DISSIPATION[c] * weighted
            + SPREADING[c] * lateral(weighted)
        )
        partial = weighted + time_step * (1.0 - flux * flux) * change
        partial_ref[c] = partial
        slots = in_slots(plan, weighted, put)
        slots_ref[c] = slots
        to_before, to_after = sending(plan, slots)
        face = jnp.where(z < plan.inlet, to_after, to_before)
        for turn in range(chips):
            at = (chips + turn) * plan.part_pad
            core_ref[turn, c] = face[at : at + plan.part_pad]


def halo_kernel(plan, weighted_ref, partial_ref, slots_ref, *outs):
    out_ref, straight_ref, diag_ref, *edge_refs = outs
    _, x, _ = place()
    half = plan.rows // 2
    edges = edges_of(
        [weighted_ref[c] for c in range(NC)], [127 * (1 - x), 64 - x, 127 * x, 63 + x]
    )
    put_edge(plan, out_ref, 0, edges[:8])
    for i, ref in enumerate(edge_refs):
        ref[...] = edges[8 * i + 8 : 8 * i + 16]
    for c in range(NC):
        out_ref[c * half : (c + 1) * half] = pack(partial_ref[c], 1 - x)
        to_before, to_after = sending(plan, slots_ref[c])
        put_parts(plan, straight_ref, c, jnp.where(x == 0, to_after, to_before))
        put_parts(plan, diag_ref, c, jnp.where(x == 0, to_before, to_after))


def ghost_kernel(plan, tangent_ref, cross_ref, inward_ref, own_ref, ghost_ref):
    _, x, _ = place()
    edges = jnp.concatenate([cross_ref[...], inward_ref[...], own_ref[...]], axis=0)
    ghosts = edges_at(edges, [127 * x, 127 * (1 - x), 64 - x])
    for c in range(NC):
        ghost = ghosts[:, c * LANES : (c + 1) * LANES]
        ghost_ref[c] = tangent_ref[c] * (SPREADING[c] * ghost)


def last_kernel(plan, partial_ref, ghost_ref, tangent_ref, get_ref, share_ref, *refs):
    chips = plan.chips
    straight_refs, diag_refs, out_ref = refs[:chips], refs[chips : 2 * chips], refs[2 * chips]
    z, x, _ = place()
    half = plan.rows // 2
    first = x == 0
    at_face = z == jnp.where(first, plan.inlet, plan.inlet - 1)
    at_end = z == jnp.where(first, 0, plan.pairs - 1)
    get = get_ref[...]
    ghosts = edges_at(get_edge(plan, share_ref, 0), [63 + x])
    for c in range(NC):
        straight = get_parts(plan, straight_refs, c)
        diag = get_parts(plan, diag_refs, c)
        slots = unpack2(jnp.where(first, straight, diag), jnp.where(first, diag, straight))
        moved = permuted(get, slots)
        halo = jnp.where(at_face, moved, jnp.where(at_end, 0.0, gathered(plan, slots)))
        down, up = coefficients(c)
        ghost = ghosts[:, c * LANES : (c + 1) * LANES]
        change = jnp.where(first, down, up) * halo + SPREADING[c] * ghost
        share = share_ref[c * half : (c + 1) * half]
        partial = pairing(plan, partial_ref[c], share, x) + ghost_ref[c]
        out_ref[c] = partial + tangent_ref[c] * change


def call(kernel, outs, *args, flops=None):
    whole = pl.BlockSpec(memory_space=pltpu.VMEM)
    return pl.pallas_call(
        kernel,
        out_shape=[jax.ShapeDtypeStruct(shape, dtype) for shape, dtype in outs],
        in_specs=[whole] * len(args),
        out_specs=[whole] * len(outs),
        compiler_params=pltpu.CompilerParams(vmem_limit_bytes=32 * 2**20),
        cost_estimate=flops
        and pl.CostEstimate(flops=flops, bytes_accessed=0, transcendentals=0),
    )(*args)


def solution(mesh):
    def local(checkpoint, adjoint, line_inverse, row_source):
        rows = checkpoint.shape[1]
        plan = Plan(mesh, rows, line_inverse.shape[1])
        chips = plan.chips

        def run(kernel, outs, *args, flops=None):
            return call(lambda *refs: kernel(plan, *refs), outs, *args, flops=flops)

        def send(part, moves):
            return lax.ppermute(part, AXES, moves)

        def share(edges):
            return ((NC * rows // 2 + edges * plan.edge_rows, LANES), f32)

        full = ((NC, rows, LANES), f32)
        half = ((NC, rows // 2, LANES), f32)
        edge = ((8, rows), f32)
        parts = ((2, chips, NC, plan.part_pad, LANES), f32)
        put_shape, get_shape = ((plan.slots, rows), bf16), ((rows, plan.slots), bf16)
        checkpoint = checkpoint.reshape(full[0])
        adjoint = adjoint.reshape(full[0])
        inverse = line_inverse.reshape(line_inverse.shape[1:])
        source = row_source.reshape(plan.span, rows)
        source = jnp.pad(source, ((0, -plan.span % 8), (0, 0)), constant_values=-1)

        (mine,) = call(pack_kernel, [half], checkpoint)
        state_got = send(mine, plan.swap_x)
        outward, inward, partner, own = run(edge_kernel, [edge] * 4, checkpoint)
        outward_got = send(outward, plan.outward)
        inward_got = send(inward, plan.inward)
        (carried,) = run(carried_kernel, [full], adjoint, inverse)
        put, get = run(slot_kernel, [put_shape, get_shape], source)
        (mine,) = run(share_kernel, [share(2)], carried, partner, inward_got, outward_got)
        share_got = send(mine, plan.swap_x)
        flux, face, *near = run(
            first_kernel,
            [full, parts] + [half] * len(plan.swap_z),
            *(checkpoint, state_got, put),
        )
        crossed = send(face[1], plan.swap_core)
        near_got = [send(part, moves) for part, moves in zip(near, plan.swap_z)]
        face_got = [
            send(jnp.stack([face[0, t], crossed[t]]), plan.swap_face[t]) for t in range(chips)
        ]
        base, pair, tangent = run(
            local_kernel,
            [full] * 3,
            *(checkpoint, state_got, flux, carried, share_got, outward_got, own),
        )
        weighted, slots, core, partial = run(
            second_kernel,
            [full, ((NC, plan.slots, LANES), f32), (parts[0][1:], f32), full],
            *(base, pair, flux, get, put, *face_got, *near_got),
        )
        crossed = send(core, plan.swap_core)
        mine, straight, diag, cross, inward, own = run(
            halo_kernel, [share(1), parts, parts] + [edge] * 3, weighted, partial, slots
        )
        cross_got = send(cross, plan.cross)
        inward_got = send(inward, plan.inward)
        share_got = send(mine, plan.swap_x)
        (ghost,) = run(
            ghost_kernel, [full], tangent, cross_got, inward_got, own, flops=GHOST_FLOPS
        )
        z, x, _ = place()
        turned = jnp.logical_xor(x == 0, z == plan.inlet)
        at_face = jnp.logical_or(z == plan.inlet, z == plan.inlet - 1)

        def halo(part, moves, by_face):
            other = jnp.where(by_face, crossed, part[1])
            return [send(jnp.stack([part[0, t], other[t]]), moves[t]) for t in range(chips)]

        straight_got = halo(straight, plan.straight, jnp.logical_and(at_face, turned))
        diag_got = halo(diag, plan.diag, jnp.logical_and(at_face, jnp.logical_not(turned)))
        (out,) = run(
            last_kernel,
            [full],
            *(partial, ghost, tangent, get, share_got, *straight_got, *diag_got),
        )
        return out.reshape(NC, rows, 1, LANES)

    return jax.shard_map(
        local,
        mesh=mesh,
        in_specs=(
            P(None, None, "stream", "span"),
            P(None, None, "stream", "span"),
            P("stream", None, None, None),
            P(),
        ),
        out_specs=P(None, None, "stream", "span"),
        check_vma=False,
    )
```

time: 43.9 us -> 38.8 us (0.88)
  the two profiles are of different devices: /device:TPU:0 before, /device:TPU:17 now
where the time goes in v2:
time: 38.8 us; the launch traced here: 38.1 us
  starting transfers between devices  15.4 us (40%)
  waiting for transfers between devices  14.9 us (38%)
  Pallas kernels  5.52 us (14%)
  local copies, waits for them, and re-layouts  1.88 us (5%)
    ppermute x16, starting transfers between devices, send(): return lax.ppermute(part, AXES, moves)  15.4 us
    ppermute x16, waiting for transfers between devices, send(): return lax.ppermute(part, AXES, moves)  14.9 us
    pallas_call x11, Pallas kernels, call(): pl.pallas_call(kernel, out_shape=[jax.ShapeDtypeStruct(shape, dtype) for...  5.52 us
    unnamed x8, local copies, waits for them, and re-layouts  1.04 us
  transfers between devices with their start and end apart: 16, of which 7 were waited for; matrix products, arithmetic and copies ran while one was open for 2% of the time, Pallas kernels for 8%

profile of v2, /device:TPU:17, one launch (start us, length us, event | category | flops | bytes accessed | tf_op | source)
XLA Modules:
  0.0 38.1 jit_solution(9579062893707179407)
XLA Ops:
  0.0 1.0 %copy-done = f32[5,192,1,128]{3,2,1,0:T(1,128)S(1)} copy-done((f32[5,192,1,128]{3,2,1,0:T(1,128)S(1)}, f32[5,192,1,128]{3,2,1,0:T(1,128)}, u32[]{:S(2)}) %copy-start) | copy-done | bytes 491544
  1.0 0.2 shard_map.46
  1.2 1.3 %collective-permute-start = (f32[5,96,128]{2,1,0:T(8,128)S(1)}, f32[5,96,128]{2,1,0:T(8,128)S(1)}, u32[]{:S(2)}, u32[]{:S(2)}) collective-permute-start(f32[5,96,128]{2,1,0:T(8,128)S(1)} %shard_map.46), channel_id=1, source_target_pairs={{0,4},{1,5},{2,6},{3,7},{4,0},{5,1},{6,2},{7,3},{8,12},{9,13},{10,... | collective-permute-start | bytes 737288 | tf_op jit(solution)/shard_map/ppermute | solution.py:488
  2.5 0.2 shard_map.50
  2.7 2.1 %collective-permute-start.2 = (f32[8,192]{1,0:T(8,128)S(1)}, f32[8,192]{1,0:T(8,128)S(1)}, u32[]{:S(2)}, u32[]{:S(2)}) collective-permute-start(f32[8,192]{1,0:T(8,128)S(1)} %get-tuple-element.31), channel_id=1, source_target_pairs={{0,1},{1,2},{2,3},{3,0},{4,7},{5,4},{6,5},{7,6},{8,9},{9,10},{10,1... | collective-permute-start | bytes 18440 | tf_op jit(solution)/shard_map/ppermute | solution.py:488
  4.9 0.0 collective-permute-start.1
  4.9 0.8 %reshape.16 = s32[4,192]{1,0:T(4,128)S(1)} reshape(s32[768]{0:T(1024)} %param.7) | data formatting | bytes 6144 | tf_op jit(solution)/shard_map/reshape | solution.py:501
  5.6 0.4 %shard_map.47 = (bf16[192,192]{1,0:T(8,128)(2,1)S(1)}, bf16[192,192]{1,0:T(8,128)(2,1)S(1)}) custom-call(s32[8,192]{1,0:T(8,128)S(1)} %pad.4.refs_0_), custom_call_target="tpu_custom_call" | custom-call | tf_op jit(solution)/shard_map/pallas_call | solution.py:467
  6.1 0.0 copy-done.2
  6.1 0.0 copy-done.3
  6.1 0.4 %shard_map.49.refs_0_.refs_3_ = f32[5,192,128]{2,1,0:T(8,128)S(1)} custom-call(f32[5,192,128]{2,1,0:T(8,128)S(1)} %bitcast.29, bf16[3,320,320]{2,1,0:T(8,128)(2,1)S(1)} %bitcast.28), custom_call_target="tpu_custom_call" | custom-call | tf_op jit(solution)/shard_map/pallas_call | solution.py:467
  6.5 0.0 copy-start.1
  6.5 0.0 collective-permute-done.2.refs_3_.refs_5_
  6.5 1.7 %collective-permute-done.1.refs_2_ = f32[8,192]{1,0:T(8,128)S(1)} collective-permute-done((f32[8,192]{1,0:T(8,128)S(1)}, f32[8,192]{1,0:T(8,128)S(1)}, u32[]{:S(2)}, u32[]{:S(2)}) %collective-permute-start.1) | collective-permute-done | bytes 6176 | tf_op jit(solution)/shard_map/ppermute | solution.py:488
  8.2 0.2 shard_map.51
  8.5 0.1 collective-permute-start.3
  8.5 0.0 collective-permute-done.refs_1_
  8.6 0.5 %shard_map.48 = (f32[5,192,128]{2,1,0:T(8,128)S(1)}, f32[2,2,5,24,128]{4,3,2,1,0:T(8,128)S(1)}, f32[5,96,128]{2,1,0:T(8,128)S(1)}) custom-call(f32[5,192,128]{2,1,0:T(8,128)S(1)} %bitcast.26, f32[5,96,128]{2,1,0:T(8,128)S(1)} %collective-permute-done.refs_1_, bf16[192,192]{1,0:T(8,128)(2,1)S(1)} %get-tuple-element.27.refs_2_.refs_4_), custom_call_target="tpu_custom_call" | custom-call | tf_op jit(solution)/shard_map/pallas_call | solution.py:467
  9.1 1.2 %collective-permute-start.4 = (f32[2,5,24,128]{3,2,1,0:T(8,128)S(1)}, f32[2,5,24,128]{3,2,1,0:T(8,128)S(1)}, u32[]{:S(2)}, u32[]{:S(2)}) collective-permute-start(f32[2,5,24,128]{3,2,1,0:T(8,128)S(1)} %slice_bitcast_fusion), channel_id=1, source_target_pairs={{0,1},{1,0},{2,3},{3,2},{4,5},{5,4},{6,7},{7,6},{8,9},{9,8},{10,11... | collective-permute-start | bytes 368648 | tf_op jit(solution)/shard_map/ppermute | solution.py:488
  10.3 1.3 %collective-permute-start.7 = (f32[5,96,128]{2,1,0:T(8,128)S(1)}, f32[5,96,128]{2,1,0:T(8,128)S(1)}, u32[]{:S(2)}, u32[]{:S(2)}) collective-permute-start(f32[5,96,128]{2,1,0:T(8,128)S(1)} %get-tuple-element.37), channel_id=1, source_target_pairs={{0,8},{1,9},{2,10},{3,11},{4,12},{5,13},{6,14},{7,15},{8,0},{9,1},... | collective-permute-start | bytes 737288 | tf_op jit(solution)/shard_map/ppermute | solution.py:488
  11.6 0.0 collective-permute-done.4
  11.6 0.1 collective-permute-start.5
  11.7 2.5 %collective-permute-start.6 = (f32[2,5,24,128]{3,2,1,0:T(8,128)S(1)}, f32[2,5,24,128]{3,2,1,0:T(8,128)S(1)}, u32[]{:S(2)}, u32[]{:S(2)}) collective-permute-start(f32[2,5,24,128]{3,2,1,0:T(8,128)S(1)} %pad_maximum_fusion.1), channel_id=1, source_target_pairs={{0,1},{1,0},{2,3},{3,2},{4,5},{5,4},{6,7},{7,6},{8,18},{9,19},{10,... | collective-permute-start | bytes 368648 | tf_op jit(solution)/shard_map/ppermute | solution.py:488
  14.2 2.0 %collective-permute-done.3.refs_4_ = f32[512,128]{1,0:T(8,128)S(1)} collective-permute-done((f32[512,128]{1,0:T(8,128)S(1)}, f32[512,128]{1,0:T(8,128)S(1)}, u32[]{:S(2)}, u32[]{:S(2)}) %collective-permute-start.3) | collective-permute-done | bytes 262176 | tf_op jit(solution)/shard_map/ppermute | solution.py:488
  16.2 0.8 %shard_map.52 = (f32[5,192,128]{2,1,0:T(8,128)S(1)}, f32[5,192,128]{2,1,0:T(8,128)S(1)}, f32[5,192,128]{2,1,0:T(8,128)S(1)}) custom-call(f32[5,192,128]{2,1,0:T(8,128)S(1)} %bitcast.27, f32[5,96,128]{2,1,0:T(8,128)S(1)} %collective-permute-done.refs_1_, f32[5,192,128]{2,1,0:T(8,128)S(1)} %get-tuple-element.28.refs_2_, ...), custom_call_target="tpu_custom_call" | custom-call | tf_op jit(solution)/shard_map/pallas_call | solution.py:467
  17.0 0.0 collective-permute-done.5.refs_5_
  17.0 2.8 %collective-permute-done.6.refs_6_ = f32[2,5,24,128]{3,2,1,0:T(8,128)S(1)} collective-permute-done((f32[2,5,24,128]{3,2,1,0:T(8,128)S(1)}, f32[2,5,24,128]{3,2,1,0:T(8,128)S(1)}, u32[]{:S(2)}, u32[]{:S(2)}) %collective-permute-start.6) | collective-permute-done | bytes 122912 | tf_op jit(solution)/shard_map/ppermute | solution.py:488
  19.8 0.0 collective-permute-done.7.refs_7_
  19.9 0.9 %shard_map.53 = (f32[5,192,128]{2,1,0:T(8,128)S(1)}, f32[5,192,128]{2,1,0:T(8,128)S(1)}, f32[2,5,24,128]{3,2,1,0:T(8,128)S(1)}, f32[5,192,128]{2,1,0:T(8,128)S(1)}) custom-call(f32[5,192,128]{2,1,0:T(8,128)S(1)} %get-tuple-element.33.refs_0_, f32[5,192,128]{2,1,0:T(8,128)S(1)} %get-tuple-element.34.refs_1_, f32[5,192,128]{2,1,0:T(8,128)S(1)} %get-tuple-element.28.refs_2_, ...), custom_call_target="tpu_custom_call" | custom-call | tf_op jit(solution)/shard_map/pallas_call | solution.py:467
  20.8 1.2 %collective-permute-start.11 = (f32[2,5,24,128]{3,2,1,0:T(8,128)S(1)}, f32[2,5,24,128]{3,2,1,0:T(8,128)S(1)}, u32[]{:S(2)}, u32[]{:S(2)}) collective-permute-start(f32[2,5,24,128]{3,2,1,0:T(8,128)S(1)} %get-tuple-element.47), channel_id=1, source_target_pairs={{0,1},{1,0},{2,3},{3,2},{4,5},{5,4},{6,7},{7,6},{8,9},{9,8},{10,11... | collective-permute-start | bytes 368648 | tf_op jit(solution)/shard_map/ppermute | solution.py:488
  22.0 0.3 shard_map.54
  22.4 1.4 %collective-permute-start.8 = (f32[8,192]{1,0:T(8,128)S(1)}, f32[8,192]{1,0:T(8,128)S(1)}, u32[]{:S(2)}, u32[]{:S(2)}) collective-permute-start(f32[8,192]{1,0:T(8,128)S(1)} %get-tuple-element.42), channel_id=1, source_target_pairs={{0,7},{1,4},{2,5},{3,6},{4,1},{5,2},{6,3},{7,0},{8,15},{9,12},{10,... | collective-permute-start | bytes 18440 | tf_op jit(solution)/shard_map/ppermute | solution.py:488
  23.7 0.2 collective-permute-start.9
  24.0 0.4 %collective-permute-start.10 = (f32[496,128]{1,0:T(8,128)S(1)}, f32[496,128]{1,0:T(8,128)S(1)}, u32[]{:S(2)}, u32[]{:S(2)}) collective-permute-start(f32[496,128]{1,0:T(8,128)S(1)} %get-tuple-element.45), channel_id=1, source_target_pairs={{0,4},{1,5},{2,6},{3,7},{4,0},{5,1},{6,2},{7,3},{8,12},{9,13},{10,... | collective-permute-start | bytes 761864 | tf_op jit(solution)/shard_map/ppermute | solution.py:488
  24.4 0.0 collective-permute-done.11
  24.5 2.0 %collective-permute-start.15 = (f32[2,5,24,128]{3,2,1,0:T(8,128)S(1)}, f32[2,5,24,128]{3,2,1,0:T(8,128)S(1)}, u32[]{:S(2)}, u32[]{:S(2)}) collective-permute-start(f32[2,5,24,128]{3,2,1,0:T(8,128)S(1)} %pad_maximum_fusion.5), channel_id=1, source_target_pairs={{0,1},{1,0},{2,3},{3,2},{4,8},{5,9},{6,10},{7,11},{8,4},{9,5},{10,... | collective-permute-start | bytes 368648 | tf_op jit(solution)/shard_map/ppermute | solution.py:488
  26.5 1.5 %collective-permute-start.14 = (f32[2,5,24,128]{3,2,1,0:T(8,128)S(1)}, f32[2,5,24,128]{3,2,1,0:T(8,128)S(1)}, u32[]{:S(2)}, u32[]{:S(2)}) collective-permute-start(f32[2,5,24,128]{3,2,1,0:T(8,128)S(1)} %pad_maximum_fusion.4), channel_id=1, source_target_pairs={{0,1},{1,0},{2,3},{3,2},{4,8},{5,9},{6,10},{7,11},{8,4},{9,5},{10,... | collective-permute-start | bytes 368648 | tf_op jit(solution)/shard_map/ppermute | solution.py:488
  28.0 0.0 collective-permute-done.8.refs_1_
  28.0 0.1 collective-permute-start.13
  28.1 0.0 collective-permute-done.9.refs_2_
  28.1 0.1 collective-permute-start.12
  28.2 0.3 shard_map.55.refs_1_
  28.4 2.6 %collective-permute-done.15.refs_8_ = f32[2,5,24,128]{3,2,1,0:T(8,128)S(1)} collective-permute-done((f32[2,5,24,128]{3,2,1,0:T(8,128)S(1)}, f32[2,5,24,128]{3,2,1,0:T(8,128)S(1)}, u32[]{:S(2)}, u32[]{:S(2)}) %collective-permute-start.15) | collective-permute-done | bytes 122912 | tf_op jit(solution)/shard_map/ppermute | solution.py:488
  31.0 2.9 %collective-permute-done.14.refs_7_ = f32[2,5,24,128]{3,2,1,0:T(8,128)S(1)} collective-permute-done((f32[2,5,24,128]{3,2,1,0:T(8,128)S(1)}, f32[2,5,24,128]{3,2,1,0:T(8,128)S(1)}, u32[]{:S(2)}, u32[]{:S(2)}) %collective-permute-start.14) | collective-permute-done | bytes 122912 | tf_op jit(solution)/shard_map/ppermute | solution.py:488
  33.9 0.0 collective-permute-done.13.refs_6_
  33.9 1.3 %collective-permute-done.12.refs_5_ = f32[2,5,24,128]{3,2,1,0:T(8,128)S(1)} collective-permute-done((f32[2,5,24,128]{3,2,1,0:T(8,128)S(1)}, f32[2,5,24,128]{3,2,1,0:T(8,128)S(1)}, u32[]{:S(2)}, u32[]{:S(2)}) %collective-permute-start.12) | collective-permute-done | bytes 122912 | tf_op jit(solution)/shard_map/ppermute | solution.py:488
  35.2 1.6 %collective-permute-done.10.refs_4_ = f32[496,128]{1,0:T(8,128)S(1)} collective-permute-done((f32[496,128]{1,0:T(8,128)S(1)}, f32[496,128]{1,0:T(8,128)S(1)}, u32[]{:S(2)}, u32[]{:S(2)}) %collective-permute-start.10) | collective-permute-done | bytes 253984 | tf_op jit(solution)/shard_map/ppermute | solution.py:488
  36.8 1.3 %shard_map.56 = f32[5,192,128]{2,1,0:T(8,128)} custom-call(f32[5,192,128]{2,1,0:T(8,128)S(1)} %get-tuple-element.38.refs_1_.refs_0_, f32[5,192,128]{2,1,0:T(8,128)S(1)} %shard_map.55.refs_1_, f32[5,192,128]{2,1,0:T(8,128)S(1)} %get-tuple-element.39.refs_0_.refs_2_, bf16[192,192]{1,0:T(8,128)(2,1)S(1)} %get-tuple-element.35.refs_3_, ...), custom_call_target="tpu_custom_call" | custom-call | tf_op jit(solution)/shard_map/pallas_call | solution.py:467
  (17 shorter events, 0.2 us)
Async XLA Ops:
  0.0 1.0 %copy-start = (f32[5,192,1,128]{3,2,1,0:T(1,128)S(1)}, f32[5,192,1,128]{3,2,1,0:T(1,128)}, u32[]{:S(2)}) copy-start(f32[5,192,1,128]{3,2,1,0:T(1,128)} %param.4) | copy-start | bytes 1474564
  1.0 5.1 %copy-start.2 = (bf16[1,3,320,320]{3,2,1,0:T(8,128)(2,1)S(1)}, bf16[1,3,320,320]{3,2,1,0:T(8,128)(2,1)}, u32[]{:S(2)}) copy-start(bf16[1,3,320,320]{3,2,1,0:T(8,128)(2,1)} %param.6) | copy-start | bytes 1843204
  1.0 5.1 %copy-start.3 = (f32[5,192,1,128]{3,2,1,0:T(1,128)S(1)}, f32[5,192,1,128]{3,2,1,0:T(1,128)}, u32[]{:S(2)}) copy-start(f32[5,192,1,128]{3,2,1,0:T(1,128)} %param.5) | copy-start | bytes 1474564
  1.2 7.3 %collective-permute-start = (f32[5,96,128]{2,1,0:T(8,128)S(1)}, f32[5,96,128]{2,1,0:T(8,128)S(1)}, u32[]{:S(2)}, u32[]{:S(2)}) collective-permute-start(f32[5,96,128]{2,1,0:T(8,128)S(1)} %shard_map.46), channel_id=1, source_target_pairs={{0,4},{1,5},{2,6},{3,7},{4,0},{5,1},{6,2},{7,3},{8,12},{9,13},{10,... | collective-permute-start | bytes 737288 | tf_op jit(solution)/shard_map/ppermute | solution.py:488
  2.7 3.8 %collective-permute-start.2 = (f32[8,192]{1,0:T(8,128)S(1)}, f32[8,192]{1,0:T(8,128)S(1)}, u32[]{:S(2)}, u32[]{:S(2)}) collective-permute-start(f32[8,192]{1,0:T(8,128)S(1)} %get-tuple-element.31), channel_id=1, source_target_pairs={{0,1},{1,2},{2,3},{3,0},{4,7},{5,4},{6,5},{7,6},{8,9},{9,10},{10,1... | collective-permute-start | bytes 18440 | tf_op jit(solution)/shard_map/ppermute | solution.py:488
  4.9 3.4 %collective-permute-start.1 = (f32[8,192]{1,0:T(8,128)S(1)}, f32[8,192]{1,0:T(8,128)S(1)}, u32[]{:S(2)}, u32[]{:S(2)}) collective-permute-start(f32[8,192]{1,0:T(8,128)S(1)} %get-tuple-element.30), channel_id=1, source_target_pairs={{0,3},{1,0},{2,1},{3,2},{4,5},{5,6},{6,7},{7,4},{8,11},{9,8},{10,9... | collective-permute-start | bytes 18440 | tf_op jit(solution)/shard_map/ppermute | solution.py:488
  6.5 2.0 %copy-start.1 = (f32[5,192,1,128]{3,2,1,0:T(1,128)S(1)}, f32[5,192,1,128]{3,2,1,0:T(1,128)}, u32[]{:S(2)}) copy-start(f32[5,192,1,128]{3,2,1,0:T(1,128)} %param.4) | copy-start | bytes 1474564
  8.5 7.8 %collective-permute-start.3 = (f32[512,128]{1,0:T(8,128)S(1)}, f32[512,128]{1,0:T(8,128)S(1)}, u32[]{:S(2)}, u32[]{:S(2)}) collective-permute-start(f32[512,128]{1,0:T(8,128)S(1)} %shard_map.51), channel_id=1, source_target_pairs={{0,4},{1,5},{2,6},{3,7},{4,0},{5,1},{6,2},{7,3},{8,12},{9,13},{10,... | collective-permute-start | bytes 786440 | tf_op jit(solution)/shard_map/ppermute | solution.py:488
  9.1 2.5 %collective-permute-start.4 = (f32[2,5,24,128]{3,2,1,0:T(8,128)S(1)}, f32[2,5,24,128]{3,2,1,0:T(8,128)S(1)}, u32[]{:S(2)}, u32[]{:S(2)}) collective-permute-start(f32[2,5,24,128]{3,2,1,0:T(8,128)S(1)} %slice_bitcast_fusion), channel_id=1, source_target_pairs={{0,1},{1,0},{2,3},{3,2},{4,5},{5,4},{6,7},{7,6},{8,9},{9,8},{10,11... | collective-permute-start | bytes 368648 | tf_op jit(solution)/shard_map/ppermute | solution.py:488
  10.3 9.6 %collective-permute-start.7 = (f32[5,96,128]{2,1,0:T(8,128)S(1)}, f32[5,96,128]{2,1,0:T(8,128)S(1)}, u32[]{:S(2)}, u32[]{:S(2)}) collective-permute-start(f32[5,96,128]{2,1,0:T(8,128)S(1)} %get-tuple-element.37), channel_id=1, source_target_pairs={{0,8},{1,9},{2,10},{3,11},{4,12},{5,13},{6,14},{7,15},{8,0},{9,1},... | collective-permute-start | bytes 737288 | tf_op jit(solution)/shard_map/ppermute | solution.py:488
  11.6 5.4 %collective-permute-start.5 = (f32[2,5,24,128]{3,2,1,0:T(8,128)S(1)}, f32[2,5,24,128]{3,2,1,0:T(8,128)S(1)}, u32[]{:S(2)}, u32[]{:S(2)}) collective-permute-start(f32[2,5,24,128]{3,2,1,0:T(8,128)S(1)} %pad_maximum_fusion), channel_id=1, source_target_pairs={{0,1},{1,0},{2,3},{3,2},{4,5},{5,4},{6,7},{7,6},{8,16},{9,17},{10,... | collective-permute-start | bytes 368648 | tf_op jit(solution)/shard_map/ppermute | solution.py:488
  11.7 8.1 %collective-permute-start.6 = (f32[2,5,24,128]{3,2,1,0:T(8,128)S(1)}, f32[2,5,24,128]{3,2,1,0:T(8,128)S(1)}, u32[]{:S(2)}, u32[]{:S(2)}) collective-permute-start(f32[2,5,24,128]{3,2,1,0:T(8,128)S(1)} %pad_maximum_fusion.1), channel_id=1, source_target_pairs={{0,1},{1,0},{2,3},{3,2},{4,5},{5,4},{6,7},{7,6},{8,18},{9,19},{10,... | collective-permute-start | bytes 368648 | tf_op jit(solution)/shard_map/ppermute | solution.py:488
  20.8 3.6 %collective-permute-start.11 = (f32[2,5,24,128]{3,2,1,0:T(8,128)S(1)}, f32[2,5,24,128]{3,2,1,0:T(8,128)S(1)}, u32[]{:S(2)}, u32[]{:S(2)}) collective-permute-start(f32[2,5,24,128]{3,2,1,0:T(8,128)S(1)} %get-tuple-element.47), channel_id=1, source_target_pairs={{0,1},{1,0},{2,3},{3,2},{4,5},{5,4},{6,7},{7,6},{8,9},{9,8},{10,11... | collective-permute-start | bytes 368648 | tf_op jit(solution)/shard_map/ppermute | solution.py:488
  22.4 5.6 %collective-permute-start.8 = (f32[8,192]{1,0:T(8,128)S(1)}, f32[8,192]{1,0:T(8,128)S(1)}, u32[]{:S(2)}, u32[]{:S(2)}) collective-permute-start(f32[8,192]{1,0:T(8,128)S(1)} %get-tuple-element.42), channel_id=1, source_target_pairs={{0,7},{1,4},{2,5},{3,6},{4,1},{5,2},{6,3},{7,0},{8,15},{9,12},{10,... | collective-permute-start | bytes 18440 | tf_op jit(solution)/shard_map/ppermute | solution.py:488
  23.7 4.3 %collective-permute-start.9 = (f32[8,192]{1,0:T(8,128)S(1)}, f32[8,192]{1,0:T(8,128)S(1)}, u32[]{:S(2)}, u32[]{:S(2)}) collective-permute-start(f32[8,192]{1,0:T(8,128)S(1)} %get-tuple-element.43), channel_id=1, source_target_pairs={{0,3},{1,0},{2,1},{3,2},{4,5},{5,6},{6,7},{7,4},{8,11},{9,8},{10,9... | collective-permute-start | bytes 18440 | tf_op jit(solution)/shard_map/ppermute | solution.py:488
  24.0 12.8 %collective-permute-start.10 = (f32[496,128]{1,0:T(8,128)S(1)}, f32[496,128]{1,0:T(8,128)S(1)}, u32[]{:S(2)}, u32[]{:S(2)}) collective-permute-start(f32[496,128]{1,0:T(8,128)S(1)} %get-tuple-element.45), channel_id=1, source_target_pairs={{0,4},{1,5},{2,6},{3,7},{4,0},{5,1},{6,2},{7,3},{8,12},{9,13},{10,... | collective-permute-start | bytes 761864 | tf_op jit(solution)/shard_map/ppermute | solution.py:488
  24.5 6.5 %collective-permute-start.15 = (f32[2,5,24,128]{3,2,1,0:T(8,128)S(1)}, f32[2,5,24,128]{3,2,1,0:T(8,128)S(1)}, u32[]{:S(2)}, u32[]{:S(2)}) collective-permute-start(f32[2,5,24,128]{3,2,1,0:T(8,128)S(1)} %pad_maximum_fusion.5), channel_id=1, source_target_pairs={{0,1},{1,0},{2,3},{3,2},{4,8},{5,9},{6,10},{7,11},{8,4},{9,5},{10,... | collective-permute-start | bytes 368648 | tf_op jit(solution)/shard_map/ppermute | solution.py:488
  26.5 7.4 %collective-permute-start.14 = (f32[2,5,24,128]{3,2,1,0:T(8,128)S(1)}, f32[2,5,24,128]{3,2,1,0:T(8,128)S(1)}, u32[]{:S(2)}, u32[]{:S(2)}) collective-permute-start(f32[2,5,24,128]{3,2,1,0:T(8,128)S(1)} %pad_maximum_fusion.4), channel_id=1, source_target_pairs={{0,1},{1,0},{2,3},{3,2},{4,8},{5,9},{6,10},{7,11},{8,4},{9,5},{10,... | collective-permute-start | bytes 368648 | tf_op jit(solution)/shard_map/ppermute | solution.py:488
  28.0 5.9 %collective-permute-start.13 = (f32[2,5,24,128]{3,2,1,0:T(8,128)S(1)}, f32[2,5,24,128]{3,2,1,0:T(8,128)S(1)}, u32[]{:S(2)}, u32[]{:S(2)}) collective-permute-start(f32[2,5,24,128]{3,2,1,0:T(8,128)S(1)} %pad_maximum_fusion.3), channel_id=1, source_target_pairs={{0,8},{1,9},{2,10},{3,11},{4,0},{5,1},{6,2},{7,3},{8,18},{9,19},{1... | collective-permute-start | bytes 368648 | tf_op jit(solution)/shard_map/ppermute | solution.py:488
  28.1 7.1 %collective-permute-start.12 = (f32[2,5,24,128]{3,2,1,0:T(8,128)S(1)}, f32[2,5,24,128]{3,2,1,0:T(8,128)S(1)}, u32[]{:S(2)}, u32[]{:S(2)}) collective-permute-start(f32[2,5,24,128]{3,2,1,0:T(8,128)S(1)} %pad_maximum_fusion.2), channel_id=1, source_target_pairs={{0,8},{1,9},{2,10},{3,11},{4,0},{5,1},{6,2},{7,3},{8,16},{9,17},{1... | collective-permute-start | bytes 368648 | tf_op jit(solution)/shard_map/ppermute | solution.py:488

commit v3 on v2

--- a/solution.py
+++ b/solution.py
@@ -15,7 +15,6 @@
 AXES = ("stream", "span")
 f32 = jnp.float32
 bf16 = jnp.bfloat16
-GHOST_FLOPS = 10**10
 
 
 class Plan:
@@ -371,7 +370,7 @@
 
 def second_kernel(plan, base_ref, pair_ref, flux_ref, get_ref, put_ref, *refs):
     chips, count = plan.chips, len(plan.swap_z)
-    face_refs, z_refs = refs[:chips], refs[chips : chips + count]
+    face_refs, z_refs = refs[:chips][::-1], refs[chips : chips + count]
     weighted_ref, slots_ref, core_ref, partial_ref = refs[chips + count :]
     z, x, _ = place()
     odd = lax.rem(z, 2) == 1
@@ -429,25 +428,23 @@
         put_parts(plan, diag_ref, c, jnp.where(x == 0, to_before, to_after))
 
 
-def ghost_kernel(plan, tangent_ref, cross_ref, inward_ref, own_ref, ghost_ref):
+def ghost_kernel(plan, rest_ref, tangent_ref, cross_ref, inward_ref, own_ref, ghost_ref):
     _, x, _ = place()
     edges = jnp.concatenate([cross_ref[...], inward_ref[...], own_ref[...]], axis=0)
     ghosts = edges_at(edges, [127 * x, 127 * (1 - x), 64 - x])
     for c in range(NC):
         ghost = ghosts[:, c * LANES : (c + 1) * LANES]
-        ghost_ref[c] = tangent_ref[c] * (SPREADING[c] * ghost)
-
-
-def last_kernel(plan, partial_ref, ghost_ref, tangent_ref, get_ref, share_ref, *refs):
+        ghost_ref[c] = rest_ref[c] + tangent_ref[c] * (SPREADING[c] * ghost)
+
+
+def rest_kernel(plan, tangent_ref, get_ref, *refs):
     chips = plan.chips
-    straight_refs, diag_refs, out_ref = refs[:chips], refs[chips : 2 * chips], refs[2 * chips]
+    diag_refs, straight_refs, rest_ref = refs[:chips], refs[chips : 2 * chips][::-1], refs[2 * chips]
     z, x, _ = place()
-    half = plan.rows // 2
     first = x == 0
     at_face = z == jnp.where(first, plan.inlet, plan.inlet - 1)
     at_end = z == jnp.where(first, 0, plan.pairs - 1)
     get = get_ref[...]
-    ghosts = edges_at(get_edge(plan, share_ref, 0), [63 + x])
     for c in range(NC):
         straight = get_parts(plan, straight_refs, c)
         diag = get_parts(plan, diag_refs, c)
@@ -455,11 +452,18 @@
         moved = permuted(get, slots)
         halo = jnp.where(at_face, moved, jnp.where(at_end, 0.0, gathered(plan, slots)))
         down, up = coefficients(c)
+        rest_ref[c] = tangent_ref[c] * (jnp.where(first, down, up) * halo)
+
+
+def last_kernel(plan, partial_ref, rest_ref, tangent_ref, share_ref, out_ref):
+    _, x, _ = place()
+    half = plan.rows // 2
+    ghosts = edges_at(get_edge(plan, share_ref, 0), [63 + x])
+    for c in range(NC):
         ghost = ghosts[:, c * LANES : (c + 1) * LANES]
-        change = jnp.where(first, down, up) * halo + SPREADING[c] * ghost
         share = share_ref[c * half : (c + 1) * half]
-        partial = pairing(plan, partial_ref[c], share, x) + ghost_ref[c]
-        out_ref[c] = partial + tangent_ref[c] * change
+        rest = rest_ref[c] + tangent_ref[c] * (SPREADING[c] * ghost)
+        out_ref[c] = pairing(plan, partial_ref[c], share, x) + rest
 
 
 def call(kernel, outs, *args, flops=None):
@@ -528,18 +532,13 @@
         weighted, slots, core, partial = run(
             second_kernel,
             [full, ((NC, plan.slots, LANES), f32), (parts[0][1:], f32), full],
-            *(base, pair, flux, get, put, *face_got, *near_got),
+            *(base, pair, flux, get, put, *face_got[::-1], *near_got),
         )
         crossed = send(core, plan.swap_core)
         mine, straight, diag, cross, inward, own = run(
             halo_kernel, [share(1), parts, parts] + [edge] * 3, weighted, partial, slots
         )
-        cross_got = send(cross, plan.cross)
-        inward_got = send(inward, plan.inward)
         share_got = send(mine, plan.swap_x)
-        (ghost,) = run(
-            ghost_kernel, [full], tangent, cross_got, inward_got, own, flops=GHOST_FLOPS
-        )
         z, x, _ = place()
         turned = jnp.logical_xor(x == 0, z == plan.inlet)
         at_face = jnp.logical_or(z == plan.inlet, z == plan.inlet - 1)
@@ -550,11 +549,12 @@
 
         straight_got = halo(straight, plan.straight, jnp.logical_and(at_face, turned))
         diag_got = halo(diag, plan.diag, jnp.logical_and(at_face, jnp.logical_not(turned)))
-        (out,) = run(
-            last_kernel,
-            [full],
-            *(partial, ghost, tangent, get, share_got, *straight_got, *diag_got),
-        )
+        (cross, inward), _ = lax.optimization_barrier(((cross, inward), diag_got[0]))
+        cross_got = send(cross, plan.cross)
+        inward_got = send(inward, plan.inward)
+        (rest,) = run(rest_kernel, [full], tangent, get, *diag_got, *straight_got[::-1])
+        (ghost,) = run(ghost_kernel, [full], rest, tangent, cross_got, inward_got, own)
+        (out,) = run(last_kernel, [full], partial, ghost, tangent, share_got)
         return out.reshape(NC, rows, 1, LANES)
 
     return jax.shard_map(

time: 38.8 us -> 37.5 us (0.966); the launches traced: 38.1 us -> 37.3 us
  waiting for transfers between devices: 14.9 us -> 13.6 us
  starting transfers between devices: 15.4 us -> 15.8 us
    ppermute x16, waiting for transfers between devices: 14.9 us -> 13.6 us  [send(): return lax.ppermute(part, AXES, moves)]
    ppermute x16, starting transfers between devices: 15.4 us -> 15.8 us  [send(): return lax.ppermute(part, AXES, moves)]
    pallas_call x11 -> x12, Pallas kernels: 5.52 us -> 5.75 us  [call(): pl.pallas_call(kernel, out_shape=[jax.ShapeDtypeStruct(shape, dtype) for...]
  transfers between devices with their start and end apart: 16 -> 16, of which waited for: 7 -> 7; matrix products, arithmetic and copies ran while one was open for 2% -> 3% of each run, Pallas kernels for 8% -> 10%
where the time goes in v3:
time: 37.5 us; the launch traced here: 37.3 us
  starting transfers between devices  15.8 us (42%)
  waiting for transfers between devices  13.6 us (36%)
  Pallas kernels  5.75 us (15%)
  local copies, waits for them, and re-layouts  1.88 us (5%)
    ppermute x16, starting transfers between devices, send(): return lax.ppermute(part, AXES, moves)  15.8 us
    ppermute x16, waiting for transfers between devices, send(): return lax.ppermute(part, AXES, moves)  13.6 us
    pallas_call x12, Pallas kernels, call(): pl.pallas_call(kernel, out_shape=[jax.ShapeDtypeStruct(shape, dtype) for...  5.75 us
    unnamed x8, local copies, waits for them, and re-layouts  1.04 us
    reshape x1, local copies, waits for them, and re-layouts, local(): source = row_source.reshape(plan.span, rows)  0.76 us
  transfers between devices with their start and end apart: 16, of which 7 were waited for; matrix products, arithmetic and copies ran while one was open for 3% of the time, Pallas kernels for 10%

profile of v3, /device:TPU:17, one launch (start us, length us, event | category | flops | bytes accessed | tf_op | source)
XLA Modules:
  0.0 37.3 jit_solution(9685742756660770174)
XLA Ops:
  0.0 1.0 %copy-done = f32[5,192,1,128]{3,2,1,0:T(1,128)S(1)} copy-done((f32[5,192,1,128]{3,2,1,0:T(1,128)S(1)}, f32[5,192,1,128]{3,2,1,0:T(1,128)}, u32[]{:S(2)}) %copy-start) | copy-done | bytes 491544
  1.0 0.2 shard_map.46
  1.2 1.3 %collective-permute-start = (f32[5,96,128]{2,1,0:T(8,128)S(1)}, f32[5,96,128]{2,1,0:T(8,128)S(1)}, u32[]{:S(2)}, u32[]{:S(2)}) collective-permute-start(f32[5,96,128]{2,1,0:T(8,128)S(1)} %shard_map.46), channel_id=1, source_target_pairs={{0,4},{1,5},{2,6},{3,7},{4,0},{5,1},{6,2},{7,3},{8,12},{9,13},{10,... | collective-permute-start | bytes 737288 | tf_op jit(solution)/shard_map/ppermute | solution.py:492
  2.5 0.2 shard_map.50
  2.7 2.1 %collective-permute-start.2 = (f32[8,192]{1,0:T(8,128)S(1)}, f32[8,192]{1,0:T(8,128)S(1)}, u32[]{:S(2)}, u32[]{:S(2)}) collective-permute-start(f32[8,192]{1,0:T(8,128)S(1)} %get-tuple-element.33), channel_id=1, source_target_pairs={{0,1},{1,2},{2,3},{3,0},{4,7},{5,4},{6,5},{7,6},{8,9},{9,10},{10,1... | collective-permute-start | bytes 18440 | tf_op jit(solution)/shard_map/ppermute | solution.py:492
  4.9 0.0 collective-permute-start.1
  4.9 0.8 %reshape.16 = s32[4,192]{1,0:T(4,128)S(1)} reshape(s32[768]{0:T(1024)} %param.7) | data formatting | bytes 6144 | tf_op jit(solution)/shard_map/reshape | solution.py:505
  5.6 0.4 %shard_map.47 = (bf16[192,192]{1,0:T(8,128)(2,1)S(1)}, bf16[192,192]{1,0:T(8,128)(2,1)S(1)}) custom-call(s32[8,192]{1,0:T(8,128)S(1)} %pad.4.refs_0_), custom_call_target="tpu_custom_call" | custom-call | tf_op jit(solution)/shard_map/pallas_call | solution.py:471
  6.1 0.0 copy-done.2
  6.1 0.4 %shard_map.49.refs_0_.refs_3_ = f32[5,192,128]{2,1,0:T(8,128)S(1)} custom-call(f32[5,192,128]{2,1,0:T(8,128)S(1)} %bitcast.29, bf16[3,320,320]{2,1,0:T(8,128)(2,1)S(1)} %bitcast.28), custom_call_target="tpu_custom_call" | custom-call | tf_op jit(solution)/shard_map/pallas_call | solution.py:471
  6.5 0.0 copy-start.1
  6.5 0.0 collective-permute-done.2.refs_3_.refs_5_
  6.5 1.7 %collective-permute-done.1.refs_2_ = f32[8,192]{1,0:T(8,128)S(1)} collective-permute-done((f32[8,192]{1,0:T(8,128)S(1)}, f32[8,192]{1,0:T(8,128)S(1)}, u32[]{:S(2)}, u32[]{:S(2)}) %collective-permute-start.1) | collective-permute-done | bytes 6176 | tf_op jit(solution)/shard_map/ppermute | solution.py:492
  8.2 0.2 shard_map.51
  8.5 0.1 collective-permute-start.3
  8.5 0.0 collective-permute-done.refs_1_
  8.6 0.5 %shard_map.48 = (f32[5,192,128]{2,1,0:T(8,128)S(1)}, f32[2,2,5,24,128]{4,3,2,1,0:T(8,128)S(1)}, f32[5,96,128]{2,1,0:T(8,128)S(1)}) custom-call(f32[5,192,128]{2,1,0:T(8,128)S(1)} %bitcast.26, f32[5,96,128]{2,1,0:T(8,128)S(1)} %collective-permute-done.refs_1_, bf16[192,192]{1,0:T(8,128)(2,1)S(1)} %get-tuple-element.29.refs_2_.refs_4_), custom_call_target="tpu_custom_call" | custom-call | tf_op jit(solution)/shard_map/pallas_call | solution.py:471
  9.1 1.2 %collective-permute-start.4 = (f32[2,5,24,128]{3,2,1,0:T(8,128)S(1)}, f32[2,5,24,128]{3,2,1,0:T(8,128)S(1)}, u32[]{:S(2)}, u32[]{:S(2)}) collective-permute-start(f32[2,5,24,128]{3,2,1,0:T(8,128)S(1)} %slice_bitcast_fusion), channel_id=1, source_target_pairs={{0,1},{1,0},{2,3},{3,2},{4,5},{5,4},{6,7},{7,6},{8,9},{9,8},{10,11... | collective-permute-start | bytes 368648 | tf_op jit(solution)/shard_map/ppermute | solution.py:492
  10.3 1.3 %collective-permute-start.7 = (f32[5,96,128]{2,1,0:T(8,128)S(1)}, f32[5,96,128]{2,1,0:T(8,128)S(1)}, u32[]{:S(2)}, u32[]{:S(2)}) collective-permute-start(f32[5,96,128]{2,1,0:T(8,128)S(1)} %get-tuple-element.39), channel_id=1, source_target_pairs={{0,8},{1,9},{2,10},{3,11},{4,12},{5,13},{6,14},{7,15},{8,0},{9,1},... | collective-permute-start | bytes 737288 | tf_op jit(solution)/shard_map/ppermute | solution.py:492
  11.6 0.0 collective-permute-done.4
  11.6 0.8 %collective-permute-start.5 = (f32[2,5,24,128]{3,2,1,0:T(8,128)S(1)}, f32[2,5,24,128]{3,2,1,0:T(8,128)S(1)}, u32[]{:S(2)}, u32[]{:S(2)}) collective-permute-start(f32[2,5,24,128]{3,2,1,0:T(8,128)S(1)} %pad_maximum_fusion), channel_id=1, source_target_pairs={{0,1},{1,0},{2,3},{3,2},{4,5},{5,4},{6,7},{7,6},{8,18},{9,19},{10,... | collective-permute-start | bytes 368648 | tf_op jit(solution)/shard_map/ppermute | solution.py:492
  12.5 1.7 %collective-permute-start.6 = (f32[2,5,24,128]{3,2,1,0:T(8,128)S(1)}, f32[2,5,24,128]{3,2,1,0:T(8,128)S(1)}, u32[]{:S(2)}, u32[]{:S(2)}) collective-permute-start(f32[2,5,24,128]{3,2,1,0:T(8,128)S(1)} %pad_maximum_fusion.1), channel_id=1, source_target_pairs={{0,1},{1,0},{2,3},{3,2},{4,5},{5,4},{6,7},{7,6},{8,16},{9,17},{10,... | collective-permute-start | bytes 368648 | tf_op jit(solution)/shard_map/ppermute | solution.py:492
  14.2 2.0 %collective-permute-done.3.refs_4_ = f32[512,128]{1,0:T(8,128)S(1)} collective-permute-done((f32[512,128]{1,0:T(8,128)S(1)}, f32[512,128]{1,0:T(8,128)S(1)}, u32[]{:S(2)}, u32[]{:S(2)}) %collective-permute-start.3) | collective-permute-done | bytes 262176 | tf_op jit(solution)/shard_map/ppermute | solution.py:492
  16.2 0.8 %shard_map.52 = (f32[5,192,128]{2,1,0:T(8,128)S(1)}, f32[5,192,128]{2,1,0:T(8,128)S(1)}, f32[5,192,128]{2,1,0:T(8,128)S(1)}) custom-call(f32[5,192,128]{2,1,0:T(8,128)S(1)} %bitcast.27, f32[5,96,128]{2,1,0:T(8,128)S(1)} %collective-permute-done.refs_1_, f32[5,192,128]{2,1,0:T(8,128)S(1)} %get-tuple-element.30.refs_2_, ...), custom_call_target="tpu_custom_call" | custom-call | tf_op jit(solution)/shard_map/pallas_call | solution.py:471
  17.0 0.1 collective-permute-done.5.refs_5_
  17.1 2.7 %collective-permute-done.6.refs_6_ = f32[2,5,24,128]{3,2,1,0:T(8,128)S(1)} collective-permute-done((f32[2,5,24,128]{3,2,1,0:T(8,128)S(1)}, f32[2,5,24,128]{3,2,1,0:T(8,128)S(1)}, u32[]{:S(2)}, u32[]{:S(2)}) %collective-permute-start.6) | collective-permute-done | bytes 122912 | tf_op jit(solution)/shard_map/ppermute | solution.py:492
  19.8 0.0 collective-permute-done.7.refs_7_
  19.9 0.9 %shard_map.53 = (f32[5,192,128]{2,1,0:T(8,128)S(1)}, f32[5,192,128]{2,1,0:T(8,128)S(1)}, f32[2,5,24,128]{3,2,1,0:T(8,128)S(1)}, f32[5,192,128]{2,1,0:T(8,128)S(1)}) custom-call(f32[5,192,128]{2,1,0:T(8,128)S(1)} %get-tuple-element.35.refs_0_, f32[5,192,128]{2,1,0:T(8,128)S(1)} %get-tuple-element.36.refs_1_, f32[5,192,128]{2,1,0:T(8,128)S(1)} %get-tuple-element.30.refs_2_, ...), custom_call_target="tpu_custom_call" | custom-call | tf_op jit(solution)/shard_map/pallas_call | solution.py:471
  20.8 1.2 %collective-permute-start.8 = (f32[2,5,24,128]{3,2,1,0:T(8,128)S(1)}, f32[2,5,24,128]{3,2,1,0:T(8,128)S(1)}, u32[]{:S(2)}, u32[]{:S(2)}) collective-permute-start(f32[2,5,24,128]{3,2,1,0:T(8,128)S(1)} %get-tuple-element.45), channel_id=1, source_target_pairs={{0,1},{1,0},{2,3},{3,2},{4,5},{5,4},{6,7},{7,6},{8,9},{9,8},{10,11... | collective-permute-start | bytes 368648 | tf_op jit(solution)/shard_map/ppermute | solution.py:492
  22.0 0.3 shard_map.54
  22.4 1.5 %collective-permute-start.15 = (f32[496,128]{1,0:T(8,128)S(1)}, f32[496,128]{1,0:T(8,128)S(1)}, u32[]{:S(2)}, u32[]{:S(2)}) collective-permute-start(f32[496,128]{1,0:T(8,128)S(1)} %get-tuple-element.52), channel_id=1, source_target_pairs={{0,4},{1,5},{2,6},{3,7},{4,0},{5,1},{6,2},{7,3},{8,12},{9,13},{10,... | collective-permute-start | bytes 761864 | tf_op jit(solution)/shard_map/ppermute | solution.py:492
  23.9 0.0 collective-permute-done.8
  23.9 0.1 collective-permute-start.9
  24.0 1.7 %collective-permute-start.12 = (f32[2,5,24,128]{3,2,1,0:T(8,128)S(1)}, f32[2,5,24,128]{3,2,1,0:T(8,128)S(1)}, u32[]{:S(2)}, u32[]{:S(2)}) collective-permute-start(f32[2,5,24,128]{3,2,1,0:T(8,128)S(1)} %pad_maximum_fusion.5), channel_id=1, source_target_pairs={{0,8},{1,9},{2,10},{3,11},{4,0},{5,1},{6,2},{7,3},{8,16},{9,17},{1... | collective-permute-start | bytes 368648 | tf_op jit(solution)/shard_map/ppermute | solution.py:492
  25.8 0.1 collective-permute-start.11
  25.9 0.7 %collective-permute-start.10 = (f32[2,5,24,128]{3,2,1,0:T(8,128)S(1)}, f32[2,5,24,128]{3,2,1,0:T(8,128)S(1)}, u32[]{:S(2)}, u32[]{:S(2)}) collective-permute-start(f32[2,5,24,128]{3,2,1,0:T(8,128)S(1)} %pad_maximum_fusion.3), channel_id=1, source_target_pairs={{0,1},{1,0},{2,3},{3,2},{4,8},{5,9},{6,10},{7,11},{8,4},{9,5},{10,... | collective-permute-start | bytes 368648 | tf_op jit(solution)/shard_map/ppermute | solution.py:492
  26.6 3.0 %collective-permute-done.9.refs_2_ = f32[2,5,24,128]{3,2,1,0:T(8,128)S(1)} collective-permute-done((f32[2,5,24,128]{3,2,1,0:T(8,128)S(1)}, f32[2,5,24,128]{3,2,1,0:T(8,128)S(1)}, u32[]{:S(2)}, u32[]{:S(2)}) %collective-permute-start.9) | collective-permute-done | bytes 122912 | tf_op jit(solution)/shard_map/ppermute | solution.py:492
  29.6 1.8 %collective-permute-start.13 = (f32[8,192]{1,0:T(8,128)S(1)}, f32[8,192]{1,0:T(8,128)S(1)}, u32[]{:S(2)}, u32[]{:S(2)}) collective-permute-start(f32[8,192]{1,0:T(8,128)S(1)} %get-tuple-element.49), channel_id=1, source_target_pairs={{0,7},{1,4},{2,5},{3,6},{4,1},{5,2},{6,3},{7,0},{8,15},{9,12},{10,... | collective-permute-start | bytes 18440 | tf_op jit(solution)/shard_map/ppermute | solution.py:492
  31.4 0.0 collective-permute-done.12.refs_5_
  31.4 0.1 collective-permute-start.14
  31.5 0.0 collective-permute-done.11.refs_4_
  31.5 1.2 %collective-permute-done.10.refs_3_ = f32[2,5,24,128]{3,2,1,0:T(8,128)S(1)} collective-permute-done((f32[2,5,24,128]{3,2,1,0:T(8,128)S(1)}, f32[2,5,24,128]{3,2,1,0:T(8,128)S(1)}, u32[]{:S(2)}, u32[]{:S(2)}) %collective-permute-start.10) | collective-permute-done | bytes 122912 | tf_op jit(solution)/shard_map/ppermute | solution.py:492
  32.7 0.4 %shard_map.55.refs_0_ = f32[5,192,128]{2,1,0:T(8,128)S(1)} custom-call(f32[5,192,128]{2,1,0:T(8,128)S(1)} %get-tuple-element.41.refs_0_.refs_1_.refs_2_, bf16[192,192]{1,0:T(8,128)(2,1)S(1)} %get-tuple-element.37.refs_3_.refs_1_, f32[2,5,24,128]{3,2,1,0:T(8,128)S(1)} %collective-permute-done.9.refs_2_, ...), custom_call_target="tpu_custom_call" | custom-call | tf_op jit(solution)/shard_map/pallas_call | solution.py:471
  33.1 2.8 %collective-permute-done.13.refs_2_ = f32[8,192]{1,0:T(8,128)S(1)} collective-permute-done((f32[8,192]{1,0:T(8,128)S(1)}, f32[8,192]{1,0:T(8,128)S(1)}, u32[]{:S(2)}, u32[]{:S(2)}) %collective-permute-start.13) | collective-permute-done | bytes 6176 | tf_op jit(solution)/shard_map/ppermute | solution.py:492
  35.9 0.0 collective-permute-done.14.refs_3_
  35.9 0.3 shard_map.56.refs_1_
  36.2 0.0 collective-permute-done.15.refs_3_
  36.2 1.1 %shard_map.57 = f32[5,192,128]{2,1,0:T(8,128)} custom-call(f32[5,192,128]{2,1,0:T(8,128)S(1)} %get-tuple-element.40.refs_1_.refs_0_, f32[5,192,128]{2,1,0:T(8,128)S(1)} %shard_map.56.refs_1_, f32[5,192,128]{2,1,0:T(8,128)S(1)} %get-tuple-element.41.refs_0_.refs_1_.refs_2_, f32[496,128]{1,0:T(8,128)S(1)} %collective-permute-done.15.refs_3_), custom_call_target="tpu_custom_call" | custom-call | tf_op jit(solution)/shard_map/pallas_call | solution.py:471
  (18 shorter events, 0.2 us)
Async XLA Ops:
  0.0 1.0 %copy-start = (f32[5,192,1,128]{3,2,1,0:T(1,128)S(1)}, f32[5,192,1,128]{3,2,1,0:T(1,128)}, u32[]{:S(2)}) copy-start(f32[5,192,1,128]{3,2,1,0:T(1,128)} %param.4) | copy-start | bytes 1474564
  1.0 5.1 %copy-start.2 = (bf16[1,3,320,320]{3,2,1,0:T(8,128)(2,1)S(1)}, bf16[1,3,320,320]{3,2,1,0:T(8,128)(2,1)}, u32[]{:S(2)}) copy-start(bf16[1,3,320,320]{3,2,1,0:T(8,128)(2,1)} %param.6) | copy-start | bytes 1843204
  1.0 5.1 %copy-start.3 = (f32[5,192,1,128]{3,2,1,0:T(1,128)S(1)}, f32[5,192,1,128]{3,2,1,0:T(1,128)}, u32[]{:S(2)}) copy-start(f32[5,192,1,128]{3,2,1,0:T(1,128)} %param.5) | copy-start | bytes 1474564
  1.2 7.3 %collective-permute-start = (f32[5,96,128]{2,1,0:T(8,128)S(1)}, f32[5,96,128]{2,1,0:T(8,128)S(1)}, u32[]{:S(2)}, u32[]{:S(2)}) collective-permute-start(f32[5,96,128]{2,1,0:T(8,128)S(1)} %shard_map.46), channel_id=1, source_target_pairs={{0,4},{1,5},{2,6},{3,7},{4,0},{5,1},{6,2},{7,3},{8,12},{9,13},{10,... | collective-permute-start | bytes 737288 | tf_op jit(solution)/shard_map/ppermute | solution.py:492
  2.7 3.8 %collective-permute-start.2 = (f32[8,192]{1,0:T(8,128)S(1)}, f32[8,192]{1,0:T(8,128)S(1)}, u32[]{:S(2)}, u32[]{:S(2)}) collective-permute-start(f32[8,192]{1,0:T(8,128)S(1)} %get-tuple-element.33), channel_id=1, source_target_pairs={{0,1},{1,2},{2,3},{3,0},{4,7},{5,4},{6,5},{7,6},{8,9},{9,10},{10,1... | collective-permute-start | bytes 18440 | tf_op jit(solution)/shard_map/ppermute | solution.py:492
  4.9 3.4 %collective-permute-start.1 = (f32[8,192]{1,0:T(8,128)S(1)}, f32[8,192]{1,0:T(8,128)S(1)}, u32[]{:S(2)}, u32[]{:S(2)}) collective-permute-start(f32[8,192]{1,0:T(8,128)S(1)} %get-tuple-element.32), channel_id=1, source_target_pairs={{0,3},{1,0},{2,1},{3,2},{4,5},{5,6},{6,7},{7,4},{8,11},{9,8},{10,9... | collective-permute-start | bytes 18440 | tf_op jit(solution)/shard_map/ppermute | solution.py:492
  6.5 2.0 %copy-start.1 = (f32[5,192,1,128]{3,2,1,0:T(1,128)S(1)}, f32[5,192,1,128]{3,2,1,0:T(1,128)}, u32[]{:S(2)}) copy-start(f32[5,192,1,128]{3,2,1,0:T(1,128)} %param.4) | copy-start | bytes 1474564
  8.5 7.8 %collective-permute-start.3 = (f32[512,128]{1,0:T(8,128)S(1)}, f32[512,128]{1,0:T(8,128)S(1)}, u32[]{:S(2)}, u32[]{:S(2)}) collective-permute-start(f32[512,128]{1,0:T(8,128)S(1)} %shard_map.51), channel_id=1, source_target_pairs={{0,4},{1,5},{2,6},{3,7},{4,0},{5,1},{6,2},{7,3},{8,12},{9,13},{10,... | collective-permute-start | bytes 786440 | tf_op jit(solution)/shard_map/ppermute | solution.py:492
  9.1 2.5 %collective-permute-start.4 = (f32[2,5,24,128]{3,2,1,0:T(8,128)S(1)}, f32[2,5,24,128]{3,2,1,0:T(8,128)S(1)}, u32[]{:S(2)}, u32[]{:S(2)}) collective-permute-start(f32[2,5,24,128]{3,2,1,0:T(8,128)S(1)} %slice_bitcast_fusion), channel_id=1, source_target_pairs={{0,1},{1,0},{2,3},{3,2},{4,5},{5,4},{6,7},{7,6},{8,9},{9,8},{10,11... | collective-permute-start | bytes 368648 | tf_op jit(solution)/shard_map/ppermute | solution.py:492
  10.3 9.6 %collective-permute-start.7 = (f32[5,96,128]{2,1,0:T(8,128)S(1)}, f32[5,96,128]{2,1,0:T(8,128)S(1)}, u32[]{:S(2)}, u32[]{:S(2)}) collective-permute-start(f32[5,96,128]{2,1,0:T(8,128)S(1)} %get-tuple-element.39), channel_id=1, source_target_pairs={{0,8},{1,9},{2,10},{3,11},{4,12},{5,13},{6,14},{7,15},{8,0},{9,1},... | collective-permute-start | bytes 737288 | tf_op jit(solution)/shard_map/ppermute | solution.py:492
  11.6 5.5 %collective-permute-start.5 = (f32[2,5,24,128]{3,2,1,0:T(8,128)S(1)}, f32[2,5,24,128]{3,2,1,0:T(8,128)S(1)}, u32[]{:S(2)}, u32[]{:S(2)}) collective-permute-start(f32[2,5,24,128]{3,2,1,0:T(8,128)S(1)} %pad_maximum_fusion), channel_id=1, source_target_pairs={{0,1},{1,0},{2,3},{3,2},{4,5},{5,4},{6,7},{7,6},{8,18},{9,19},{10,... | collective-permute-start | bytes 368648 | tf_op jit(solution)/shard_map/ppermute | solution.py:492
  12.5 7.4 %collective-permute-start.6 = (f32[2,5,24,128]{3,2,1,0:T(8,128)S(1)}, f32[2,5,24,128]{3,2,1,0:T(8,128)S(1)}, u32[]{:S(2)}, u32[]{:S(2)}) collective-permute-start(f32[2,5,24,128]{3,2,1,0:T(8,128)S(1)} %pad_maximum_fusion.1), channel_id=1, source_target_pairs={{0,1},{1,0},{2,3},{3,2},{4,5},{5,4},{6,7},{7,6},{8,16},{9,17},{10,... | collective-permute-start | bytes 368648 | tf_op jit(solution)/shard_map/ppermute | solution.py:492
  20.8 3.1 %collective-permute-start.8 = (f32[2,5,24,128]{3,2,1,0:T(8,128)S(1)}, f32[2,5,24,128]{3,2,1,0:T(8,128)S(1)}, u32[]{:S(2)}, u32[]{:S(2)}) collective-permute-start(f32[2,5,24,128]{3,2,1,0:T(8,128)S(1)} %get-tuple-element.45), channel_id=1, source_target_pairs={{0,1},{1,0},{2,3},{3,2},{4,5},{5,4},{6,7},{7,6},{8,9},{9,8},{10,11... | collective-permute-start | bytes 368648 | tf_op jit(solution)/shard_map/ppermute | solution.py:492
  22.4 13.9 %collective-permute-start.15 = (f32[496,128]{1,0:T(8,128)S(1)}, f32[496,128]{1,0:T(8,128)S(1)}, u32[]{:S(2)}, u32[]{:S(2)}) collective-permute-start(f32[496,128]{1,0:T(8,128)S(1)} %get-tuple-element.52), channel_id=1, source_target_pairs={{0,4},{1,5},{2,6},{3,7},{4,0},{5,1},{6,2},{7,3},{8,12},{9,13},{10,... | collective-permute-start | bytes 761864 | tf_op jit(solution)/shard_map/ppermute | solution.py:492
  23.9 5.6 %collective-permute-start.9 = (f32[2,5,24,128]{3,2,1,0:T(8,128)S(1)}, f32[2,5,24,128]{3,2,1,0:T(8,128)S(1)}, u32[]{:S(2)}, u32[]{:S(2)}) collective-permute-start(f32[2,5,24,128]{3,2,1,0:T(8,128)S(1)} %pad_maximum_fusion.2), channel_id=1, source_target_pairs={{0,1},{1,0},{2,3},{3,2},{4,8},{5,9},{6,10},{7,11},{8,4},{9,5},{10,... | collective-permute-start | bytes 368648 | tf_op jit(solution)/shard_map/ppermute | solution.py:492
  24.0 7.3 %collective-permute-start.12 = (f32[2,5,24,128]{3,2,1,0:T(8,128)S(1)}, f32[2,5,24,128]{3,2,1,0:T(8,128)S(1)}, u32[]{:S(2)}, u32[]{:S(2)}) collective-permute-start(f32[2,5,24,128]{3,2,1,0:T(8,128)S(1)} %pad_maximum_fusion.5), channel_id=1, source_target_pairs={{0,8},{1,9},{2,10},{3,11},{4,0},{5,1},{6,2},{7,3},{8,16},{9,17},{1... | collective-permute-start | bytes 368648 | tf_op jit(solution)/shard_map/ppermute | solution.py:492
  25.8 5.7 %collective-permute-start.11 = (f32[2,5,24,128]{3,2,1,0:T(8,128)S(1)}, f32[2,5,24,128]{3,2,1,0:T(8,128)S(1)}, u32[]{:S(2)}, u32[]{:S(2)}) collective-permute-start(f32[2,5,24,128]{3,2,1,0:T(8,128)S(1)} %pad_maximum_fusion.4), channel_id=1, source_target_pairs={{0,8},{1,9},{2,10},{3,11},{4,0},{5,1},{6,2},{7,3},{8,18},{9,19},{1... | collective-permute-start | bytes 368648 | tf_op jit(solution)/shard_map/ppermute | solution.py:492
  25.9 6.8 %collective-permute-start.10 = (f32[2,5,24,128]{3,2,1,0:T(8,128)S(1)}, f32[2,5,24,128]{3,2,1,0:T(8,128)S(1)}, u32[]{:S(2)}, u32[]{:S(2)}) collective-permute-start(f32[2,5,24,128]{3,2,1,0:T(8,128)S(1)} %pad_maximum_fusion.3), channel_id=1, source_target_pairs={{0,1},{1,0},{2,3},{3,2},{4,8},{5,9},{6,10},{7,11},{8,4},{9,5},{10,... | collective-permute-start | bytes 368648 | tf_op jit(solution)/shard_map/ppermute | solution.py:492
  29.6 6.4 %collective-permute-start.13 = (f32[8,192]{1,0:T(8,128)S(1)}, f32[8,192]{1,0:T(8,128)S(1)}, u32[]{:S(2)}, u32[]{:S(2)}) collective-permute-start(f32[8,192]{1,0:T(8,128)S(1)} %get-tuple-element.49), channel_id=1, source_target_pairs={{0,7},{1,4},{2,5},{3,6},{4,1},{5,2},{6,3},{7,0},{8,15},{9,12},{10,... | collective-permute-start | bytes 18440 | tf_op jit(solution)/shard_map/ppermute | solution.py:492
  31.4 4.5 %collective-permute-start.14 = (f32[8,192]{1,0:T(8,128)S(1)}, f32[8,192]{1,0:T(8,128)S(1)}, u32[]{:S(2)}, u32[]{:S(2)}) collective-permute-start(f32[8,192]{1,0:T(8,128)S(1)} %get-tuple-element.50), channel_id=1, source_target_pairs={{0,3},{1,0},{2,1},{3,2},{4,5},{5,6},{6,7},{7,4},{8,11},{9,8},{10,9... | collective-permute-start | bytes 18440 | tf_op jit(solution)/shard_map/ppermute | solution.py:492

commit v4 on v3

--- a/solution.py
+++ b/solution.py
@@ -205,11 +205,24 @@
     return jnp.concatenate(parts, axis=1)
 
 
+def lane_row(values):
+    lane = lax.broadcasted_iota(jnp.int32, (1, LANES), 1)
+    row = jnp.zeros((1, LANES), f32)
+    for hit, value in values(lane):
+        row = jnp.where(hit, value, row)
+    return row
+
+
 def lateral(block):
-    cell = lax.broadcasted_iota(jnp.int32, block.shape, 1) & (HALF - 1)
-    left = jnp.where(cell == 0, 0.0, pltpu.roll(block, 1, 1))
-    right = jnp.where(cell == HALF - 1, 0.0, pltpu.roll(block, LANES - 1, 1))
+    inner_left = lane_row(lambda lane: [((lane & (HALF - 1)) != 0, 1.0)])
+    inner_right = lane_row(lambda lane: [((lane & (HALF - 1)) != HALF - 1, 1.0)])
+    left = pltpu.roll(block, 1, 1) * inner_left
+    right = pltpu.roll(block, LANES - 1, 1) * inner_right
     return left + right - 2.0 * block
+
+
+def halves(low, high):
+    return lane_row(lambda lane: [(lane < HALF, low), (lane >= HALF, high)])
 
 
 def coefficients(c):
@@ -262,6 +275,7 @@
     put = lax.broadcasted_iota(jnp.int32, (plan.slots, rows), 0) == row
     get = lax.broadcasted_iota(jnp.int32, (rows, plan.slots), 1) == col
     put_ref[...] = jnp.where(put, 1.0, 0.0).astype(bf16)
+    get = jnp.logical_and(get, jnp.logical_or(stator, z == plan.inlet - 1))
     get_ref[...] = jnp.where(get, 1.0, 0.0).astype(bf16)
 
 
@@ -344,7 +358,7 @@
 def local_kernel(
     plan, block_ref, arrived_ref, flux_ref, carried_ref, share_ref, *refs
 ):
-    outward_ref, own_ref, base_ref, pair_ref, tangent_ref = refs
+    outward_ref, own_ref, base_ref, pair_ref, tangent_ref, pair_tangent_ref = refs
     _, x, _ = place()
     half = plan.rows // 2
     low = is_low(plan.rows)
@@ -357,21 +371,22 @@
         down, up = coefficients(c)
         ghost = ghosts[:, c * LANES : (c + 1) * LANES]
         change = (
-            jnp.where(low, down, up) * half_turn(flux)
+            halves(down, up) * half_turn(flux)
             - 2.0 * DISSIPATION[c] * flux
             + SPREADING[c] * (lateral(flux) + ghost)
         )
         base_ref[c] = state + time_step * change
+        pair_tangent_ref[c] = time_step * (1.0 - flux * flux)
         share = share_ref[c * half : (c + 1) * half]
         pair_ref[c] = pairing(plan, carried_ref[c], share, x)
         flux = jnp.tanh(own)
         tangent_ref[c] = time_step * (1.0 - flux * flux)
 
 
-def second_kernel(plan, base_ref, pair_ref, flux_ref, get_ref, put_ref, *refs):
+def second_kernel(plan, base_ref, pair_ref, tangent_ref, get_ref, put_ref, *refs):
     chips, count = plan.chips, len(plan.swap_z)
     face_refs, z_refs = refs[:chips][::-1], refs[chips : chips + count]
-    weighted_ref, slots_ref, core_ref, partial_ref = refs[chips + count :]
+    core_ref, partial_ref, out_ref, straight_ref, diag_ref, *edge_refs = refs[chips + count :]
     z, x, _ = place()
     odd = lax.rem(z, 2) == 1
     low = is_low(plan.rows)
@@ -379,6 +394,8 @@
     at_face = jnp.logical_or(z == plan.inlet, z == plan.inlet - 1)
     at_end = jnp.logical_or(z == 0, z == plan.pairs - 1)
     put, get = put_ref[...], get_ref[...]
+    half = plan.rows // 2
+    blocks = []
     for c in range(NC):
         face = get_parts(plan, face_refs, c)
         near = padded(plan, z_refs[0][c])
@@ -387,54 +404,33 @@
         if count > 1:
             far = padded(plan, z_refs[1][c])
             slots = unpack2(jnp.where(odd, near, far), jnp.where(odd, far, near))
-        slots = gathered(plan, slots)
-        other = jnp.where(at_face, moved, jnp.where(at_end, 0.0, slots))
-        halo = jnp.where(swapped, slots, other)
+            far = jnp.where(jnp.logical_or(at_face, at_end), moved, gathered(plan, slots))
+        else:
+            far = moved
+        halo = jnp.where(swapped, gathered(plan, slots), far)
         down, up = coefficients(c)
-        slope = jnp.tanh(base_ref[c] + time_step * jnp.where(low, up, down) * halo)
+        slope = jnp.tanh(base_ref[c] + halves(time_step * up, time_step * down) * halo)
         weighted = (2.0 - slope * slope) * pair_ref[c]
-        weighted_ref[c] = weighted
-        flux = flux_ref[c]
         change = (
-            jnp.where(low, up, down) * half_turn(weighted)
+            halves(up, down) * half_turn(weighted)
             - 2.0 * DISSIPATION[c] * weighted
             + SPREADING[c] * lateral(weighted)
         )
-        partial = weighted + time_step * (1.0 - flux * flux) * change
+        partial = weighted + tangent_ref[c] * change
         partial_ref[c] = partial
-        slots = in_slots(plan, weighted, put)
-        slots_ref[c] = slots
-        to_before, to_after = sending(plan, slots)
+        out_ref[c * half : (c + 1) * half] = pack(partial, 1 - x)
+        to_before, to_after = sending(plan, in_slots(plan, weighted, put))
+        put_parts(plan, straight_ref, c, jnp.where(x == 0, to_after, to_before))
+        put_parts(plan, diag_ref, c, jnp.where(x == 0, to_before, to_after))
         face = jnp.where(z < plan.inlet, to_after, to_before)
         for turn in range(chips):
             at = (chips + turn) * plan.part_pad
             core_ref[turn, c] = face[at : at + plan.part_pad]
-
-
-def halo_kernel(plan, weighted_ref, partial_ref, slots_ref, *outs):
-    out_ref, straight_ref, diag_ref, *edge_refs = outs
-    _, x, _ = place()
-    half = plan.rows // 2
-    edges = edges_of(
-        [weighted_ref[c] for c in range(NC)], [127 * (1 - x), 64 - x, 127 * x, 63 + x]
-    )
+        blocks.append(weighted)
+    edges = edges_of(blocks, [127 * (1 - x), 64 - x, 127 * x, 63 + x])
     put_edge(plan, out_ref, 0, edges[:8])
     for i, ref in enumerate(edge_refs):
         ref[...] = edges[8 * i + 8 : 8 * i + 16]
-    for c in range(NC):
-        out_ref[c * half : (c + 1) * half] = pack(partial_ref[c], 1 - x)
-        to_before, to_after = sending(plan, slots_ref[c])
-        put_parts(plan, straight_ref, c, jnp.where(x == 0, to_after, to_before))
-        put_parts(plan, diag_ref, c, jnp.where(x == 0, to_before, to_after))
-
-
-def ghost_kernel(plan, rest_ref, tangent_ref, cross_ref, inward_ref, own_ref, ghost_ref):
-    _, x, _ = place()
-    edges = jnp.concatenate([cross_ref[...], inward_ref[...], own_ref[...]], axis=0)
-    ghosts = edges_at(edges, [127 * x, 127 * (1 - x), 64 - x])
-    for c in range(NC):
-        ghost = ghosts[:, c * LANES : (c + 1) * LANES]
-        ghost_ref[c] = rest_ref[c] + tangent_ref[c] * (SPREADING[c] * ghost)
 
 
 def rest_kernel(plan, tangent_ref, get_ref, *refs):
@@ -455,10 +451,14 @@
         rest_ref[c] = tangent_ref[c] * (jnp.where(first, down, up) * halo)
 
 
-def last_kernel(plan, partial_ref, rest_ref, tangent_ref, share_ref, out_ref):
+def last_kernel(plan, partial_ref, rest_ref, tangent_ref, share_ref, *refs):
+    cross_ref, inward_ref, own_ref, out_ref = refs
     _, x, _ = place()
     half = plan.rows // 2
-    ghosts = edges_at(get_edge(plan, share_ref, 0), [63 + x])
+    edges = [get_edge(plan, share_ref, 0), cross_ref[...], inward_ref[...], own_ref[...]]
+    ghosts = edges_at(
+        jnp.concatenate(edges, axis=0), [63 + x, 127 * x, 127 * (1 - x), 64 - x]
+    )
     for c in range(NC):
         ghost = ghosts[:, c * LANES : (c + 1) * LANES]
         share = share_ref[c * half : (c + 1) * half]
@@ -524,20 +524,17 @@
         face_got = [
             send(jnp.stack([face[0, t], crossed[t]]), plan.swap_face[t]) for t in range(chips)
         ]
-        base, pair, tangent = run(
+        base, pair, tangent, pair_tangent = run(
             local_kernel,
-            [full] * 3,
+            [full] * 4,
             *(checkpoint, state_got, flux, carried, share_got, outward_got, own),
         )
-        weighted, slots, core, partial = run(
+        core, partial, mine, straight, diag, cross, inward, own = run(
             second_kernel,
-            [full, ((NC, plan.slots, LANES), f32), (parts[0][1:], f32), full],
-            *(base, pair, flux, get, put, *face_got[::-1], *near_got),
+            [(parts[0][1:], f32), full, share(1), parts, parts] + [edge] * 3,
+            *(base, pair, pair_tangent, get, put, *face_got[::-1], *near_got),
         )
         crossed = send(core, plan.swap_core)
-        mine, straight, diag, cross, inward, own = run(
-            halo_kernel, [share(1), parts, parts] + [edge] * 3, weighted, partial, slots
-        )
         share_got = send(mine, plan.swap_x)
         z, x, _ = place()
         turned = jnp.logical_xor(x == 0, z == plan.inlet)
@@ -553,8 +550,11 @@
         cross_got = send(cross, plan.cross)
         inward_got = send(inward, plan.inward)
         (rest,) = run(rest_kernel, [full], tangent, get, *diag_got, *straight_got[::-1])
-        (ghost,) = run(ghost_kernel, [full], rest, tangent, cross_got, inward_got, own)
-        (out,) = run(last_kernel, [full], partial, ghost, tangent, share_got)
+        (out,) = run(
+            last_kernel,
+            [full],
+            *(partial, rest, tangent, share_got, cross_got, inward_got, own),
+        )
         return out.reshape(NC, rows, 1, LANES)
 
     return jax.shard_map(

time: 37.5 us -> 37.1 us (0.989)
  waiting for transfers between devices: 13.6 us -> 12.7 us
  starting transfers between devices: 15.8 us -> 16.6 us
    ppermute x16, waiting for transfers between devices: 13.6 us -> 12.7 us  [send(): return lax.ppermute(part, AXES, moves)]
    ppermute x16, starting transfers between devices: 15.8 us -> 16.6 us  [send(): return lax.ppermute(part, AXES, moves)]
    pallas_call x12 -> x10, Pallas kernels: 5.75 us -> 5.44 us  [call(): pl.pallas_call(kernel, out_shape=[jax.ShapeDtypeStruct(shape, dtype) for...]
  transfers between devices with their start and end apart: 16 -> 16, of which waited for: 7 -> 7; matrix products, arithmetic and copies ran while one was open for 3% -> 3% of each run, Pallas kernels for 10% -> 8%
where the time goes in v4:
time: 37.1 us; the launch traced here: 36.9 us
  starting transfers between devices  16.6 us (45%)
  waiting for transfers between devices  12.7 us (34%)
  Pallas kernels  5.44 us (15%)
  local copies, waits for them, and re-layouts  1.88 us (5%)
    ppermute x16, starting transfers between devices, send(): return lax.ppermute(part, AXES, moves)  16.6 us
    ppermute x16, waiting for transfers between devices, send(): return lax.ppermute(part, AXES, moves)  12.7 us
    pallas_call x10, Pallas kernels, call(): pl.pallas_call(kernel, out_shape=[jax.ShapeDtypeStruct(shape, dtype) for...  5.44 us
    unnamed x8, local copies, waits for them, and re-layouts  1.04 us
    reshape x1, local copies, waits for them, and re-layouts, local(): source = row_source.reshape(plan.span, rows)  0.76 us
  transfers between devices with their start and end apart: 16, of which 7 were waited for; matrix products, arithmetic and copies ran while one was open for 3% of the time, Pallas kernels for 8%

profile of v4, /device:TPU:17, one launch (start us, length us, event | category | flops | bytes accessed | tf_op | source)
XLA Modules:
  0.0 36.9 jit_solution(4853993881707426914)
XLA Ops:
  0.0 1.0 %copy-done = f32[5,192,1,128]{3,2,1,0:T(1,128)S(1)} copy-done((f32[5,192,1,128]{3,2,1,0:T(1,128)S(1)}, f32[5,192,1,128]{3,2,1,0:T(1,128)}, u32[]{:S(2)}) %copy-start) | copy-done | bytes 491544
  1.0 0.2 shard_map.46
  1.2 1.3 %collective-permute-start = (f32[5,96,128]{2,1,0:T(8,128)S(1)}, f32[5,96,128]{2,1,0:T(8,128)S(1)}, u32[]{:S(2)}, u32[]{:S(2)}) collective-permute-start(f32[5,96,128]{2,1,0:T(8,128)S(1)} %shard_map.46), channel_id=1, source_target_pairs={{0,4},{1,5},{2,6},{3,7},{4,0},{5,1},{6,2},{7,3},{8,12},{9,13},{10,... | collective-permute-start | bytes 737288 | tf_op jit(solution)/shard_map/ppermute | solution.py:492
  2.5 0.2 shard_map.50
  2.7 2.1 %collective-permute-start.2 = (f32[8,192]{1,0:T(8,128)S(1)}, f32[8,192]{1,0:T(8,128)S(1)}, u32[]{:S(2)}, u32[]{:S(2)}) collective-permute-start(f32[8,192]{1,0:T(8,128)S(1)} %get-tuple-element.32), channel_id=1, source_target_pairs={{0,1},{1,2},{2,3},{3,0},{4,7},{5,4},{6,5},{7,6},{8,9},{9,10},{10,1... | collective-permute-start | bytes 18440 | tf_op jit(solution)/shard_map/ppermute | solution.py:492
  4.9 0.0 collective-permute-start.1
  4.9 0.8 %reshape.16 = s32[4,192]{1,0:T(4,128)S(1)} reshape(s32[768]{0:T(1024)} %param.7) | data formatting | bytes 6144 | tf_op jit(solution)/shard_map/reshape | solution.py:505
  5.6 0.4 %shard_map.47 = (bf16[192,192]{1,0:T(8,128)(2,1)S(1)}, bf16[192,192]{1,0:T(8,128)(2,1)S(1)}) custom-call(s32[8,192]{1,0:T(8,128)S(1)} %pad.4.refs_0_), custom_call_target="tpu_custom_call" | custom-call | tf_op jit(solution)/shard_map/pallas_call | solution.py:471
  6.1 0.0 copy-done.2
  6.1 0.0 copy-done.3
  6.1 0.4 %shard_map.49.refs_0_.refs_3_ = f32[5,192,128]{2,1,0:T(8,128)S(1)} custom-call(f32[5,192,128]{2,1,0:T(8,128)S(1)} %bitcast.29, bf16[3,320,320]{2,1,0:T(8,128)(2,1)S(1)} %bitcast.28), custom_call_target="tpu_custom_call" | custom-call | tf_op jit(solution)/shard_map/pallas_call | solution.py:471
  6.5 0.0 copy-start.1
  6.5 0.0 collective-permute-done.2.refs_3_.refs_5_
  6.5 1.7 %collective-permute-done.1.refs_2_ = f32[8,192]{1,0:T(8,128)S(1)} collective-permute-done((f32[8,192]{1,0:T(8,128)S(1)}, f32[8,192]{1,0:T(8,128)S(1)}, u32[]{:S(2)}, u32[]{:S(2)}) %collective-permute-start.1) | collective-permute-done | bytes 6176 | tf_op jit(solution)/shard_map/ppermute | solution.py:492
  8.2 0.2 shard_map.51
  8.5 0.1 collective-permute-start.3
  8.5 0.0 collective-permute-done.refs_1_
  8.5 0.0 copy-done.1
  8.6 0.5 %shard_map.48 = (f32[5,192,128]{2,1,0:T(8,128)S(1)}, f32[2,2,5,24,128]{4,3,2,1,0:T(8,128)S(1)}, f32[5,96,128]{2,1,0:T(8,128)S(1)}) custom-call(f32[5,192,128]{2,1,0:T(8,128)S(1)} %bitcast.26, f32[5,96,128]{2,1,0:T(8,128)S(1)} %collective-permute-done.refs_1_, bf16[192,192]{1,0:T(8,128)(2,1)S(1)} %get-tuple-element.28.refs_2_.refs_4_), custom_call_target="tpu_custom_call" | custom-call | tf_op jit(solution)/shard_map/pallas_call | solution.py:471
  9.1 1.2 %collective-permute-start.4 = (f32[2,5,24,128]{3,2,1,0:T(8,128)S(1)}, f32[2,5,24,128]{3,2,1,0:T(8,128)S(1)}, u32[]{:S(2)}, u32[]{:S(2)}) collective-permute-start(f32[2,5,24,128]{3,2,1,0:T(8,128)S(1)} %slice_bitcast_fusion), channel_id=1, source_target_pairs={{0,1},{1,0},{2,3},{3,2},{4,5},{5,4},{6,7},{7,6},{8,9},{9,8},{10,11... | collective-permute-start | bytes 368648 | tf_op jit(solution)/shard_map/ppermute | solution.py:492
  10.3 1.3 %collective-permute-start.7 = (f32[5,96,128]{2,1,0:T(8,128)S(1)}, f32[5,96,128]{2,1,0:T(8,128)S(1)}, u32[]{:S(2)}, u32[]{:S(2)}) collective-permute-start(f32[5,96,128]{2,1,0:T(8,128)S(1)} %get-tuple-element.39), channel_id=1, source_target_pairs={{0,8},{1,9},{2,10},{3,11},{4,12},{5,13},{6,14},{7,15},{8,0},{9,1},... | collective-permute-start | bytes 737288 | tf_op jit(solution)/shard_map/ppermute | solution.py:492
  11.6 0.0 collective-permute-done.4
  11.6 0.8 %collective-permute-start.5 = (f32[2,5,24,128]{3,2,1,0:T(8,128)S(1)}, f32[2,5,24,128]{3,2,1,0:T(8,128)S(1)}, u32[]{:S(2)}, u32[]{:S(2)}) collective-permute-start(f32[2,5,24,128]{3,2,1,0:T(8,128)S(1)} %pad_maximum_fusion), channel_id=1, source_target_pairs={{0,1},{1,0},{2,3},{3,2},{4,5},{5,4},{6,7},{7,6},{8,18},{9,19},{10,... | collective-permute-start | bytes 368648 | tf_op jit(solution)/shard_map/ppermute | solution.py:492
  12.5 1.7 %collective-permute-start.6 = (f32[2,5,24,128]{3,2,1,0:T(8,128)S(1)}, f32[2,5,24,128]{3,2,1,0:T(8,128)S(1)}, u32[]{:S(2)}, u32[]{:S(2)}) collective-permute-start(f32[2,5,24,128]{3,2,1,0:T(8,128)S(1)} %pad_maximum_fusion.1), channel_id=1, source_target_pairs={{0,1},{1,0},{2,3},{3,2},{4,5},{5,4},{6,7},{7,6},{8,16},{9,17},{10,... | collective-permute-start | bytes 368648 | tf_op jit(solution)/shard_map/ppermute | solution.py:492
  14.2 2.0 %collective-permute-done.3.refs_4_ = f32[512,128]{1,0:T(8,128)S(1)} collective-permute-done((f32[512,128]{1,0:T(8,128)S(1)}, f32[512,128]{1,0:T(8,128)S(1)}, u32[]{:S(2)}, u32[]{:S(2)}) %collective-permute-start.3) | collective-permute-done | bytes 262176 | tf_op jit(solution)/shard_map/ppermute | solution.py:492
  16.2 0.8 %shard_map.52 = (f32[5,192,128]{2,1,0:T(8,128)S(1)}, f32[5,192,128]{2,1,0:T(8,128)S(1)}, f32[5,192,128]{2,1,0:T(8,128)S(1)}, f32[5,192,128]{2,1,0:T(8,128)S(1)}) custom-call(f32[5,192,128]{2,1,0:T(8,128)S(1)} %bitcast.27, f32[5,96,128]{2,1,0:T(8,128)S(1)} %collective-permute-done.refs_1_, f32[5,192,128]{2,1,0:T(8,128)S(1)} %get-tuple-element.29.refs_2_, ...), custom_call_target="tpu_custom_call" | custom-call | tf_op jit(solution)/shard_map/pallas_call | solution.py:471
  17.0 0.1 collective-permute-done.5.refs_5_
  17.1 2.7 %collective-permute-done.6.refs_6_ = f32[2,5,24,128]{3,2,1,0:T(8,128)S(1)} collective-permute-done((f32[2,5,24,128]{3,2,1,0:T(8,128)S(1)}, f32[2,5,24,128]{3,2,1,0:T(8,128)S(1)}, u32[]{:S(2)}, u32[]{:S(2)}) %collective-permute-start.6) | collective-permute-done | bytes 122912 | tf_op jit(solution)/shard_map/ppermute | solution.py:492
  19.8 0.0 collective-permute-done.7.refs_7_
  19.9 1.2 %shard_map.53 = (f32[2,5,24,128]{3,2,1,0:T(8,128)S(1)}, f32[5,192,128]{2,1,0:T(8,128)S(1)}, f32[496,128]{1,0:T(8,128)S(1)}, f32[2,2,5,24,128]{4,3,2,1,0:T(8,128)...) custom-call(f32[5,192,128]{2,1,0:T(8,128)S(1)} %get-tuple-element.34, ...), custom_call_target="tpu_custom_call" | custom-call | tf_op jit(solution)/shard_map/pallas_call | solution.py:471
  21.1 1.2 %collective-permute-start.8 = (f32[2,5,24,128]{3,2,1,0:T(8,128)S(1)}, f32[2,5,24,128]{3,2,1,0:T(8,128)S(1)}, u32[]{:S(2)}, u32[]{:S(2)}) collective-permute-start(f32[2,5,24,128]{3,2,1,0:T(8,128)S(1)} %get-tuple-element.43), channel_id=1, source_target_pairs={{0,1},{1,0},{2,3},{3,2},{4,5},{5,4},{6,7},{7,6},{8,9},{9,8},{10,11... | collective-permute-start | bytes 368648 | tf_op jit(solution)/shard_map/ppermute | solution.py:492
  22.3 1.4 %collective-permute-start.13 = (f32[496,128]{1,0:T(8,128)S(1)}, f32[496,128]{1,0:T(8,128)S(1)}, u32[]{:S(2)}, u32[]{:S(2)}) collective-permute-start(f32[496,128]{1,0:T(8,128)S(1)} %get-tuple-element.45), channel_id=1, source_target_pairs={{0,4},{1,5},{2,6},{3,7},{4,0},{5,1},{6,2},{7,3},{8,12},{9,13},{10,... | collective-permute-start | bytes 761864 | tf_op jit(solution)/shard_map/ppermute | solution.py:492
  23.8 0.0 collective-permute-done.8
  23.9 0.5 %collective-permute-start.9 = (f32[2,5,24,128]{3,2,1,0:T(8,128)S(1)}, f32[2,5,24,128]{3,2,1,0:T(8,128)S(1)}, u32[]{:S(2)}, u32[]{:S(2)}) collective-permute-start(f32[2,5,24,128]{3,2,1,0:T(8,128)S(1)} %pad_maximum_fusion.2), channel_id=1, source_target_pairs={{0,1},{1,0},{2,3},{3,2},{4,8},{5,9},{6,10},{7,11},{8,4},{9,5},{10,... | collective-permute-start | bytes 368648 | tf_op jit(solution)/shard_map/ppermute | solution.py:492
  24.4 1.7 %collective-permute-start.12 = (f32[2,5,24,128]{3,2,1,0:T(8,128)S(1)}, f32[2,5,24,128]{3,2,1,0:T(8,128)S(1)}, u32[]{:S(2)}, u32[]{:S(2)}) collective-permute-start(f32[2,5,24,128]{3,2,1,0:T(8,128)S(1)} %pad_maximum_fusion.5), channel_id=1, source_target_pairs={{0,8},{1,9},{2,10},{3,11},{4,0},{5,1},{6,2},{7,3},{8,16},{9,17},{1... | collective-permute-start | bytes 368648 | tf_op jit(solution)/shard_map/ppermute | solution.py:492
  26.1 0.1 collective-permute-start.11
  26.2 0.3 collective-permute-start.10
  26.5 2.9 %collective-permute-done.9.refs_2_ = f32[2,5,24,128]{3,2,1,0:T(8,128)S(1)} collective-permute-done((f32[2,5,24,128]{3,2,1,0:T(8,128)S(1)}, f32[2,5,24,128]{3,2,1,0:T(8,128)S(1)}, u32[]{:S(2)}, u32[]{:S(2)}) %collective-permute-start.9) | collective-permute-done | bytes 122912 | tf_op jit(solution)/shard_map/ppermute | solution.py:492
  29.4 2.7 %collective-permute-start.14 = (f32[8,192]{1,0:T(8,128)S(1)}, f32[8,192]{1,0:T(8,128)S(1)}, u32[]{:S(2)}, u32[]{:S(2)}) collective-permute-start(f32[8,192]{1,0:T(8,128)S(1)} %get-tuple-element.48), channel_id=1, source_target_pairs={{0,7},{1,4},{2,5},{3,6},{4,1},{5,2},{6,3},{7,0},{8,15},{9,12},{10,... | collective-permute-start | bytes 18440 | tf_op jit(solution)/shard_map/ppermute | solution.py:492
  32.2 0.0 collective-permute-done.12.refs_5_
  32.2 0.0 collective-permute-start.15
  32.2 0.0 collective-permute-done.11.refs_4_
  32.2 0.9 %collective-permute-done.10.refs_3_ = f32[2,5,24,128]{3,2,1,0:T(8,128)S(1)} collective-permute-done((f32[2,5,24,128]{3,2,1,0:T(8,128)S(1)}, f32[2,5,24,128]{3,2,1,0:T(8,128)S(1)}, u32[]{:S(2)}, u32[]{:S(2)}) %collective-permute-start.10) | collective-permute-done | bytes 122912 | tf_op jit(solution)/shard_map/ppermute | solution.py:492
  33.1 0.4 %shard_map.54.refs_1_ = f32[5,192,128]{2,1,0:T(8,128)S(1)} custom-call(f32[5,192,128]{2,1,0:T(8,128)S(1)} %get-tuple-element.41.refs_0_.refs_2_, bf16[192,192]{1,0:T(8,128)(2,1)S(1)} %get-tuple-element.37.refs_3_.refs_1_, f32[2,5,24,128]{3,2,1,0:T(8,128)S(1)} %collective-permute-done.9.refs_2_, f32[2,5,24,128]{3,2,1,0:T(8,128)S(1)} %collective-permute-done.10.refs_3_, ...), custom_call_target="tpu_custom_call" | custom-call | tf_op jit(solution)/shard_map/pallas_call | solution.py:471
  33.5 2.3 %collective-permute-done.14.refs_4_ = f32[8,192]{1,0:T(8,128)S(1)} collective-permute-done((f32[8,192]{1,0:T(8,128)S(1)}, f32[8,192]{1,0:T(8,128)S(1)}, u32[]{:S(2)}, u32[]{:S(2)}) %collective-permute-start.14) | collective-permute-done | bytes 6176 | tf_op jit(solution)/shard_map/ppermute | solution.py:492
  35.8 0.0 collective-permute-done.15.refs_5_
  35.8 0.0 collective-permute-done.13.refs_3_
  35.8 1.1 %shard_map.55 = f32[5,192,128]{2,1,0:T(8,128)} custom-call(f32[5,192,128]{2,1,0:T(8,128)S(1)} %get-tuple-element.40.refs_0_, f32[5,192,128]{2,1,0:T(8,128)S(1)} %shard_map.54.refs_1_, f32[5,192,128]{2,1,0:T(8,128)S(1)} %get-tuple-element.41.refs_0_.refs_2_, f32[496,128]{1,0:T(8,128)S(1)} %collective-permute-done.13.refs_3_, ...), custom_call_target="tpu_custom_call" | custom-call | tf_op jit(solution)/shard_map/pallas_call | solution.py:471
  (16 shorter events, 0.2 us)
Async XLA Ops:
  0.0 1.0 %copy-start = (f32[5,192,1,128]{3,2,1,0:T(1,128)S(1)}, f32[5,192,1,128]{3,2,1,0:T(1,128)}, u32[]{:S(2)}) copy-start(f32[5,192,1,128]{3,2,1,0:T(1,128)} %param.4) | copy-start | bytes 1474564
  1.0 5.1 %copy-start.2 = (bf16[1,3,320,320]{3,2,1,0:T(8,128)(2,1)S(1)}, bf16[1,3,320,320]{3,2,1,0:T(8,128)(2,1)}, u32[]{:S(2)}) copy-start(bf16[1,3,320,320]{3,2,1,0:T(8,128)(2,1)} %param.6) | copy-start | bytes 1843204
  1.0 5.1 %copy-start.3 = (f32[5,192,1,128]{3,2,1,0:T(1,128)S(1)}, f32[5,192,1,128]{3,2,1,0:T(1,128)}, u32[]{:S(2)}) copy-start(f32[5,192,1,128]{3,2,1,0:T(1,128)} %param.5) | copy-start | bytes 1474564
  1.2 7.3 %collective-permute-start = (f32[5,96,128]{2,1,0:T(8,128)S(1)}, f32[5,96,128]{2,1,0:T(8,128)S(1)}, u32[]{:S(2)}, u32[]{:S(2)}) collective-permute-start(f32[5,96,128]{2,1,0:T(8,128)S(1)} %shard_map.46), channel_id=1, source_target_pairs={{0,4},{1,5},{2,6},{3,7},{4,0},{5,1},{6,2},{7,3},{8,12},{9,13},{10,... | collective-permute-start | bytes 737288 | tf_op jit(solution)/shard_map/ppermute | solution.py:492
  2.7 3.8 %collective-permute-start.2 = (f32[8,192]{1,0:T(8,128)S(1)}, f32[8,192]{1,0:T(8,128)S(1)}, u32[]{:S(2)}, u32[]{:S(2)}) collective-permute-start(f32[8,192]{1,0:T(8,128)S(1)} %get-tuple-element.32), channel_id=1, source_target_pairs={{0,1},{1,2},{2,3},{3,0},{4,7},{5,4},{6,5},{7,6},{8,9},{9,10},{10,1... | collective-permute-start | bytes 18440 | tf_op jit(solution)/shard_map/ppermute | solution.py:492
  4.9 3.4 %collective-permute-start.1 = (f32[8,192]{1,0:T(8,128)S(1)}, f32[8,192]{1,0:T(8,128)S(1)}, u32[]{:S(2)}, u32[]{:S(2)}) collective-permute-start(f32[8,192]{1,0:T(8,128)S(1)} %get-tuple-element.31), channel_id=1, source_target_pairs={{0,3},{1,0},{2,1},{3,2},{4,5},{5,6},{6,7},{7,4},{8,11},{9,8},{10,9... | collective-permute-start | bytes 18440 | tf_op jit(solution)/shard_map/ppermute | solution.py:492
  6.5 2.0 %copy-start.1 = (f32[5,192,1,128]{3,2,1,0:T(1,128)S(1)}, f32[5,192,1,128]{3,2,1,0:T(1,128)}, u32[]{:S(2)}) copy-start(f32[5,192,1,128]{3,2,1,0:T(1,128)} %param.4) | copy-start | bytes 1474564
  8.5 7.8 %collective-permute-start.3 = (f32[512,128]{1,0:T(8,128)S(1)}, f32[512,128]{1,0:T(8,128)S(1)}, u32[]{:S(2)}, u32[]{:S(2)}) collective-permute-start(f32[512,128]{1,0:T(8,128)S(1)} %shard_map.51), channel_id=1, source_target_pairs={{0,4},{1,5},{2,6},{3,7},{4,0},{5,1},{6,2},{7,3},{8,12},{9,13},{10,... | collective-permute-start | bytes 786440 | tf_op jit(solution)/shard_map/ppermute | solution.py:492
  9.1 2.5 %collective-permute-start.4 = (f32[2,5,24,128]{3,2,1,0:T(8,128)S(1)}, f32[2,5,24,128]{3,2,1,0:T(8,128)S(1)}, u32[]{:S(2)}, u32[]{:S(2)}) collective-permute-start(f32[2,5,24,128]{3,2,1,0:T(8,128)S(1)} %slice_bitcast_fusion), channel_id=1, source_target_pairs={{0,1},{1,0},{2,3},{3,2},{4,5},{5,4},{6,7},{7,6},{8,9},{9,8},{10,11... | collective-permute-start | bytes 368648 | tf_op jit(solution)/shard_map/ppermute | solution.py:492
  10.3 9.6 %collective-permute-start.7 = (f32[5,96,128]{2,1,0:T(8,128)S(1)}, f32[5,96,128]{2,1,0:T(8,128)S(1)}, u32[]{:S(2)}, u32[]{:S(2)}) collective-permute-start(f32[5,96,128]{2,1,0:T(8,128)S(1)} %get-tuple-element.39), channel_id=1, source_target_pairs={{0,8},{1,9},{2,10},{3,11},{4,12},{5,13},{6,14},{7,15},{8,0},{9,1},... | collective-permute-start | bytes 737288 | tf_op jit(solution)/shard_map/ppermute | solution.py:492
  11.6 5.5 %collective-permute-start.5 = (f32[2,5,24,128]{3,2,1,0:T(8,128)S(1)}, f32[2,5,24,128]{3,2,1,0:T(8,128)S(1)}, u32[]{:S(2)}, u32[]{:S(2)}) collective-permute-start(f32[2,5,24,128]{3,2,1,0:T(8,128)S(1)} %pad_maximum_fusion), channel_id=1, source_target_pairs={{0,1},{1,0},{2,3},{3,2},{4,5},{5,4},{6,7},{7,6},{8,18},{9,19},{10,... | collective-permute-start | bytes 368648 | tf_op jit(solution)/shard_map/ppermute | solution.py:492
  12.5 7.4 %collective-permute-start.6 = (f32[2,5,24,128]{3,2,1,0:T(8,128)S(1)}, f32[2,5,24,128]{3,2,1,0:T(8,128)S(1)}, u32[]{:S(2)}, u32[]{:S(2)}) collective-permute-start(f32[2,5,24,128]{3,2,1,0:T(8,128)S(1)} %pad_maximum_fusion.1), channel_id=1, source_target_pairs={{0,1},{1,0},{2,3},{3,2},{4,5},{5,4},{6,7},{7,6},{8,16},{9,17},{10,... | collective-permute-start | bytes 368648 | tf_op jit(solution)/shard_map/ppermute | solution.py:492
  21.1 2.7 %collective-permute-start.8 = (f32[2,5,24,128]{3,2,1,0:T(8,128)S(1)}, f32[2,5,24,128]{3,2,1,0:T(8,128)S(1)}, u32[]{:S(2)}, u32[]{:S(2)}) collective-permute-start(f32[2,5,24,128]{3,2,1,0:T(8,128)S(1)} %get-tuple-element.43), channel_id=1, source_target_pairs={{0,1},{1,0},{2,3},{3,2},{4,5},{5,4},{6,7},{7,6},{8,9},{9,8},{10,11... | collective-permute-start | bytes 368648 | tf_op jit(solution)/shard_map/ppermute | solution.py:492
  22.3 13.5 %collective-permute-start.13 = (f32[496,128]{1,0:T(8,128)S(1)}, f32[496,128]{1,0:T(8,128)S(1)}, u32[]{:S(2)}, u32[]{:S(2)}) collective-permute-start(f32[496,128]{1,0:T(8,128)S(1)} %get-tuple-element.45), channel_id=1, source_target_pairs={{0,4},{1,5},{2,6},{3,7},{4,0},{5,1},{6,2},{7,3},{8,12},{9,13},{10,... | collective-permute-start | bytes 761864 | tf_op jit(solution)/shard_map/ppermute | solution.py:492
  23.9 5.6 %collective-permute-start.9 = (f32[2,5,24,128]{3,2,1,0:T(8,128)S(1)}, f32[2,5,24,128]{3,2,1,0:T(8,128)S(1)}, u32[]{:S(2)}, u32[]{:S(2)}) collective-permute-start(f32[2,5,24,128]{3,2,1,0:T(8,128)S(1)} %pad_maximum_fusion.2), channel_id=1, source_target_pairs={{0,1},{1,0},{2,3},{3,2},{4,8},{5,9},{6,10},{7,11},{8,4},{9,5},{10,... | collective-permute-start | bytes 368648 | tf_op jit(solution)/shard_map/ppermute | solution.py:492
  24.4 7.8 %collective-permute-start.12 = (f32[2,5,24,128]{3,2,1,0:T(8,128)S(1)}, f32[2,5,24,128]{3,2,1,0:T(8,128)S(1)}, u32[]{:S(2)}, u32[]{:S(2)}) collective-permute-start(f32[2,5,24,128]{3,2,1,0:T(8,128)S(1)} %pad_maximum_fusion.5), channel_id=1, source_target_pairs={{0,8},{1,9},{2,10},{3,11},{4,0},{5,1},{6,2},{7,3},{8,16},{9,17},{1... | collective-permute-start | bytes 368648 | tf_op jit(solution)/shard_map/ppermute | solution.py:492
  26.1 6.1 %collective-permute-start.11 = (f32[2,5,24,128]{3,2,1,0:T(8,128)S(1)}, f32[2,5,24,128]{3,2,1,0:T(8,128)S(1)}, u32[]{:S(2)}, u32[]{:S(2)}) collective-permute-start(f32[2,5,24,128]{3,2,1,0:T(8,128)S(1)} %pad_maximum_fusion.4), channel_id=1, source_target_pairs={{0,8},{1,9},{2,10},{3,11},{4,0},{5,1},{6,2},{7,3},{8,18},{9,19},{1... | collective-permute-start | bytes 368648 | tf_op jit(solution)/shard_map/ppermute | solution.py:492
  26.2 6.9 %collective-permute-start.10 = (f32[2,5,24,128]{3,2,1,0:T(8,128)S(1)}, f32[2,5,24,128]{3,2,1,0:T(8,128)S(1)}, u32[]{:S(2)}, u32[]{:S(2)}) collective-permute-start(f32[2,5,24,128]{3,2,1,0:T(8,128)S(1)} %pad_maximum_fusion.3), channel_id=1, source_target_pairs={{0,1},{1,0},{2,3},{3,2},{4,8},{5,9},{6,10},{7,11},{8,4},{9,5},{10,... | collective-permute-start | bytes 368648 | tf_op jit(solution)/shard_map/ppermute | solution.py:492
  29.4 6.4 %collective-permute-start.14 = (f32[8,192]{1,0:T(8,128)S(1)}, f32[8,192]{1,0:T(8,128)S(1)}, u32[]{:S(2)}, u32[]{:S(2)}) collective-permute-start(f32[8,192]{1,0:T(8,128)S(1)} %get-tuple-element.48), channel_id=1, source_target_pairs={{0,7},{1,4},{2,5},{3,6},{4,1},{5,2},{6,3},{7,0},{8,15},{9,12},{10,... | collective-permute-start | bytes 18440 | tf_op jit(solution)/shard_map/ppermute | solution.py:492
  32.2 3.7 %collective-permute-start.15 = (f32[8,192]{1,0:T(8,128)S(1)}, f32[8,192]{1,0:T(8,128)S(1)}, u32[]{:S(2)}, u32[]{:S(2)}) collective-permute-start(f32[8,192]{1,0:T(8,128)S(1)} %get-tuple-element.49), channel_id=1, source_target_pairs={{0,3},{1,0},{2,1},{3,2},{4,5},{5,6},{6,7},{7,4},{8,11},{9,8},{10,9... | collective-permute-start | bytes 18440 | tf_op jit(solution)/shard_map/ppermute | solution.py:492

commit v5 on v4

--- a/solution.py
+++ b/solution.py
@@ -240,7 +240,9 @@
 def slot_kernel(plan, source_ref, put_ref, get_ref):
     rows, span, chips = plan.rows, plan.span, plan.chips
     z, _, j = place()
-    source = source_ref[...]
+    source = [source_ref[:, d * rows : (d + 1) * rows] for d in range(span)]
+    source += [jnp.full((1, rows), -1, jnp.int32)] * (-span % 8)
+    source = jnp.concatenate(source, axis=0)
     own_chip, own_core = j // 2, lax.rem(j, 2)
 
     def order(other, sign):
@@ -473,7 +475,7 @@
         out_shape=[jax.ShapeDtypeStruct(shape, dtype) for shape, dtype in outs],
         in_specs=[whole] * len(args),
         out_specs=[whole] * len(outs),
-        compiler_params=pltpu.CompilerParams(vmem_limit_bytes=32 * 2**20),
+        compiler_params=pltpu.CompilerParams(vmem_limit_bytes=16 * 2**20),
         cost_estimate=flops
         and pl.CostEstimate(flops=flops, bytes_accessed=0, transcendentals=0),
     )(*args)
@@ -502,8 +504,7 @@
         checkpoint = checkpoint.reshape(full[0])
         adjoint = adjoint.reshape(full[0])
         inverse = line_inverse.reshape(line_inverse.shape[1:])
-        source = row_source.reshape(plan.span, rows)
-        source = jnp.pad(source, ((0, -plan.span % 8), (0, 0)), constant_values=-1)
+        source = row_source.reshape(1, plan.span * rows)
 
         (mine,) = call(pack_kernel, [half], checkpoint)
         state_got = send(mine, plan.swap_x)

time: 37.1 us -> 37.1 us (level)
  transfers between devices with their start and end apart: 16 -> 16, of which waited for: 7 -> 7; matrix products, arithmetic and copies ran while one was open for 3% -> 2% of each run, Pallas kernels for 8% -> 8%
where the time goes in v5:
time: 37.1 us; the launch traced here: 36.9 us
  starting transfers between devices  16.6 us (45%)
  waiting for transfers between devices  12.8 us (35%)
  Pallas kernels  5.48 us (15%)
  local copies, waits for them, and re-layouts  1.8 us (5%)
    ppermute x16, starting transfers between devices, send(): return lax.ppermute(part, AXES, moves)  16.6 us
    ppermute x16, waiting for transfers between devices, send(): return lax.ppermute(part, AXES, moves)  12.8 us
    pallas_call x10, Pallas kernels, call(): pl.pallas_call(kernel, out_shape=[jax.ShapeDtypeStruct(shape, dtype) for...  5.48 us
    unnamed x8, local copies, waits for them, and re-layouts  1.04 us
  transfers between devices with their start and end apart: 16, of which 7 were waited for; matrix products, arithmetic and copies ran while one was open for 2% of the time, Pallas kernels for 8%

profile of v5, /device:TPU:17, one launch (start us, length us, event | category | flops | bytes accessed | tf_op | source)
XLA Modules:
  0.0 36.9 jit_solution(12669957232888840647)
XLA Ops:
  0.0 1.0 %copy-done = f32[5,192,1,128]{3,2,1,0:T(1,128)S(1)} copy-done((f32[5,192,1,128]{3,2,1,0:T(1,128)S(1)}, f32[5,192,1,128]{3,2,1,0:T(1,128)}, u32[]{:S(2)}) %copy-start) | copy-done | bytes 491544
  1.0 0.2 shard_map.46
  1.2 1.3 %collective-permute-start = (f32[5,96,128]{2,1,0:T(8,128)S(1)}, f32[5,96,128]{2,1,0:T(8,128)S(1)}, u32[]{:S(2)}, u32[]{:S(2)}) collective-permute-start(f32[5,96,128]{2,1,0:T(8,128)S(1)} %shard_map.46), channel_id=1, source_target_pairs={{0,4},{1,5},{2,6},{3,7},{4,0},{5,1},{6,2},{7,3},{8,12},{9,13},{10,... | collective-permute-start | bytes 737288 | tf_op jit(solution)/shard_map/ppermute | solution.py:494
  2.5 0.2 shard_map.50
  2.7 2.1 %collective-permute-start.2 = (f32[8,192]{1,0:T(8,128)S(1)}, f32[8,192]{1,0:T(8,128)S(1)}, u32[]{:S(2)}, u32[]{:S(2)}) collective-permute-start(f32[8,192]{1,0:T(8,128)S(1)} %get-tuple-element.32), channel_id=1, source_target_pairs={{0,1},{1,2},{2,3},{3,0},{4,7},{5,4},{6,5},{7,6},{8,9},{9,10},{10,1... | collective-permute-start | bytes 18440 | tf_op jit(solution)/shard_map/ppermute | solution.py:494
  4.9 0.0 collective-permute-start.1
  4.9 0.7 %reshape.16.refs_0_ = s32[1,768]{1,0:T(1,128)S(1)} reshape(s32[768]{0:T(1024)} %param.7) | data formatting | bytes 6144 | tf_op jit(solution)/shard_map/reshape | solution.py:507
  5.6 0.5 %shard_map.47 = (bf16[192,192]{1,0:T(8,128)(2,1)S(1)}, bf16[192,192]{1,0:T(8,128)(2,1)S(1)}) custom-call(s32[1,768]{1,0:T(1,128)S(1)} %reshape.16.refs_0_), custom_call_target="tpu_custom_call" | custom-call | tf_op jit(solution)/shard_map/pallas_call | solution.py:473
  6.0 0.0 copy-done.2
  6.1 0.0 copy-done.3
  6.1 0.4 %shard_map.49.refs_0_.refs_3_ = f32[5,192,128]{2,1,0:T(8,128)S(1)} custom-call(f32[5,192,128]{2,1,0:T(8,128)S(1)} %bitcast.29, bf16[3,320,320]{2,1,0:T(8,128)(2,1)S(1)} %bitcast.28), custom_call_target="tpu_custom_call" | custom-call | tf_op jit(solution)/shard_map/pallas_call | solution.py:473
  6.5 0.0 copy-start.1
  6.5 0.0 collective-permute-done.2.refs_3_.refs_5_
  6.5 1.7 %collective-permute-done.1.refs_2_ = f32[8,192]{1,0:T(8,128)S(1)} collective-permute-done((f32[8,192]{1,0:T(8,128)S(1)}, f32[8,192]{1,0:T(8,128)S(1)}, u32[]{:S(2)}, u32[]{:S(2)}) %collective-permute-start.1) | collective-permute-done | bytes 6176 | tf_op jit(solution)/shard_map/ppermute | solution.py:494
  8.2 0.2 shard_map.51
  8.5 0.1 collective-permute-start.3
  8.5 0.0 collective-permute-done.refs_1_
  8.5 0.0 copy-done.1
  8.6 0.5 %shard_map.48 = (f32[5,192,128]{2,1,0:T(8,128)S(1)}, f32[2,2,5,24,128]{4,3,2,1,0:T(8,128)S(1)}, f32[5,96,128]{2,1,0:T(8,128)S(1)}) custom-call(f32[5,192,128]{2,1,0:T(8,128)S(1)} %bitcast.26, f32[5,96,128]{2,1,0:T(8,128)S(1)} %collective-permute-done.refs_1_, bf16[192,192]{1,0:T(8,128)(2,1)S(1)} %get-tuple-element.28.refs_2_.refs_4_), custom_call_target="tpu_custom_call" | custom-call | tf_op jit(solution)/shard_map/pallas_call | solution.py:473
  9.1 1.2 %collective-permute-start.4 = (f32[2,5,24,128]{3,2,1,0:T(8,128)S(1)}, f32[2,5,24,128]{3,2,1,0:T(8,128)S(1)}, u32[]{:S(2)}, u32[]{:S(2)}) collective-permute-start(f32[2,5,24,128]{3,2,1,0:T(8,128)S(1)} %slice_bitcast_fusion), channel_id=1, source_target_pairs={{0,1},{1,0},{2,3},{3,2},{4,5},{5,4},{6,7},{7,6},{8,9},{9,8},{10,11... | collective-permute-start | bytes 368648 | tf_op jit(solution)/shard_map/ppermute | solution.py:494
  10.3 1.3 %collective-permute-start.7 = (f32[5,96,128]{2,1,0:T(8,128)S(1)}, f32[5,96,128]{2,1,0:T(8,128)S(1)}, u32[]{:S(2)}, u32[]{:S(2)}) collective-permute-start(f32[5,96,128]{2,1,0:T(8,128)S(1)} %get-tuple-element.39), channel_id=1, source_target_pairs={{0,8},{1,9},{2,10},{3,11},{4,12},{5,13},{6,14},{7,15},{8,0},{9,1},... | collective-permute-start | bytes 737288 | tf_op jit(solution)/shard_map/ppermute | solution.py:494
  11.6 0.0 collective-permute-done.4
  11.6 0.8 %collective-permute-start.5 = (f32[2,5,24,128]{3,2,1,0:T(8,128)S(1)}, f32[2,5,24,128]{3,2,1,0:T(8,128)S(1)}, u32[]{:S(2)}, u32[]{:S(2)}) collective-permute-start(f32[2,5,24,128]{3,2,1,0:T(8,128)S(1)} %pad_maximum_fusion), channel_id=1, source_target_pairs={{0,1},{1,0},{2,3},{3,2},{4,5},{5,4},{6,7},{7,6},{8,18},{9,19},{10,... | collective-permute-start | bytes 368648 | tf_op jit(solution)/shard_map/ppermute | solution.py:494
  12.5 1.7 %collective-permute-start.6 = (f32[2,5,24,128]{3,2,1,0:T(8,128)S(1)}, f32[2,5,24,128]{3,2,1,0:T(8,128)S(1)}, u32[]{:S(2)}, u32[]{:S(2)}) collective-permute-start(f32[2,5,24,128]{3,2,1,0:T(8,128)S(1)} %pad_maximum_fusion.1), channel_id=1, source_target_pairs={{0,1},{1,0},{2,3},{3,2},{4,5},{5,4},{6,7},{7,6},{8,16},{9,17},{10,... | collective-permute-start | bytes 368648 | tf_op jit(solution)/shard_map/ppermute | solution.py:494
  14.2 2.0 %collective-permute-done.3.refs_4_ = f32[512,128]{1,0:T(8,128)S(1)} collective-permute-done((f32[512,128]{1,0:T(8,128)S(1)}, f32[512,128]{1,0:T(8,128)S(1)}, u32[]{:S(2)}, u32[]{:S(2)}) %collective-permute-start.3) | collective-permute-done | bytes 262176 | tf_op jit(solution)/shard_map/ppermute | solution.py:494
  16.2 0.8 %shard_map.52 = (f32[5,192,128]{2,1,0:T(8,128)S(1)}, f32[5,192,128]{2,1,0:T(8,128)S(1)}, f32[5,192,128]{2,1,0:T(8,128)S(1)}, f32[5,192,128]{2,1,0:T(8,128)S(1)}) custom-call(f32[5,192,128]{2,1,0:T(8,128)S(1)} %bitcast.27, f32[5,96,128]{2,1,0:T(8,128)S(1)} %collective-permute-done.refs_1_, f32[5,192,128]{2,1,0:T(8,128)S(1)} %get-tuple-element.29.refs_2_, ...), custom_call_target="tpu_custom_call" | custom-call | tf_op jit(solution)/shard_map/pallas_call | solution.py:473
  17.0 0.2 collective-permute-done.5.refs_5_
  17.1 2.7 %collective-permute-done.6.refs_6_ = f32[2,5,24,128]{3,2,1,0:T(8,128)S(1)} collective-permute-done((f32[2,5,24,128]{3,2,1,0:T(8,128)S(1)}, f32[2,5,24,128]{3,2,1,0:T(8,128)S(1)}, u32[]{:S(2)}, u32[]{:S(2)}) %collective-permute-start.6) | collective-permute-done | bytes 122912 | tf_op jit(solution)/shard_map/ppermute | solution.py:494
  19.8 0.0 collective-permute-done.7.refs_7_
  19.9 1.2 %shard_map.53 = (f32[2,5,24,128]{3,2,1,0:T(8,128)S(1)}, f32[5,192,128]{2,1,0:T(8,128)S(1)}, f32[496,128]{1,0:T(8,128)S(1)}, f32[2,2,5,24,128]{4,3,2,1,0:T(8,128)...) custom-call(f32[5,192,128]{2,1,0:T(8,128)S(1)} %get-tuple-element.34, ...), custom_call_target="tpu_custom_call" | custom-call | tf_op jit(solution)/shard_map/pallas_call | solution.py:473
  21.1 1.2 %collective-permute-start.8 = (f32[2,5,24,128]{3,2,1,0:T(8,128)S(1)}, f32[2,5,24,128]{3,2,1,0:T(8,128)S(1)}, u32[]{:S(2)}, u32[]{:S(2)}) collective-permute-start(f32[2,5,24,128]{3,2,1,0:T(8,128)S(1)} %get-tuple-element.43), channel_id=1, source_target_pairs={{0,1},{1,0},{2,3},{3,2},{4,5},{5,4},{6,7},{7,6},{8,9},{9,8},{10,11... | collective-permute-start | bytes 368648 | tf_op jit(solution)/shard_map/ppermute | solution.py:494
  22.3 1.4 %collective-permute-start.13 = (f32[496,128]{1,0:T(8,128)S(1)}, f32[496,128]{1,0:T(8,128)S(1)}, u32[]{:S(2)}, u32[]{:S(2)}) collective-permute-start(f32[496,128]{1,0:T(8,128)S(1)} %get-tuple-element.45), channel_id=1, source_target_pairs={{0,4},{1,5},{2,6},{3,7},{4,0},{5,1},{6,2},{7,3},{8,12},{9,13},{10,... | collective-permute-start | bytes 761864 | tf_op jit(solution)/shard_map/ppermute | solution.py:494
  23.8 0.0 collective-permute-done.8
  23.9 0.5 %collective-permute-start.9 = (f32[2,5,24,128]{3,2,1,0:T(8,128)S(1)}, f32[2,5,24,128]{3,2,1,0:T(8,128)S(1)}, u32[]{:S(2)}, u32[]{:S(2)}) collective-permute-start(f32[2,5,24,128]{3,2,1,0:T(8,128)S(1)} %pad_maximum_fusion.2), channel_id=1, source_target_pairs={{0,1},{1,0},{2,3},{3,2},{4,8},{5,9},{6,10},{7,11},{8,4},{9,5},{10,... | collective-permute-start | bytes 368648 | tf_op jit(solution)/shard_map/ppermute | solution.py:494
  24.4 1.7 %collective-permute-start.12 = (f32[2,5,24,128]{3,2,1,0:T(8,128)S(1)}, f32[2,5,24,128]{3,2,1,0:T(8,128)S(1)}, u32[]{:S(2)}, u32[]{:S(2)}) collective-permute-start(f32[2,5,24,128]{3,2,1,0:T(8,128)S(1)} %pad_maximum_fusion.5), channel_id=1, source_target_pairs={{0,8},{1,9},{2,10},{3,11},{4,0},{5,1},{6,2},{7,3},{8,16},{9,17},{1... | collective-permute-start | bytes 368648 | tf_op jit(solution)/shard_map/ppermute | solution.py:494
  26.1 0.1 collective-permute-start.11
  26.2 0.3 collective-permute-start.10
  26.5 2.9 %collective-permute-done.9.refs_2_ = f32[2,5,24,128]{3,2,1,0:T(8,128)S(1)} collective-permute-done((f32[2,5,24,128]{3,2,1,0:T(8,128)S(1)}, f32[2,5,24,128]{3,2,1,0:T(8,128)S(1)}, u32[]{:S(2)}, u32[]{:S(2)}) %collective-permute-start.9) | collective-permute-done | bytes 122912 | tf_op jit(solution)/shard_map/ppermute | solution.py:494
  29.4 2.7 %collective-permute-start.14 = (f32[8,192]{1,0:T(8,128)S(1)}, f32[8,192]{1,0:T(8,128)S(1)}, u32[]{:S(2)}, u32[]{:S(2)}) collective-permute-start(f32[8,192]{1,0:T(8,128)S(1)} %get-tuple-element.48), channel_id=1, source_target_pairs={{0,7},{1,4},{2,5},{3,6},{4,1},{5,2},{6,3},{7,0},{8,15},{9,12},{10,... | collective-permute-start | bytes 18440 | tf_op jit(solution)/shard_map/ppermute | solution.py:494
  32.2 0.0 collective-permute-done.12.refs_5_
  32.2 0.0 collective-permute-start.15
  32.2 0.0 collective-permute-done.11.refs_4_
  32.2 0.9 %collective-permute-done.10.refs_3_ = f32[2,5,24,128]{3,2,1,0:T(8,128)S(1)} collective-permute-done((f32[2,5,24,128]{3,2,1,0:T(8,128)S(1)}, f32[2,5,24,128]{3,2,1,0:T(8,128)S(1)}, u32[]{:S(2)}, u32[]{:S(2)}) %collective-permute-start.10) | collective-permute-done | bytes 122912 | tf_op jit(solution)/shard_map/ppermute | solution.py:494
  33.1 0.4 %shard_map.54.refs_1_ = f32[5,192,128]{2,1,0:T(8,128)S(1)} custom-call(f32[5,192,128]{2,1,0:T(8,128)S(1)} %get-tuple-element.41.refs_0_.refs_2_, bf16[192,192]{1,0:T(8,128)(2,1)S(1)} %get-tuple-element.37.refs_3_.refs_1_, f32[2,5,24,128]{3,2,1,0:T(8,128)S(1)} %collective-permute-done.9.refs_2_, f32[2,5,24,128]{3,2,1,0:T(8,128)S(1)} %collective-permute-done.10.refs_3_, ...), custom_call_target="tpu_custom_call" | custom-call | tf_op jit(solution)/shard_map/pallas_call | solution.py:473
  33.5 2.3 %collective-permute-done.14.refs_4_ = f32[8,192]{1,0:T(8,128)S(1)} collective-permute-done((f32[8,192]{1,0:T(8,128)S(1)}, f32[8,192]{1,0:T(8,128)S(1)}, u32[]{:S(2)}, u32[]{:S(2)}) %collective-permute-start.14) | collective-permute-done | bytes 6176 | tf_op jit(solution)/shard_map/ppermute | solution.py:494
  35.8 0.0 collective-permute-done.15.refs_5_
  35.8 0.0 collective-permute-done.13.refs_3_
  35.8 1.1 %shard_map.55 = f32[5,192,128]{2,1,0:T(8,128)} custom-call(f32[5,192,128]{2,1,0:T(8,128)S(1)} %get-tuple-element.40.refs_0_, f32[5,192,128]{2,1,0:T(8,128)S(1)} %shard_map.54.refs_1_, f32[5,192,128]{2,1,0:T(8,128)S(1)} %get-tuple-element.41.refs_0_.refs_2_, f32[496,128]{1,0:T(8,128)S(1)} %collective-permute-done.13.refs_3_, ...), custom_call_target="tpu_custom_call" | custom-call | tf_op jit(solution)/shard_map/pallas_call | solution.py:473
  (15 shorter events, 0.2 us)
Async XLA Ops:
  0.0 1.0 %copy-start = (f32[5,192,1,128]{3,2,1,0:T(1,128)S(1)}, f32[5,192,1,128]{3,2,1,0:T(1,128)}, u32[]{:S(2)}) copy-start(f32[5,192,1,128]{3,2,1,0:T(1,128)} %param.4) | copy-start | bytes 1474564
  1.0 5.0 %copy-start.2 = (bf16[1,3,320,320]{3,2,1,0:T(8,128)(2,1)S(1)}, bf16[1,3,320,320]{3,2,1,0:T(8,128)(2,1)}, u32[]{:S(2)}) copy-start(bf16[1,3,320,320]{3,2,1,0:T(8,128)(2,1)} %param.6) | copy-start | bytes 1843204
  1.0 5.0 %copy-start.3 = (f32[5,192,1,128]{3,2,1,0:T(1,128)S(1)}, f32[5,192,1,128]{3,2,1,0:T(1,128)}, u32[]{:S(2)}) copy-start(f32[5,192,1,128]{3,2,1,0:T(1,128)} %param.5) | copy-start | bytes 1474564
  1.2 7.3 %collective-permute-start = (f32[5,96,128]{2,1,0:T(8,128)S(1)}, f32[5,96,128]{2,1,0:T(8,128)S(1)}, u32[]{:S(2)}, u32[]{:S(2)}) collective-permute-start(f32[5,96,128]{2,1,0:T(8,128)S(1)} %shard_map.46), channel_id=1, source_target_pairs={{0,4},{1,5},{2,6},{3,7},{4,0},{5,1},{6,2},{7,3},{8,12},{9,13},{10,... | collective-permute-start | bytes 737288 | tf_op jit(solution)/shard_map/ppermute | solution.py:494
  2.7 3.8 %collective-permute-start.2 = (f32[8,192]{1,0:T(8,128)S(1)}, f32[8,192]{1,0:T(8,128)S(1)}, u32[]{:S(2)}, u32[]{:S(2)}) collective-permute-start(f32[8,192]{1,0:T(8,128)S(1)} %get-tuple-element.32), channel_id=1, source_target_pairs={{0,1},{1,2},{2,3},{3,0},{4,7},{5,4},{6,5},{7,6},{8,9},{9,10},{10,1... | collective-permute-start | bytes 18440 | tf_op jit(solution)/shard_map/ppermute | solution.py:494
  4.9 3.4 %collective-permute-start.1 = (f32[8,192]{1,0:T(8,128)S(1)}, f32[8,192]{1,0:T(8,128)S(1)}, u32[]{:S(2)}, u32[]{:S(2)}) collective-permute-start(f32[8,192]{1,0:T(8,128)S(1)} %get-tuple-element.31), channel_id=1, source_target_pairs={{0,3},{1,0},{2,1},{3,2},{4,5},{5,6},{6,7},{7,4},{8,11},{9,8},{10,9... | collective-permute-start | bytes 18440 | tf_op jit(solution)/shard_map/ppermute | solution.py:494
  6.5 2.1 %copy-start.1 = (f32[5,192,1,128]{3,2,1,0:T(1,128)S(1)}, f32[5,192,1,128]{3,2,1,0:T(1,128)}, u32[]{:S(2)}) copy-start(f32[5,192,1,128]{3,2,1,0:T(1,128)} %param.4) | copy-start | bytes 1474564
  8.5 7.7 %collective-permute-start.3 = (f32[512,128]{1,0:T(8,128)S(1)}, f32[512,128]{1,0:T(8,128)S(1)}, u32[]{:S(2)}, u32[]{:S(2)}) collective-permute-start(f32[512,128]{1,0:T(8,128)S(1)} %shard_map.51), channel_id=1, source_target_pairs={{0,4},{1,5},{2,6},{3,7},{4,0},{5,1},{6,2},{7,3},{8,12},{9,13},{10,... | collective-permute-start | bytes 786440 | tf_op jit(solution)/shard_map/ppermute | solution.py:494
  9.1 2.5 %collective-permute-start.4 = (f32[2,5,24,128]{3,2,1,0:T(8,128)S(1)}, f32[2,5,24,128]{3,2,1,0:T(8,128)S(1)}, u32[]{:S(2)}, u32[]{:S(2)}) collective-permute-start(f32[2,5,24,128]{3,2,1,0:T(8,128)S(1)} %slice_bitcast_fusion), channel_id=1, source_target_pairs={{0,1},{1,0},{2,3},{3,2},{4,5},{5,4},{6,7},{7,6},{8,9},{9,8},{10,11... | collective-permute-start | bytes 368648 | tf_op jit(solution)/shard_map/ppermute | solution.py:494
  10.3 9.6 %collective-permute-start.7 = (f32[5,96,128]{2,1,0:T(8,128)S(1)}, f32[5,96,128]{2,1,0:T(8,128)S(1)}, u32[]{:S(2)}, u32[]{:S(2)}) collective-permute-start(f32[5,96,128]{2,1,0:T(8,128)S(1)} %get-tuple-element.39), channel_id=1, source_target_pairs={{0,8},{1,9},{2,10},{3,11},{4,12},{5,13},{6,14},{7,15},{8,0},{9,1},... | collective-permute-start | bytes 737288 | tf_op jit(solution)/shard_map/ppermute | solution.py:494
  11.6 5.5 %collective-permute-start.5 = (f32[2,5,24,128]{3,2,1,0:T(8,128)S(1)}, f32[2,5,24,128]{3,2,1,0:T(8,128)S(1)}, u32[]{:S(2)}, u32[]{:S(2)}) collective-permute-start(f32[2,5,24,128]{3,2,1,0:T(8,128)S(1)} %pad_maximum_fusion), channel_id=1, source_target_pairs={{0,1},{1,0},{2,3},{3,2},{4,5},{5,4},{6,7},{7,6},{8,18},{9,19},{10,... | collective-permute-start | bytes 368648 | tf_op jit(solution)/shard_map/ppermute | solution.py:494
  12.5 7.4 %collective-permute-start.6 = (f32[2,5,24,128]{3,2,1,0:T(8,128)S(1)}, f32[2,5,24,128]{3,2,1,0:T(8,128)S(1)}, u32[]{:S(2)}, u32[]{:S(2)}) collective-permute-start(f32[2,5,24,128]{3,2,1,0:T(8,128)S(1)} %pad_maximum_fusion.1), channel_id=1, source_target_pairs={{0,1},{1,0},{2,3},{3,2},{4,5},{5,4},{6,7},{7,6},{8,16},{9,17},{10,... | collective-permute-start | bytes 368648 | tf_op jit(solution)/shard_map/ppermute | solution.py:494
  21.1 2.7 %collective-permute-start.8 = (f32[2,5,24,128]{3,2,1,0:T(8,128)S(1)}, f32[2,5,24,128]{3,2,1,0:T(8,128)S(1)}, u32[]{:S(2)}, u32[]{:S(2)}) collective-permute-start(f32[2,5,24,128]{3,2,1,0:T(8,128)S(1)} %get-tuple-element.43), channel_id=1, source_target_pairs={{0,1},{1,0},{2,3},{3,2},{4,5},{5,4},{6,7},{7,6},{8,9},{9,8},{10,11... | collective-permute-start | bytes 368648 | tf_op jit(solution)/shard_map/ppermute | solution.py:494
  22.3 13.5 %collective-permute-start.13 = (f32[496,128]{1,0:T(8,128)S(1)}, f32[496,128]{1,0:T(8,128)S(1)}, u32[]{:S(2)}, u32[]{:S(2)}) collective-permute-start(f32[496,128]{1,0:T(8,128)S(1)} %get-tuple-element.45), channel_id=1, source_target_pairs={{0,4},{1,5},{2,6},{3,7},{4,0},{5,1},{6,2},{7,3},{8,12},{9,13},{10,... | collective-permute-start | bytes 761864 | tf_op jit(solution)/shard_map/ppermute | solution.py:494
  23.9 5.6 %collective-permute-start.9 = (f32[2,5,24,128]{3,2,1,0:T(8,128)S(1)}, f32[2,5,24,128]{3,2,1,0:T(8,128)S(1)}, u32[]{:S(2)}, u32[]{:S(2)}) collective-permute-start(f32[2,5,24,128]{3,2,1,0:T(8,128)S(1)} %pad_maximum_fusion.2), channel_id=1, source_target_pairs={{0,1},{1,0},{2,3},{3,2},{4,8},{5,9},{6,10},{7,11},{8,4},{9,5},{10,... | collective-permute-start | bytes 368648 | tf_op jit(solution)/shard_map/ppermute | solution.py:494
  24.4 7.8 %collective-permute-start.12 = (f32[2,5,24,128]{3,2,1,0:T(8,128)S(1)}, f32[2,5,24,128]{3,2,1,0:T(8,128)S(1)}, u32[]{:S(2)}, u32[]{:S(2)}) collective-permute-start(f32[2,5,24,128]{3,2,1,0:T(8,128)S(1)} %pad_maximum_fusion.5), channel_id=1, source_target_pairs={{0,8},{1,9},{2,10},{3,11},{4,0},{5,1},{6,2},{7,3},{8,16},{9,17},{1... | collective-permute-start | bytes 368648 | tf_op jit(solution)/shard_map/ppermute | solution.py:494
  26.1 6.1 %collective-permute-start.11 = (f32[2,5,24,128]{3,2,1,0:T(8,128)S(1)}, f32[2,5,24,128]{3,2,1,0:T(8,128)S(1)}, u32[]{:S(2)}, u32[]{:S(2)}) collective-permute-start(f32[2,5,24,128]{3,2,1,0:T(8,128)S(1)} %pad_maximum_fusion.4), channel_id=1, source_target_pairs={{0,8},{1,9},{2,10},{3,11},{4,0},{5,1},{6,2},{7,3},{8,18},{9,19},{1... | collective-permute-start | bytes 368648 | tf_op jit(solution)/shard_map/ppermute | solution.py:494
  26.2 6.9 %collective-permute-start.10 = (f32[2,5,24,128]{3,2,1,0:T(8,128)S(1)}, f32[2,5,24,128]{3,2,1,0:T(8,128)S(1)}, u32[]{:S(2)}, u32[]{:S(2)}) collective-permute-start(f32[2,5,24,128]{3,2,1,0:T(8,128)S(1)} %pad_maximum_fusion.3), channel_id=1, source_target_pairs={{0,1},{1,0},{2,3},{3,2},{4,8},{5,9},{6,10},{7,11},{8,4},{9,5},{10,... | collective-permute-start | bytes 368648 | tf_op jit(solution)/shard_map/ppermute | solution.py:494
  29.4 6.4 %collective-permute-start.14 = (f32[8,192]{1,0:T(8,128)S(1)}, f32[8,192]{1,0:T(8,128)S(1)}, u32[]{:S(2)}, u32[]{:S(2)}) collective-permute-start(f32[8,192]{1,0:T(8,128)S(1)} %get-tuple-element.48), channel_id=1, source_target_pairs={{0,7},{1,4},{2,5},{3,6},{4,1},{5,2},{6,3},{7,0},{8,15},{9,12},{10,... | collective-permute-start | bytes 18440 | tf_op jit(solution)/shard_map/ppermute | solution.py:494
  32.2 3.7 %collective-permute-start.15 = (f32[8,192]{1,0:T(8,128)S(1)}, f32[8,192]{1,0:T(8,128)S(1)}, u32[]{:S(2)}, u32[]{:S(2)}) collective-permute-start(f32[8,192]{1,0:T(8,128)S(1)} %get-tuple-element.49), channel_id=1, source_target_pairs={{0,3},{1,0},{2,1},{3,2},{4,5},{5,6},{6,7},{7,4},{8,11},{9,8},{10,9... | collective-permute-start | bytes 18440 | tf_op jit(solution)/shard_map/ppermute | solution.py:494

commit v6 on v4

--- a/solution.py
+++ b/solution.py
@@ -177,6 +177,11 @@
     return jnp.where(hit, 1.0, 0.0).astype(bf16)
 
 
+def edge_of(c, block, lanes):
+    chosen = picks(lanes)[:, c * LANES : (c + 1) * LANES]
+    return dot(chosen, block.astype(bf16), ((1,), (1,)))
+
+
 def edges_of(blocks, lanes):
     blocks = jnp.concatenate([block.astype(bf16) for block in blocks], axis=1)
     return dot(picks(lanes), blocks, ((1,), (1,)))
@@ -386,7 +391,7 @@
 def second_kernel(plan, base_ref, pair_ref, tangent_ref, get_ref, put_ref, *refs):
     chips, count = plan.chips, len(plan.swap_z)
     face_refs, z_refs = refs[:chips][::-1], refs[chips : chips + count]
-    core_ref, partial_ref, out_ref, straight_ref, diag_ref, *edge_refs = refs[chips + count :]
+    core_ref, partial_ref, out_ref, straight_ref, diag_ref, weighted_ref = refs[chips + count :]
     z, x, _ = place()
     odd = lax.rem(z, 2) == 1
     low = is_low(plan.rows)
@@ -395,7 +400,7 @@
     at_end = jnp.logical_or(z == 0, z == plan.pairs - 1)
     put, get = put_ref[...], get_ref[...]
     half = plan.rows // 2
-    blocks = []
+    edge = jnp.zeros((8, plan.rows), f32)
     for c in range(NC):
         face = get_parts(plan, face_refs, c)
         near = padded(plan, z_refs[0][c])
@@ -426,11 +431,16 @@
         for turn in range(chips):
             at = (chips + turn) * plan.part_pad
             core_ref[turn, c] = face[at : at + plan.part_pad]
-        blocks.append(weighted)
-    edges = edges_of(blocks, [127 * (1 - x), 64 - x, 127 * x, 63 + x])
-    put_edge(plan, out_ref, 0, edges[:8])
-    for i, ref in enumerate(edge_refs):
-        ref[...] = edges[8 * i + 8 : 8 * i + 16]
+        weighted_ref[c] = weighted
+        edge += edge_of(c, weighted, [127 * (1 - x)])
+    put_edge(plan, out_ref, 0, edge)
+
+
+def edge2_kernel(plan, weighted_ref, cross_ref, inward_ref, own_ref):
+    _, x, _ = place()
+    edges = edges_of([weighted_ref[c] for c in range(NC)], [64 - x, 127 * x, 63 + x])
+    for i, ref in enumerate((cross_ref, inward_ref, own_ref)):
+        ref[...] = edges[8 * i : 8 * i + 8]
 
 
 def rest_kernel(plan, tangent_ref, get_ref, *refs):
@@ -529,12 +539,13 @@
             [full] * 4,
             *(checkpoint, state_got, flux, carried, share_got, outward_got, own),
         )
-        core, partial, mine, straight, diag, cross, inward, own = run(
+        core, partial, mine, straight, diag, weighted = run(
             second_kernel,
-            [(parts[0][1:], f32), full, share(1), parts, parts] + [edge] * 3,
+            [(parts[0][1:], f32), full, share(1), parts, parts, full],
             *(base, pair, pair_tangent, get, put, *face_got[::-1], *near_got),
         )
         crossed = send(core, plan.swap_core)
+        cross, inward, own = run(edge2_kernel, [edge] * 3, weighted)
         share_got = send(mine, plan.swap_x)
         z, x, _ = place()
         turned = jnp.logical_xor(x == 0, z == plan.inlet)

time: 37.1 us -> 37.1 us (level)
    pallas_call x10 -> x11, Pallas kernels: 5.44 us -> 5.59 us  [call(): pl.pallas_call(kernel, out_shape=[jax.ShapeDtypeStruct(shape, dtype) for...]
where the time goes in v6:
time: 37.1 us; the launch traced here: 36.9 us
  starting transfers between devices  16.6 us (45%)
  waiting for transfers between devices  12.5 us (34%)
  Pallas kernels  5.59 us (15%)
  local copies, waits for them, and re-layouts  1.88 us (5%)
    ppermute x16, starting transfers between devices, send(): return lax.ppermute(part, AXES, moves)  16.6 us
    ppermute x16, waiting for transfers between devices, send(): return lax.ppermute(part, AXES, moves)  12.5 us
    pallas_call x11, Pallas kernels, call(): pl.pallas_call(kernel, out_shape=[jax.ShapeDtypeStruct(shape, dtype) for...  5.59 us
    unnamed x8, local copies, waits for them, and re-layouts  1.04 us
    reshape x1, local copies, waits for them, and re-layouts, local(): source = row_source.reshape(plan.span, rows)  0.76 us
  transfers between devices with their start and end apart: 16, of which 7 were waited for; matrix products, arithmetic and copies ran while one was open for 3% of the time, Pallas kernels for 8%

profile of v6, /device:TPU:17, one launch (start us, length us, event | category | flops | bytes accessed | tf_op | source)
XLA Modules:
  0.0 36.9 jit_solution(11065446695106196754)
XLA Ops:
  0.0 1.0 %copy-done = f32[5,192,1,128]{3,2,1,0:T(1,128)S(1)} copy-done((f32[5,192,1,128]{3,2,1,0:T(1,128)S(1)}, f32[5,192,1,128]{3,2,1,0:T(1,128)}, u32[]{:S(2)}) %copy-start) | copy-done | bytes 491544
  1.0 0.2 shard_map.46
  1.2 1.3 %collective-permute-start = (f32[5,96,128]{2,1,0:T(8,128)S(1)}, f32[5,96,128]{2,1,0:T(8,128)S(1)}, u32[]{:S(2)}, u32[]{:S(2)}) collective-permute-start(f32[5,96,128]{2,1,0:T(8,128)S(1)} %shard_map.46), channel_id=1, source_target_pairs={{0,4},{1,5},{2,6},{3,7},{4,0},{5,1},{6,2},{7,3},{8,12},{9,13},{10,... | collective-permute-start | bytes 737288 | tf_op jit(solution)/shard_map/ppermute | solution.py:502
  2.5 0.2 shard_map.50
  2.7 2.1 %collective-permute-start.2 = (f32[8,192]{1,0:T(8,128)S(1)}, f32[8,192]{1,0:T(8,128)S(1)}, u32[]{:S(2)}, u32[]{:S(2)}) collective-permute-start(f32[8,192]{1,0:T(8,128)S(1)} %get-tuple-element.33), channel_id=1, source_target_pairs={{0,1},{1,2},{2,3},{3,0},{4,7},{5,4},{6,5},{7,6},{8,9},{9,10},{10,1... | collective-permute-start | bytes 18440 | tf_op jit(solution)/shard_map/ppermute | solution.py:502
  4.9 0.0 collective-permute-start.1
  4.9 0.8 %reshape.16 = s32[4,192]{1,0:T(4,128)S(1)} reshape(s32[768]{0:T(1024)} %param.7) | data formatting | bytes 6144 | tf_op jit(solution)/shard_map/reshape | solution.py:515
  5.6 0.4 %shard_map.47 = (bf16[192,192]{1,0:T(8,128)(2,1)S(1)}, bf16[192,192]{1,0:T(8,128)(2,1)S(1)}) custom-call(s32[8,192]{1,0:T(8,128)S(1)} %pad.4.refs_0_), custom_call_target="tpu_custom_call" | custom-call | tf_op jit(solution)/shard_map/pallas_call | solution.py:481
  6.1 0.0 copy-done.2
  6.1 0.0 copy-done.3
  6.1 0.4 %shard_map.49.refs_0_.refs_3_ = f32[5,192,128]{2,1,0:T(8,128)S(1)} custom-call(f32[5,192,128]{2,1,0:T(8,128)S(1)} %bitcast.29, bf16[3,320,320]{2,1,0:T(8,128)(2,1)S(1)} %bitcast.28), custom_call_target="tpu_custom_call" | custom-call | tf_op jit(solution)/shard_map/pallas_call | solution.py:481
  6.5 0.0 copy-start.1
  6.5 0.0 collective-permute-done.2.refs_3_.refs_5_
  6.5 1.7 %collective-permute-done.1.refs_2_ = f32[8,192]{1,0:T(8,128)S(1)} collective-permute-done((f32[8,192]{1,0:T(8,128)S(1)}, f32[8,192]{1,0:T(8,128)S(1)}, u32[]{:S(2)}, u32[]{:S(2)}) %collective-permute-start.1) | collective-permute-done | bytes 6176 | tf_op jit(solution)/shard_map/ppermute | solution.py:502
  8.2 0.2 shard_map.51
  8.5 0.1 collective-permute-start.3
  8.5 0.0 collective-permute-done.refs_1_
  8.6 0.5 %shard_map.48 = (f32[5,192,128]{2,1,0:T(8,128)S(1)}, f32[2,2,5,24,128]{4,3,2,1,0:T(8,128)S(1)}, f32[5,96,128]{2,1,0:T(8,128)S(1)}) custom-call(f32[5,192,128]{2,1,0:T(8,128)S(1)} %bitcast.26, f32[5,96,128]{2,1,0:T(8,128)S(1)} %collective-permute-done.refs_1_, bf16[192,192]{1,0:T(8,128)(2,1)S(1)} %get-tuple-element.29.refs_2_.refs_4_), custom_call_target="tpu_custom_call" | custom-call | tf_op jit(solution)/shard_map/pallas_call | solution.py:481
  9.1 1.2 %collective-permute-start.4 = (f32[2,5,24,128]{3,2,1,0:T(8,128)S(1)}, f32[2,5,24,128]{3,2,1,0:T(8,128)S(1)}, u32[]{:S(2)}, u32[]{:S(2)}) collective-permute-start(f32[2,5,24,128]{3,2,1,0:T(8,128)S(1)} %slice_bitcast_fusion), channel_id=1, source_target_pairs={{0,1},{1,0},{2,3},{3,2},{4,5},{5,4},{6,7},{7,6},{8,9},{9,8},{10,11... | collective-permute-start | bytes 368648 | tf_op jit(solution)/shard_map/ppermute | solution.py:502
  10.3 1.3 %collective-permute-start.7 = (f32[5,96,128]{2,1,0:T(8,128)S(1)}, f32[5,96,128]{2,1,0:T(8,128)S(1)}, u32[]{:S(2)}, u32[]{:S(2)}) collective-permute-start(f32[5,96,128]{2,1,0:T(8,128)S(1)} %get-tuple-element.40), channel_id=1, source_target_pairs={{0,8},{1,9},{2,10},{3,11},{4,12},{5,13},{6,14},{7,15},{8,0},{9,1},... | collective-permute-start | bytes 737288 | tf_op jit(solution)/shard_map/ppermute | solution.py:502
  11.6 0.0 collective-permute-done.4
  11.6 0.8 %collective-permute-start.5 = (f32[2,5,24,128]{3,2,1,0:T(8,128)S(1)}, f32[2,5,24,128]{3,2,1,0:T(8,128)S(1)}, u32[]{:S(2)}, u32[]{:S(2)}) collective-permute-start(f32[2,5,24,128]{3,2,1,0:T(8,128)S(1)} %pad_maximum_fusion), channel_id=1, source_target_pairs={{0,1},{1,0},{2,3},{3,2},{4,5},{5,4},{6,7},{7,6},{8,18},{9,19},{10,... | collective-permute-start | bytes 368648 | tf_op jit(solution)/shard_map/ppermute | solution.py:502
  12.5 1.7 %collective-permute-start.6 = (f32[2,5,24,128]{3,2,1,0:T(8,128)S(1)}, f32[2,5,24,128]{3,2,1,0:T(8,128)S(1)}, u32[]{:S(2)}, u32[]{:S(2)}) collective-permute-start(f32[2,5,24,128]{3,2,1,0:T(8,128)S(1)} %pad_maximum_fusion.1), channel_id=1, source_target_pairs={{0,1},{1,0},{2,3},{3,2},{4,5},{5,4},{6,7},{7,6},{8,16},{9,17},{10,... | collective-permute-start | bytes 368648 | tf_op jit(solution)/shard_map/ppermute | solution.py:502
  14.2 2.0 %collective-permute-done.3.refs_4_ = f32[512,128]{1,0:T(8,128)S(1)} collective-permute-done((f32[512,128]{1,0:T(8,128)S(1)}, f32[512,128]{1,0:T(8,128)S(1)}, u32[]{:S(2)}, u32[]{:S(2)}) %collective-permute-start.3) | collective-permute-done | bytes 262176 | tf_op jit(solution)/shard_map/ppermute | solution.py:502
  16.2 0.8 %shard_map.52 = (f32[5,192,128]{2,1,0:T(8,128)S(1)}, f32[5,192,128]{2,1,0:T(8,128)S(1)}, f32[5,192,128]{2,1,0:T(8,128)S(1)}, f32[5,192,128]{2,1,0:T(8,128)S(1)}) custom-call(f32[5,192,128]{2,1,0:T(8,128)S(1)} %bitcast.27, f32[5,96,128]{2,1,0:T(8,128)S(1)} %collective-permute-done.refs_1_, f32[5,192,128]{2,1,0:T(8,128)S(1)} %get-tuple-element.30.refs_2_, ...), custom_call_target="tpu_custom_call" | custom-call | tf_op jit(solution)/shard_map/pallas_call | solution.py:481
  17.0 0.1 collective-permute-done.5.refs_5_
  17.1 2.7 %collective-permute-done.6.refs_6_ = f32[2,5,24,128]{3,2,1,0:T(8,128)S(1)} collective-permute-done((f32[2,5,24,128]{3,2,1,0:T(8,128)S(1)}, f32[2,5,24,128]{3,2,1,0:T(8,128)S(1)}, u32[]{:S(2)}, u32[]{:S(2)}) %collective-permute-start.6) | collective-permute-done | bytes 122912 | tf_op jit(solution)/shard_map/ppermute | solution.py:502
  19.8 0.0 collective-permute-done.7.refs_7_
  19.9 1.2 %shard_map.53 = (f32[2,5,24,128]{3,2,1,0:T(8,128)S(1)}, f32[5,192,128]{2,1,0:T(8,128)S(1)}, f32[496,128]{1,0:T(8,128)S(1)}, f32[2,2,5,24,128]{4,3,2,1,0:T(8,128)...) custom-call(f32[5,192,128]{2,1,0:T(8,128)S(1)} %get-tuple-element.35.refs_0_, ...), custom_call_target="tpu_custom_call" | custom-call | tf_op jit(solution)/shard_map/pallas_call | solution.py:481
  21.0 1.2 %collective-permute-start.8 = (f32[2,5,24,128]{3,2,1,0:T(8,128)S(1)}, f32[2,5,24,128]{3,2,1,0:T(8,128)S(1)}, u32[]{:S(2)}, u32[]{:S(2)}) collective-permute-start(f32[2,5,24,128]{3,2,1,0:T(8,128)S(1)} %get-tuple-element.44), channel_id=1, source_target_pairs={{0,1},{1,0},{2,3},{3,2},{4,5},{5,4},{6,7},{7,6},{8,9},{9,8},{10,11... | collective-permute-start | bytes 368648 | tf_op jit(solution)/shard_map/ppermute | solution.py:502
  22.3 1.4 %collective-permute-start.13 = (f32[496,128]{1,0:T(8,128)S(1)}, f32[496,128]{1,0:T(8,128)S(1)}, u32[]{:S(2)}, u32[]{:S(2)}) collective-permute-start(f32[496,128]{1,0:T(8,128)S(1)} %get-tuple-element.46), channel_id=1, source_target_pairs={{0,4},{1,5},{2,6},{3,7},{4,0},{5,1},{6,2},{7,3},{8,12},{9,13},{10,... | collective-permute-start | bytes 761864 | tf_op jit(solution)/shard_map/ppermute | solution.py:502
  23.7 0.0 collective-permute-done.8
  23.8 0.5 %collective-permute-start.9 = (f32[2,5,24,128]{3,2,1,0:T(8,128)S(1)}, f32[2,5,24,128]{3,2,1,0:T(8,128)S(1)}, u32[]{:S(2)}, u32[]{:S(2)}) collective-permute-start(f32[2,5,24,128]{3,2,1,0:T(8,128)S(1)} %pad_maximum_fusion.2), channel_id=1, source_target_pairs={{0,1},{1,0},{2,3},{3,2},{4,8},{5,9},{6,10},{7,11},{8,4},{9,5},{10,... | collective-permute-start | bytes 368648 | tf_op jit(solution)/shard_map/ppermute | solution.py:502
  24.3 1.7 %collective-permute-start.12 = (f32[2,5,24,128]{3,2,1,0:T(8,128)S(1)}, f32[2,5,24,128]{3,2,1,0:T(8,128)S(1)}, u32[]{:S(2)}, u32[]{:S(2)}) collective-permute-start(f32[2,5,24,128]{3,2,1,0:T(8,128)S(1)} %pad_maximum_fusion.5), channel_id=1, source_target_pairs={{0,8},{1,9},{2,10},{3,11},{4,0},{5,1},{6,2},{7,3},{8,16},{9,17},{1... | collective-permute-start | bytes 368648 | tf_op jit(solution)/shard_map/ppermute | solution.py:502
  26.1 0.1 collective-permute-start.11
  26.1 0.3 collective-permute-start.10
  26.5 0.2 shard_map.55
  26.7 2.7 %collective-permute-done.9.refs_2_ = f32[2,5,24,128]{3,2,1,0:T(8,128)S(1)} collective-permute-done((f32[2,5,24,128]{3,2,1,0:T(8,128)S(1)}, f32[2,5,24,128]{3,2,1,0:T(8,128)S(1)}, u32[]{:S(2)}, u32[]{:S(2)}) %collective-permute-start.9) | collective-permute-done | bytes 122912 | tf_op jit(solution)/shard_map/ppermute | solution.py:502
  29.4 2.7 %collective-permute-start.14 = (f32[8,192]{1,0:T(8,128)S(1)}, f32[8,192]{1,0:T(8,128)S(1)}, u32[]{:S(2)}, u32[]{:S(2)}) collective-permute-start(f32[8,192]{1,0:T(8,128)S(1)} %get-tuple-element.50), channel_id=1, source_target_pairs={{0,7},{1,4},{2,5},{3,6},{4,1},{5,2},{6,3},{7,0},{8,15},{9,12},{10,... | collective-permute-start | bytes 18440 | tf_op jit(solution)/shard_map/ppermute | solution.py:502
  32.1 0.0 collective-permute-done.12.refs_5_
  32.1 0.0 collective-permute-start.15
  32.1 0.0 collective-permute-done.11.refs_4_
  32.1 0.9 %collective-permute-done.10.refs_3_ = f32[2,5,24,128]{3,2,1,0:T(8,128)S(1)} collective-permute-done((f32[2,5,24,128]{3,2,1,0:T(8,128)S(1)}, f32[2,5,24,128]{3,2,1,0:T(8,128)S(1)}, u32[]{:S(2)}, u32[]{:S(2)}) %collective-permute-start.10) | collective-permute-done | bytes 122912 | tf_op jit(solution)/shard_map/ppermute | solution.py:502
  33.0 0.4 %shard_map.54.refs_1_ = f32[5,192,128]{2,1,0:T(8,128)S(1)} custom-call(f32[5,192,128]{2,1,0:T(8,128)S(1)} %get-tuple-element.42.refs_0_.refs_2_, bf16[192,192]{1,0:T(8,128)(2,1)S(1)} %get-tuple-element.38.refs_3_.refs_1_, f32[2,5,24,128]{3,2,1,0:T(8,128)S(1)} %collective-permute-done.9.refs_2_, f32[2,5,24,128]{3,2,1,0:T(8,128)S(1)} %collective-permute-done.10.refs_3_, ...), custom_call_target="tpu_custom_call" | custom-call | tf_op jit(solution)/shard_map/pallas_call | solution.py:481
  33.4 2.3 %collective-permute-done.14.refs_4_ = f32[8,192]{1,0:T(8,128)S(1)} collective-permute-done((f32[8,192]{1,0:T(8,128)S(1)}, f32[8,192]{1,0:T(8,128)S(1)}, u32[]{:S(2)}, u32[]{:S(2)}) %collective-permute-start.14) | collective-permute-done | bytes 6176 | tf_op jit(solution)/shard_map/ppermute | solution.py:502
  35.8 0.0 collective-permute-done.15.refs_5_
  35.8 0.0 collective-permute-done.13.refs_3_
  35.8 1.1 %shard_map.56 = f32[5,192,128]{2,1,0:T(8,128)} custom-call(f32[5,192,128]{2,1,0:T(8,128)S(1)} %get-tuple-element.41.refs_0_, f32[5,192,128]{2,1,0:T(8,128)S(1)} %shard_map.54.refs_1_, f32[5,192,128]{2,1,0:T(8,128)S(1)} %get-tuple-element.42.refs_0_.refs_2_, f32[496,128]{1,0:T(8,128)S(1)} %collective-permute-done.13.refs_3_, ...), custom_call_target="tpu_custom_call" | custom-call | tf_op jit(solution)/shard_map/pallas_call | solution.py:481
  (17 shorter events, 0.2 us)
Async XLA Ops:
  0.0 1.0 %copy-start = (f32[5,192,1,128]{3,2,1,0:T(1,128)S(1)}, f32[5,192,1,128]{3,2,1,0:T(1,128)}, u32[]{:S(2)}) copy-start(f32[5,192,1,128]{3,2,1,0:T(1,128)} %param.4) | copy-start | bytes 1474564
  1.0 5.1 %copy-start.2 = (bf16[1,3,320,320]{3,2,1,0:T(8,128)(2,1)S(1)}, bf16[1,3,320,320]{3,2,1,0:T(8,128)(2,1)}, u32[]{:S(2)}) copy-start(bf16[1,3,320,320]{3,2,1,0:T(8,128)(2,1)} %param.6) | copy-start | bytes 1843204
  1.0 5.1 %copy-start.3 = (f32[5,192,1,128]{3,2,1,0:T(1,128)S(1)}, f32[5,192,1,128]{3,2,1,0:T(1,128)}, u32[]{:S(2)}) copy-start(f32[5,192,1,128]{3,2,1,0:T(1,128)} %param.5) | copy-start | bytes 1474564
  1.2 7.3 %collective-permute-start = (f32[5,96,128]{2,1,0:T(8,128)S(1)}, f32[5,96,128]{2,1,0:T(8,128)S(1)}, u32[]{:S(2)}, u32[]{:S(2)}) collective-permute-start(f32[5,96,128]{2,1,0:T(8,128)S(1)} %shard_map.46), channel_id=1, source_target_pairs={{0,4},{1,5},{2,6},{3,7},{4,0},{5,1},{6,2},{7,3},{8,12},{9,13},{10,... | collective-permute-start | bytes 737288 | tf_op jit(solution)/shard_map/ppermute | solution.py:502
  2.7 3.8 %collective-permute-start.2 = (f32[8,192]{1,0:T(8,128)S(1)}, f32[8,192]{1,0:T(8,128)S(1)}, u32[]{:S(2)}, u32[]{:S(2)}) collective-permute-start(f32[8,192]{1,0:T(8,128)S(1)} %get-tuple-element.33), channel_id=1, source_target_pairs={{0,1},{1,2},{2,3},{3,0},{4,7},{5,4},{6,5},{7,6},{8,9},{9,10},{10,1... | collective-permute-start | bytes 18440 | tf_op jit(solution)/shard_map/ppermute | solution.py:502
  4.9 3.4 %collective-permute-start.1 = (f32[8,192]{1,0:T(8,128)S(1)}, f32[8,192]{1,0:T(8,128)S(1)}, u32[]{:S(2)}, u32[]{:S(2)}) collective-permute-start(f32[8,192]{1,0:T(8,128)S(1)} %get-tuple-element.32), channel_id=1, source_target_pairs={{0,3},{1,0},{2,1},{3,2},{4,5},{5,6},{6,7},{7,4},{8,11},{9,8},{10,9... | collective-permute-start | bytes 18440 | tf_op jit(solution)/shard_map/ppermute | solution.py:502
  6.5 2.0 %copy-start.1 = (f32[5,192,1,128]{3,2,1,0:T(1,128)S(1)}, f32[5,192,1,128]{3,2,1,0:T(1,128)}, u32[]{:S(2)}) copy-start(f32[5,192,1,128]{3,2,1,0:T(1,128)} %param.4) | copy-start | bytes 1474564
  8.5 7.8 %collective-permute-start.3 = (f32[512,128]{1,0:T(8,128)S(1)}, f32[512,128]{1,0:T(8,128)S(1)}, u32[]{:S(2)}, u32[]{:S(2)}) collective-permute-start(f32[512,128]{1,0:T(8,128)S(1)} %shard_map.51), channel_id=1, source_target_pairs={{0,4},{1,5},{2,6},{3,7},{4,0},{5,1},{6,2},{7,3},{8,12},{9,13},{10,... | collective-permute-start | bytes 786440 | tf_op jit(solution)/shard_map/ppermute | solution.py:502
  9.1 2.5 %collective-permute-start.4 = (f32[2,5,24,128]{3,2,1,0:T(8,128)S(1)}, f32[2,5,24,128]{3,2,1,0:T(8,128)S(1)}, u32[]{:S(2)}, u32[]{:S(2)}) collective-permute-start(f32[2,5,24,128]{3,2,1,0:T(8,128)S(1)} %slice_bitcast_fusion), channel_id=1, source_target_pairs={{0,1},{1,0},{2,3},{3,2},{4,5},{5,4},{6,7},{7,6},{8,9},{9,8},{10,11... | collective-permute-start | bytes 368648 | tf_op jit(solution)/shard_map/ppermute | solution.py:502
  10.3 9.6 %collective-permute-start.7 = (f32[5,96,128]{2,1,0:T(8,128)S(1)}, f32[5,96,128]{2,1,0:T(8,128)S(1)}, u32[]{:S(2)}, u32[]{:S(2)}) collective-permute-start(f32[5,96,128]{2,1,0:T(8,128)S(1)} %get-tuple-element.40), channel_id=1, source_target_pairs={{0,8},{1,9},{2,10},{3,11},{4,12},{5,13},{6,14},{7,15},{8,0},{9,1},... | collective-permute-start | bytes 737288 | tf_op jit(solution)/shard_map/ppermute | solution.py:502
  11.6 5.5 %collective-permute-start.5 = (f32[2,5,24,128]{3,2,1,0:T(8,128)S(1)}, f32[2,5,24,128]{3,2,1,0:T(8,128)S(1)}, u32[]{:S(2)}, u32[]{:S(2)}) collective-permute-start(f32[2,5,24,128]{3,2,1,0:T(8,128)S(1)} %pad_maximum_fusion), channel_id=1, source_target_pairs={{0,1},{1,0},{2,3},{3,2},{4,5},{5,4},{6,7},{7,6},{8,18},{9,19},{10,... | collective-permute-start | bytes 368648 | tf_op jit(solution)/shard_map/ppermute | solution.py:502
  12.5 7.4 %collective-permute-start.6 = (f32[2,5,24,128]{3,2,1,0:T(8,128)S(1)}, f32[2,5,24,128]{3,2,1,0:T(8,128)S(1)}, u32[]{:S(2)}, u32[]{:S(2)}) collective-permute-start(f32[2,5,24,128]{3,2,1,0:T(8,128)S(1)} %pad_maximum_fusion.1), channel_id=1, source_target_pairs={{0,1},{1,0},{2,3},{3,2},{4,5},{5,4},{6,7},{7,6},{8,16},{9,17},{10,... | collective-permute-start | bytes 368648 | tf_op jit(solution)/shard_map/ppermute | solution.py:502
  21.0 2.7 %collective-permute-start.8 = (f32[2,5,24,128]{3,2,1,0:T(8,128)S(1)}, f32[2,5,24,128]{3,2,1,0:T(8,128)S(1)}, u32[]{:S(2)}, u32[]{:S(2)}) collective-permute-start(f32[2,5,24,128]{3,2,1,0:T(8,128)S(1)} %get-tuple-element.44), channel_id=1, source_target_pairs={{0,1},{1,0},{2,3},{3,2},{4,5},{5,4},{6,7},{7,6},{8,9},{9,8},{10,11... | collective-permute-start | bytes 368648 | tf_op jit(solution)/shard_map/ppermute | solution.py:502
  22.3 13.5 %collective-permute-start.13 = (f32[496,128]{1,0:T(8,128)S(1)}, f32[496,128]{1,0:T(8,128)S(1)}, u32[]{:S(2)}, u32[]{:S(2)}) collective-permute-start(f32[496,128]{1,0:T(8,128)S(1)} %get-tuple-element.46), channel_id=1, source_target_pairs={{0,4},{1,5},{2,6},{3,7},{4,0},{5,1},{6,2},{7,3},{8,12},{9,13},{10,... | collective-permute-start | bytes 761864 | tf_op jit(solution)/shard_map/ppermute | solution.py:502
  23.8 5.6 %collective-permute-start.9 = (f32[2,5,24,128]{3,2,1,0:T(8,128)S(1)}, f32[2,5,24,128]{3,2,1,0:T(8,128)S(1)}, u32[]{:S(2)}, u32[]{:S(2)}) collective-permute-start(f32[2,5,24,128]{3,2,1,0:T(8,128)S(1)} %pad_maximum_fusion.2), channel_id=1, source_target_pairs={{0,1},{1,0},{2,3},{3,2},{4,8},{5,9},{6,10},{7,11},{8,4},{9,5},{10,... | collective-permute-start | bytes 368648 | tf_op jit(solution)/shard_map/ppermute | solution.py:502
  24.3 7.8 %collective-permute-start.12 = (f32[2,5,24,128]{3,2,1,0:T(8,128)S(1)}, f32[2,5,24,128]{3,2,1,0:T(8,128)S(1)}, u32[]{:S(2)}, u32[]{:S(2)}) collective-permute-start(f32[2,5,24,128]{3,2,1,0:T(8,128)S(1)} %pad_maximum_fusion.5), channel_id=1, source_target_pairs={{0,8},{1,9},{2,10},{3,11},{4,0},{5,1},{6,2},{7,3},{8,16},{9,17},{1... | collective-permute-start | bytes 368648 | tf_op jit(solution)/shard_map/ppermute | solution.py:502
  26.1 6.1 %collective-permute-start.11 = (f32[2,5,24,128]{3,2,1,0:T(8,128)S(1)}, f32[2,5,24,128]{3,2,1,0:T(8,128)S(1)}, u32[]{:S(2)}, u32[]{:S(2)}) collective-permute-start(f32[2,5,24,128]{3,2,1,0:T(8,128)S(1)} %pad_maximum_fusion.4), channel_id=1, source_target_pairs={{0,8},{1,9},{2,10},{3,11},{4,0},{5,1},{6,2},{7,3},{8,18},{9,19},{1... | collective-permute-start | bytes 368648 | tf_op jit(solution)/shard_map/ppermute | solution.py:502
  26.1 6.9 %collective-permute-start.10 = (f32[2,5,24,128]{3,2,1,0:T(8,128)S(1)}, f32[2,5,24,128]{3,2,1,0:T(8,128)S(1)}, u32[]{:S(2)}, u32[]{:S(2)}) collective-permute-start(f32[2,5,24,128]{3,2,1,0:T(8,128)S(1)} %pad_maximum_fusion.3), channel_id=1, source_target_pairs={{0,1},{1,0},{2,3},{3,2},{4,8},{5,9},{6,10},{7,11},{8,4},{9,5},{10,... | collective-permute-start | bytes 368648 | tf_op jit(solution)/shard_map/ppermute | solution.py:502
  29.4 6.4 %collective-permute-start.14 = (f32[8,192]{1,0:T(8,128)S(1)}, f32[8,192]{1,0:T(8,128)S(1)}, u32[]{:S(2)}, u32[]{:S(2)}) collective-permute-start(f32[8,192]{1,0:T(8,128)S(1)} %get-tuple-element.50), channel_id=1, source_target_pairs={{0,7},{1,4},{2,5},{3,6},{4,1},{5,2},{6,3},{7,0},{8,15},{9,12},{10,... | collective-permute-start | bytes 18440 | tf_op jit(solution)/shard_map/ppermute | solution.py:502
  32.1 3.7 %collective-permute-start.15 = (f32[8,192]{1,0:T(8,128)S(1)}, f32[8,192]{1,0:T(8,128)S(1)}, u32[]{:S(2)}, u32[]{:S(2)}) collective-permute-start(f32[8,192]{1,0:T(8,128)S(1)} %get-tuple-element.51), channel_id=1, source_target_pairs={{0,3},{1,0},{2,1},{3,2},{4,5},{5,6},{6,7},{7,4},{8,11},{9,8},{10,9... | collective-permute-start | bytes 18440 | tf_op jit(solution)/shard_map/ppermute | solution.py:502
